TPU v7x, 32 devices: a whole 2x2x4 slice. The times are simulated.
32 devices in a mesh: dp: 2 (over x), seq: 16 (over z, y, core).
Axes of the slice: x: 2, y: 2, z: 4, core: 2. Of those that a mesh axis runs over, the one named last changes fastest.
Arguments:
- token_ids: int32 [2, 2048], P('dp', 'seq'), may hold values from 0 to 11
- embed_table: float32 [12, 768], replicated, may hold values from -6 to 6
- gain_one: float32 [768], replicated, may hold values from 0.1 to 1.9
- bias_one: float32 [768], replicated, may hold values from -1.75 to 1.75
- in_weight: float32 [768, 2304], P(('dp', 'seq')), may hold values from -0.21875 to 0.21875
- in_bias: float32 [2304], replicated, may hold values from -1.75 to 1.75
- short_taps: float32 [3, 2304], replicated, may hold values from -3.5 to 3.5
- short_bias: float32 [2304], replicated, may hold values from -1.75 to 1.75
- freq_weight: float32 [33, 64], replicated, may hold values from -6 to 6
- freq_bias: float32 [64], replicated, may hold values from -3.140625 to 3.140625
- inner_weight: float32 [64, 64], replicated, may hold values from -3 to 3
- inner_bias: float32 [64], replicated, may hold values from -3.140625 to 3.140625
- filter_weight: float32 [1536, 64], P(('dp', 'seq')), may hold values from -0.046875 to 0.046875
- skip_scale: float32 [2, 768], replicated, may hold values from -6 to 6
- out_weight: float32 [768, 768], P(('dp', 'seq')), may hold values from -0.21875 to 0.21875
- out_bias: float32 [768], replicated, may hold values from -1.75 to 1.75
- gain_two: float32 [768], replicated, may hold values from 0.1 to 1.9
- bias_two: float32 [768], replicated, may hold values from -1.75 to 1.75
- up_weight: float32 [768, 3072], P(('dp', 'seq')), may hold values from -0.21875 to 0.21875
- up_bias: float32 [3072], replicated, may hold values from -1.75 to 1.75
- down_weight: float32 [3072, 768], P(('dp', 'seq')), may hold values from -0.21875 to 0.21875
- down_bias: float32 [768], replicated, may hold values from -1.75 to 1.75
- cotangent: bfloat16 [2, 2048, 768], P('dp', 'seq'), may hold values from -6 to 6
Outputs:
- block_out: float32 [2, 2048, 768], P('dp', 'seq')
- grad_embed: float32 [12, 768], replicated
- grad_gain_one: float32 [768], replicated
- grad_bias_one: float32 [768], replicated
- grad_in_weight: float32 [768, 2304], P(('dp', 'seq'))
- grad_in_bias: float32 [2304], replicated
- grad_short_taps: float32 [3, 2304], replicated
- grad_short_bias: float32 [2304], replicated
- grad_freq_weight: float32 [33, 64], replicated
- grad_freq_bias: float32 [64], replicated
- grad_inner_weight: float32 [64, 64], replicated
- grad_inner_bias: float32 [64], replicated
- grad_filter_weight: float32 [1536, 64], P(('dp', 'seq'))
- grad_skip_scale: float32 [2, 768], replicated
- grad_out_weight: float32 [768, 768], P(('dp', 'seq'))
- grad_out_bias: float32 [768], replicated
- grad_gain_two: float32 [768], replicated
- grad_bias_two: float32 [768], replicated
- grad_up_weight: float32 [768, 3072], P(('dp', 'seq'))
- grad_up_bias: float32 [3072], replicated
- grad_down_weight: float32 [3072, 768], P(('dp', 'seq'))
- grad_down_bias: float32 [768], replicated
All inputs are finite; a program needn't handle non-finite values.
Results may differ from a plain program's by a relative error of at most 0.012.
Values may be sent and summed in bfloat16 or wider, within the bound.
A program may use at most 192 MiB of HBM per device.

v0:
```python
import math

import jax
import jax.numpy as jnp
from jax import lax
from jax.sharding import PartitionSpec as P

epsilon = 1e-05
slow_rate = -math.log(0.01) / 1.5
fast_rate = -math.log(0.01) / 0.3
decay_shift = 0.05
highest = lax.Precision.HIGHEST


def passed_along(value, axis, steps):
    count = lax.axis_size(axis)
    leading, last = (max(0, -steps), min(count, count - steps))
    return lax.ppermute(value, axis, [(source, source + steps) for source in range(leading, last)])


def exact_dot(left_side, right_side):
    return jnp.dot(left_side, right_side, precision=highest, preferred_element_type=jnp.float32)


def narrow_dot(left_side, right_side):
    return jnp.dot(left_side, right_side, preferred_element_type=jnp.float32)


def rows_inner(left_side, right_side, accuracy=None):
    return lax.dot_general(
        left_side,
        right_side,
        (((0,), (0,)), ((), ())),
        precision=accuracy,
        preferred_element_type=jnp.float32,
    )


def against_rows(left_side, right_side, accuracy=None):
    return lax.dot_general(
        left_side,
        right_side,
        (((1,), (1,)), ((), ())),
        precision=accuracy,
        preferred_element_type=jnp.float32,
    )


def normalize(values):
    center = values - jnp.mean(values, axis=-1, keepdims=True)
    inverse = lax.rsqrt(jnp.mean(center * center, axis=-1, keepdims=True) + epsilon)
    return (center * inverse, inverse)


def norm_back(upstream, unit_vals, inverse):
    return inverse * (
        upstream
        - jnp.mean(upstream, axis=-1, keepdims=True)
        - unit_vals * jnp.mean(upstream * unit_vals, axis=-1, keepdims=True)
    )


def angle_table(row_count, column_count, modulus):
    product = (
        jnp.arange(row_count, dtype=jnp.int32)[:, None]
        * jnp.arange(column_count, dtype=jnp.int32)[None, :]
        % modulus
    )
    angles = 2.0 * math.pi / modulus * product.astype(jnp.float32)
    return (jnp.cos(angles), jnp.sin(angles))


def forward_transform(signal, tables):
    cos_section, sin_section, cos_twist, sin_twist, cos_last, sin_last = tables
    real_first = jnp.einsum("kn,...nm->...km", cos_section, signal, precision=highest)
    imag_first = -jnp.einsum("kn,...nm->...km", sin_section, signal, precision=highest)
    real_turn = real_first * cos_twist + imag_first * sin_twist
    imag_turn = imag_first * cos_twist - real_first * sin_twist
    real_out = exact_dot(real_turn, cos_last) + exact_dot(imag_turn, sin_last)
    imag_out = exact_dot(imag_turn, cos_last) - exact_dot(real_turn, sin_last)
    return (real_out, imag_out)


def inverse_transform(real_spec, imag_spec, tables):
    cos_section, sin_section, cos_twist, sin_twist, cos_last, sin_last = tables
    real_turn = exact_dot(real_spec, cos_last) - exact_dot(imag_spec, sin_last)
    imag_turn = exact_dot(imag_spec, cos_last) + exact_dot(real_spec, sin_last)
    real_first = real_turn * cos_twist - imag_turn * sin_twist
    imag_first = imag_turn * cos_twist + real_turn * sin_twist
    signal = jnp.einsum("kn,...km->...nm", cos_section, real_first, precision=highest) - jnp.einsum(
        "kn,...km->...nm", sin_section, imag_first, precision=highest
    )
    return signal / (cos_twist.shape[0] * cos_twist.shape[1])


def multiply(real_one, imag_one, real_two, imag_two):
    return (real_one * real_two - imag_one * imag_two, real_one * imag_two + imag_one * real_two)


def multiply_conj(real_one, imag_one, real_two, imag_two):
    return (real_one * real_two + imag_one * imag_two, imag_one * real_two - real_one * imag_two)


def to_channels(rows_in):
    return lax.all_to_all(rows_in.T, "seq", split_axis=0, concat_axis=1, tiled=True)


def to_rows(columns):
    return lax.all_to_all(columns, "seq", split_axis=1, concat_axis=0, tiled=True).T


def per_device(
    token_ids,
    embed_table,
    gain_one,
    bias_one,
    in_weight,
    in_bias,
    short_taps,
    short_bias,
    freq_weight,
    freq_bias,
    inner_weight,
    inner_bias,
    filter_weight,
    skip_scale,
    out_weight,
    out_bias,
    gain_two,
    bias_two,
    up_weight,
    up_bias,
    down_weight,
    down_bias,
    cotangent,
):
    in_full, out_full, up_full, down_full, filter_full = (
        lax.all_gather(in_weight.astype(jnp.bfloat16), ("dp", "seq"), axis=0, tiled=True),
        lax.all_gather(out_weight.astype(jnp.bfloat16), ("dp", "seq"), axis=0, tiled=True),
        lax.all_gather(up_weight.astype(jnp.bfloat16), ("dp", "seq"), axis=0, tiled=True),
        lax.all_gather(down_weight.astype(jnp.bfloat16), ("dp", "seq"), axis=0, tiled=True),
        lax.all_gather(filter_weight.astype(jnp.bfloat16), ("dp", "seq"), axis=0, tiled=True),
    )
    tokens = token_ids[0]
    row_count = tokens.shape[0]
    model_width = embed_table.shape[1]
    seq_parts = lax.axis_size("seq")
    seq_index = lax.axis_index("seq")
    local_width = model_width // seq_parts
    length = row_count * seq_parts
    freq_rows = 2 * seq_parts
    cos_section, sin_section = angle_table(freq_rows, seq_parts, freq_rows)
    cos_twist, sin_twist = angle_table(freq_rows, row_count, freq_rows * row_count)
    cos_last, sin_last = angle_table(row_count, row_count, row_count)
    tables = (cos_section, sin_section, cos_twist, sin_twist, cos_last, sin_last)
    onehot = (tokens[:, None] == jnp.arange(embed_table.shape[0], dtype=jnp.int32)[None, :]).astype(
        jnp.float32
    )
    hidden = exact_dot(onehot, embed_table)
    unit_one, inverse_one = normalize(hidden)
    normed = (unit_one * gain_one + bias_one).astype(jnp.bfloat16)
    projected = narrow_dot(normed, in_full) + in_bias
    before = passed_along(projected[row_count - 2 :], "seq", 1)
    padded = jnp.concatenate([before, projected], axis=0)
    mixed = (
        short_taps[0] * padded[:row_count]
        + short_taps[1] * padded[1 : row_count + 1]
        + short_taps[2] * padded[2:]
        + short_bias
    )
    gate_outer = mixed[:, :model_width]
    gate_inner = mixed[:, model_width : 2 * model_width]
    value_part = mixed[:, 2 * model_width :]
    count = (freq_weight.shape[0] - 1) // 2
    position_phase = jnp.arange(length, dtype=jnp.float32) / length
    levels = 0.0001 + jnp.arange(count, dtype=jnp.float32) * ((count - 1 - 0.0001) / (count - 1))
    angles = 2.0 * math.pi * position_phase[None, :] * levels[:, None]
    features = jnp.concatenate([position_phase[None, :], jnp.cos(angles), -jnp.sin(angles)], axis=0)
    first_pre = rows_inner(freq_weight, features, highest) + freq_bias[:, None]
    first_act = jnp.sin(first_pre)
    second_pre = rows_inner(inner_weight, first_act, highest) + inner_bias[:, None]
    second_act = jnp.sin(second_pre)
    channel = (seq_index * local_width + jnp.arange(local_width, dtype=jnp.int32)).astype(
        jnp.float32
    ) / (model_width - 1)
    decay_rate = slow_rate + (fast_rate - slow_rate) * channel
    decay = jnp.exp(-position_phase[None, :] * decay_rate[:, None]) + decay_shift
    low_rows = seq_index * local_width
    local_filter = jnp.concatenate(
        [
            lax.dynamic_slice_in_dim(filter_full, low_rows, local_width, 0),
            lax.dynamic_slice_in_dim(filter_full, model_width + low_rows, local_width, 0),
        ],
        axis=0,
    ).astype(jnp.float32)
    kernels = exact_dot(local_filter, second_act).reshape(2, local_width, length) * decay
    kernel_real, kernel_imag = forward_transform(
        kernels.reshape(2, local_width, seq_parts, row_count), tables
    )
    value_real, value_imag = forward_transform(
        to_channels(value_part).reshape(local_width, seq_parts, row_count), tables
    )
    first_real, first_imag = multiply(value_real, value_imag, kernel_real[0], kernel_imag[0])
    first_conv = (
        to_rows(inverse_transform(first_real, first_imag, tables).reshape(local_width, length))
        + skip_scale[0] * value_part
    )
    gated = gate_inner * first_conv
    gated_real, gated_imag = forward_transform(
        to_channels(gated).reshape(local_width, seq_parts, row_count), tables
    )
    second_real, second_imag = multiply(gated_real, gated_imag, kernel_real[1], kernel_imag[1])
    second_conv = (
        to_rows(inverse_transform(second_real, second_imag, tables).reshape(local_width, length))
        + skip_scale[1] * gated
    )
    mixer = (gate_outer * second_conv).astype(jnp.bfloat16)
    residual = hidden + narrow_dot(mixer, out_full) + out_bias
    unit_two, inverse_two = normalize(residual)
    normed_two = (unit_two * gain_two + bias_two).astype(jnp.bfloat16)
    lifted = narrow_dot(normed_two, up_full) + up_bias
    activated = jax.nn.gelu(lifted, approximate=False).astype(jnp.bfloat16)
    block_out = residual + narrow_dot(activated, down_full) + down_bias
    in_back, out_back, up_back, down_back = (in_full, out_full, up_full, down_full)
    seed = cotangent[0].astype(jnp.float32)
    grad_down_bias = jnp.sum(seed, axis=0)
    seed_low = seed.astype(jnp.bfloat16)
    grad_down = rows_inner(activated, seed_low)
    grad_activated = against_rows(seed_low, down_back)
    normal_cdf = 0.5 * (1.0 + lax.erf(lifted * (1.0 / math.sqrt(2.0))))
    normal_pdf = jnp.exp(-0.5 * lifted * lifted) * (1.0 / math.sqrt(2.0 * math.pi))
    grad_lifted = grad_activated * (normal_cdf + lifted * normal_pdf)
    grad_up_bias = jnp.sum(grad_lifted, axis=0)
    lifted_low = grad_lifted.astype(jnp.bfloat16)
    grad_up = rows_inner(normed_two, lifted_low)
    grad_normed_two = against_rows(lifted_low, up_back)
    grad_gain_two = jnp.sum(grad_normed_two * unit_two, axis=0)
    grad_bias_two = jnp.sum(grad_normed_two, axis=0)
    grad_residual = seed + norm_back(grad_normed_two * gain_two, unit_two, inverse_two)
    grad_out_bias = jnp.sum(grad_residual, axis=0)
    residual_low = grad_residual.astype(jnp.bfloat16)
    grad_out = rows_inner(mixer, residual_low)
    grad_mixer = against_rows(residual_low, out_back)
    grad_outer = grad_mixer * second_conv
    grad_second = grad_mixer * gate_outer
    skip_second = jnp.sum(grad_second * gated, axis=0)
    back_real, back_imag = forward_transform(
        to_channels(grad_second).reshape(local_width, seq_parts, row_count), tables
    )
    through_real, through_imag = multiply_conj(back_real, back_imag, kernel_real[1], kernel_imag[1])
    grad_gated = grad_second * skip_scale[1] + to_rows(
        inverse_transform(through_real, through_imag, tables).reshape(local_width, length)
    )
    cross_real, cross_imag = multiply_conj(back_real, back_imag, gated_real, gated_imag)
    kernel_grad_two = inverse_transform(cross_real, cross_imag, tables).reshape(local_width, length)
    grad_inner_gate = grad_gated * first_conv
    grad_first = grad_gated * gate_inner
    skip_first = jnp.sum(grad_first * value_part, axis=0)
    early_real, early_imag = forward_transform(
        to_channels(grad_first).reshape(local_width, seq_parts, row_count), tables
    )
    passed_real, passed_imag = multiply_conj(early_real, early_imag, kernel_real[0], kernel_imag[0])
    grad_value = grad_first * skip_scale[0] + to_rows(
        inverse_transform(passed_real, passed_imag, tables).reshape(local_width, length)
    )
    match_real, match_imag = multiply_conj(early_real, early_imag, value_real, value_imag)
    kernel_grad_one = inverse_transform(match_real, match_imag, tables).reshape(local_width, length)
    grad_mixed = jnp.concatenate([grad_outer, grad_inner_gate, grad_value], axis=1)
    grad_short_bias = jnp.sum(grad_mixed, axis=0)
    grad_taps = jnp.stack(
        [
            jnp.sum(padded[:row_count] * grad_mixed, axis=0),
            jnp.sum(padded[1 : row_count + 1] * grad_mixed, axis=0),
            jnp.sum(padded[2:] * grad_mixed, axis=0),
        ]
    )
    after = passed_along(grad_mixed[:2], "seq", -1)
    grad_padded = jnp.concatenate([grad_mixed, after], axis=0)
    grad_projected = (
        short_taps[2] * grad_padded[:row_count]
        + short_taps[1] * grad_padded[1 : row_count + 1]
        + short_taps[0] * grad_padded[2:]
    )
    grad_in_bias = jnp.sum(grad_projected, axis=0)
    projected_low = grad_projected.astype(jnp.bfloat16)
    grad_in = rows_inner(normed, projected_low)
    grad_normed = against_rows(projected_low, in_back)
    grad_gain_one = jnp.sum(grad_normed * unit_one, axis=0)
    grad_bias_one = jnp.sum(grad_normed, axis=0)
    grad_hidden = grad_residual + norm_back(grad_normed * gain_one, unit_one, inverse_one)
    grad_embed = rows_inner(onehot, grad_hidden, highest)
    raw_grads = (jnp.stack([kernel_grad_one, kernel_grad_two]) * decay).reshape(
        2 * local_width, length
    )
    grad_local_filter = against_rows(raw_grads, second_act, highest)
    grad_second_act = rows_inner(local_filter, raw_grads, highest)
    grad_second_pre = grad_second_act * jnp.cos(second_pre)
    grad_inner_weight = against_rows(first_act, grad_second_pre, highest)
    grad_inner_bias = jnp.sum(grad_second_pre, axis=1)
    grad_first_pre = exact_dot(inner_weight, grad_second_pre) * jnp.cos(first_pre)
    grad_freq_weight = against_rows(features, grad_first_pre, highest)
    grad_freq_bias = jnp.sum(grad_first_pre, axis=1)
    grad_filter = jnp.zeros((2 * model_width, local_filter.shape[1]), jnp.float32)
    grad_filter = lax.dynamic_update_slice_in_dim(
        grad_filter, grad_local_filter[:local_width], low_rows, 0
    )
    grad_filter = lax.dynamic_update_slice_in_dim(
        grad_filter, grad_local_filter[local_width:], model_width + low_rows, 0
    )
    grad_skip = jnp.stack([skip_first, skip_second])
    sum_in, sum_out, sum_up, sum_down, sum_filter = (
        lax.psum_scatter(grad_in, ("dp", "seq"), scatter_dimension=0, tiled=True),
        lax.psum_scatter(grad_out, ("dp", "seq"), scatter_dimension=0, tiled=True),
        lax.psum_scatter(grad_up, ("dp", "seq"), scatter_dimension=0, tiled=True),
        lax.psum_scatter(grad_down, ("dp", "seq"), scatter_dimension=0, tiled=True),
        lax.psum_scatter(grad_filter, ("dp", "seq"), scatter_dimension=0, tiled=True),
    )
    (
        sum_embed,
        sum_gain_one,
        sum_bias_one,
        sum_in_bias,
        sum_taps,
        sum_short_bias,
        sum_freq_weight,
        sum_freq_bias,
        sum_inner_weight,
        sum_inner_bias,
        sum_skip,
        sum_out_bias,
        sum_gain_two,
        sum_bias_two,
        sum_up_bias,
        sum_down_bias,
    ) = lax.psum(
        (
            grad_embed,
            grad_gain_one,
            grad_bias_one,
            grad_in_bias,
            grad_taps,
            grad_short_bias,
            grad_freq_weight,
            grad_freq_bias,
            grad_inner_weight,
            grad_inner_bias,
            grad_skip,
            grad_out_bias,
            grad_gain_two,
            grad_bias_two,
            grad_up_bias,
            grad_down_bias,
        ),
        ("dp", "seq"),
    )
    return (
        block_out[None],
        sum_embed,
        sum_gain_one,
        sum_bias_one,
        sum_in,
        sum_in_bias,
        sum_taps,
        sum_short_bias,
        sum_freq_weight,
        sum_freq_bias,
        sum_inner_weight,
        sum_inner_bias,
        sum_filter,
        sum_skip,
        sum_out,
        sum_out_bias,
        sum_gain_two,
        sum_bias_two,
        sum_up,
        sum_up_bias,
        sum_down,
        sum_down_bias,
    )


def solution(mesh):
    in_specs = (
        P("dp", "seq"),
        P(),
        P(),
        P(),
        P(("dp", "seq"), None),
        P(),
        P(),
        P(),
        P(),
        P(),
        P(),
        P(),
        P(("dp", "seq"), None),
        P(),
        P(("dp", "seq"), None),
        P(),
        P(),
        P(),
        P(("dp", "seq"), None),
        P(),
        P(("dp", "seq"), None),
        P(),
        P("dp", "seq", None),
    )
    out_specs = (
        P("dp", "seq", None),
        P(),
        P(),
        P(),
        P(("dp", "seq"), None),
        P(),
        P(),
        P(),
        P(),
        P(),
        P(),
        P(),
        P(("dp", "seq"), None),
        P(),
        P(("dp", "seq"), None),
        P(),
        P(),
        P(),
        P(("dp", "seq"), None),
        P(),
        P(("dp", "seq"), None),
        P(),
    )
    return jax.shard_map(
        per_device, mesh=mesh, in_specs=in_specs, out_specs=out_specs, check_vma=False
    )
```

profile of v0, /device:TPU:0, one launch (start us, length us, event | category | flops | bytes accessed | tf_op | source)
XLA Modules:
  0.0 1201.7 jit_solution(17319521566536501723)
XLA Ops:
  15.9 44.8 %all_gather.16 = bf16[1536,64]{1,0:T(8,128)(2,1)S(1)} all-gather(bf16[48,64]{1,0:T(8,128)(2,1)S(1)} %convert_element_type.291), channel_id=1, replica_groups=mesh['dp'=2,'seq'=16] {'dp','seq'}, dimensions={0}, use_global_device_ids=true | all-gather | bytes 202752 | tf_op jit(solution)/shard_map/all_gather | solution.py:142
  61.3 3.2 fusion.613
  64.6 3.2 fusion.614
  71.7 2.8 fusion.85
  74.6 2.8 convolution_add_fusion
  77.4 2.2 collective-permute-start
  81.8 1.8 slice_bitcast_fusion.4
  83.5 1.9 copy.73
  85.4 6.8 all-to-all-start
  92.3 4.2 convolution_add_fusion.4
  98.2 2.9 convolution_subtract_fusion
  101.1 3.2 all-to-all-done
  104.3 1.9 fusion.19
  106.2 1.9 convolution_bitcast_fusion.4
  112.1 2.1 multiply_subtract_fusion.8
  115.2 13.1 %convolution_add_fusion.13 = f32[48,32,128]{2,1,0:T(8,128)S(1)} fusion(f32[48,32,128]{2,1,0:T(8,128)S(1)} %fusion.221, f32[48,32,128]{2,1,0:T(8,128)S(1)} %get-tuple-element.69), kind=kOutput, calls=%fused_computation.56 | convolution fusion | flops 302415872 | bytes 2359296 | tf_op jit(solution)/shard_map/dot_general | solution.py:22
  132.5 3.6 all-to-all-start.1
  136.2 12.2 %all-to-all-done.1 = f32[48,16,128]{2,0,1:T(8,128)S(1)} async-done(((f32[48,16,128]{2,0,1:T(8,128)}), f32[48,16,128]{2,0,1:T(8,128)S(1)}, u32[]{:S(2)}, u32[]{:S(2)}) %all-to-all-start.1) | async-done | bytes 393248 | tf_op jit(solution)/shard_map/all_to_all | solution.py:109
  151.5 19.8 %all_to_all.128 = f32[16,48,128]{2,1,0:T(8,128)S(1)} all-to-all(f32[16,48,128]{2,1,0:T(8,128)} %bitcast.400), channel_id=1, replica_groups=mesh['dp'=2,'seq'=16] {'seq'}, dimensions={0} | all-to-all | bytes 786432 | tf_op jit(solution)/shard_map/all_to_all | solution.py:105
  176.6 2.1 multiply_subtract_fusion.6
  184.2 22.9 %all_to_all.129 = f32[48,16,128]{2,0,1:T(8,128)} all-to-all(f32[48,16,128]{2,0,1:T(8,128)S(1)} %copy.79), channel_id=1, replica_groups=mesh['dp'=2,'seq'=16] {'seq'}, dimensions={1} | all-to-all | bytes 786432 | tf_op jit(solution)/shard_map/all_to_all | solution.py:109
  207.2 1.9 copy.80
  212.3 7.8 fusion.2
  220.2 52.4 %all-gather.11.cloned.1.call-done = bf16[3072,768]{1,0:T(8,128)(2,1)} async-done(((bf16[96,768]{1,0:T(8,128)(2,1)}), bf16[3072,768]{1,0:T(8,128)(2,1)}) %all-gather.11.cloned.1.call-update) | async-done | bytes 4718608 | tf_op jit(solution)/shard_map/all_gather | solution.py:141
  272.6 5.4 fusion.618
  277.9 2.3 multiply_reduce_fusion.3
  281.4 2.4 multiply_reduce_fusion.4
  283.8 1.9 copy.81
  285.8 4.7 all-to-all-start.4
  291.3 11.3 all-to-all-done.4
  302.7 1.9 fusion.17
  304.5 1.9 convolution_bitcast_fusion.1
  310.3 2.6 multiply_add_fusion
  319.2 4.2 all-to-all-start.5
  323.4 2.2 fusion.195
  325.7 1.9 fusion.197
  327.6 1.9 convolution_add_fusion.5
  329.5 6.2 all-to-all-done.5
  335.6 1.9 copy.84
  337.5 2.5 multiply_reduce_fusion.5
  340.0 1.9 copy.85
  341.9 4.6 all-to-all-start.6
  346.5 2.5 convolution_subtract_fusion.1
  351.1 1.8 stack_reshape.7
  353.5 4.8 all-to-all-done.6
  358.3 1.9 fusion.16
  360.2 1.9 convolution_bitcast_fusion
  365.8 2.5 multiply_add_fusion.1
  374.8 4.2 all-to-all-start.7
  386.9 2.7 fusion.617
  389.9 4.2 fusion.616
  402.4 2.8 multiply_reduce_fusion.2
  405.2 1.9 multiply_reduce_fusion.6
  409.0 1.9 fusion.164
  412.0 4.1 fusion.140
  417.3 5.2 fusion.101
  423.6 5.1 fusion.153
  429.4 3.9 fusion.22
  433.3 64.0 %reduce-scatter.8.cloned.1.call-done = f32[48,64]{1,0:T(8,128)} async-done(((f32[1536,64]{1,0:T(8,128)}), f32[48,64]{1,0:T(8,128)}) %reduce-scatter.8.cloned.1.call-update) | async-done | bytes 12304 | tf_op jit(solution)/shard_map/reduce_scatter | solution.py:316
  497.3 159.9 %all-reduce.3.cloned.1.call-done = (f32[12,768]{1,0:T(8,128)}, f32[768]{0:T(1024)}, f32[768]{0:T(1024)}, f32[2304]{0:T(1024)}, f32[3,2304]{1,0:T(4,128)}, /*inde...) async-done(((f32[12,768]{1,0:T(8,128)}, f32[768]{0:T(1024)}, ...) | async-done | bytes 145168 | tf_op jit(solution)/shard_map/psum | solution.py:335
  657.2 108.1 %reduce-scatter.10.cloned.1.call-done = f32[24,768]{1,0:T(8,128)} async-done(((f32[768,768]{1,0:T(8,128)}), f32[24,768]{1,0:T(8,128)}) %reduce-scatter.10.cloned.1.call-update) | async-done | bytes 73744 | tf_op jit(solution)/shard_map/reduce_scatter | solution.py:313
  765.3 125.3 %reduce-scatter.6.cloned.1.call-done = f32[24,2304]{1,0:T(8,128)} async-done(((f32[768,2304]{1,0:T(8,128)}), f32[24,2304]{1,0:T(8,128)}) %reduce-scatter.6.cloned.1.call-update) | async-done | bytes 221200 | tf_op jit(solution)/shard_map/reduce_scatter | solution.py:312
  890.7 141.4 %reduce-scatter.12.cloned.1.call-done = f32[24,3072]{1,0:T(8,128)} async-done(((f32[768,3072]{1,0:T(8,128)}), f32[24,3072]{1,0:T(8,128)}) %reduce-scatter.12.cloned.1.call-update) | async-done | bytes 294928 | tf_op jit(solution)/shard_map/reduce_scatter | solution.py:314
  1032.1 142.0 %reduce-scatter.14.cloned.1.call-done = f32[96,768]{1,0:T(8,128)} async-done(((f32[3072,768]{1,0:T(8,128)}), f32[96,768]{1,0:T(8,128)}) %reduce-scatter.14.cloned.1.call-update) | async-done | bytes 294928 | tf_op jit(solution)/shard_map/reduce_scatter | solution.py:315
  (336 shorter events, 110.6 us)
Async XLA Ops:
  7.2 7.5 copy-start
  7.2 7.5 copy-start.82
  7.2 8.7 copy-start.72
  7.2 67.3 %all-gather.5.cloned.1.call-start = ((), (), s32[]{:S(2)}) async-start(), calls=%async_computation.13 | async-start | bytes 3649536 | tf_op jit(solution)/shard_map/all_gather | solution.py:138
  8.9 52.5 %copy-start.74 = (f32[33,64]{1,0:T(8,128)S(1)}, f32[33,64]{1,0:T(8,128)}, u32[]{:S(2)}) copy-start(f32[33,64]{1,0:T(8,128)} %param.31) | copy-start | bytes 25348
  8.9 52.5 %copy-start.86 = (f32[64]{0:T(128)S(1)}, f32[64]{0:T(128)}, u32[]{:S(2)}) copy-start(f32[64]{0:T(128)} %param.32) | copy-start | bytes 772
  8.9 201.4 %all-gather.7.cloned.1.call-start = ((), (), s32[]{:S(2)}) async-start(), calls=%async_computation.14 | async-start | bytes 1216512 | tf_op jit(solution)/shard_map/all_gather | solution.py:139
  10.5 201.8 %all-gather.9.cloned.1.call-start = ((), (), s32[]{:S(2)}) async-start(), calls=%async_computation.15 | async-start | bytes 4866048 | tf_op jit(solution)/shard_map/all_gather | solution.py:140
  12.2 260.4 %all-gather.11.cloned.1.call-start = ((), (), s32[]{:S(2)}) async-start(), calls=%async_computation.16 | async-start | bytes 4866048 | tf_op jit(solution)/shard_map/all_gather | solution.py:141
  13.9 50.7 %copy-start.54 = (f32[64,64]{1,0:T(8,128)S(1)}, f32[64,64]{1,0:T(8,128)}, u32[]{:S(2)}) copy-start(f32[64,64]{1,0:T(8,128)} %param.33) | copy-start | bytes 49156
  13.9 50.7 %copy-start.87 = (f32[64]{0:T(128)S(1)}, f32[64]{0:T(128)}, u32[]{:S(2)}) copy-start(f32[64]{0:T(128)} %param.34) | copy-start | bytes 772
  14.7 53.1 %copy-start.69 = (f32[1,2048]{1,0:T(1,128)}, f32[1,2048]{1,0:T(1,128)S(1)}, u32[]{:S(2)}) copy-start(f32[1,2048]{1,0:T(1,128)S(1)} %iota_multiply_fusion.1) | copy-start | bytes 24580
  15.9 52.6 %copy-start.84 = (f32[48]{0:T(128)}, f32[48]{0:T(128)S(1)}, u32[]{:S(2)}) copy-start(f32[48]{0:T(128)S(1)} %multiply_add_fusion.18) | copy-start | bytes 580
  61.3 7.0 copy-start.46
  61.3 7.0 copy-start.48
  64.6 3.9 copy-start.30
  74.6 5.0 copy-start.73
  74.6 5.8 copy-start.78
  77.3 3.0 copy-start.11
  77.4 3.0 collective-permute-start
  85.4 18.9 %all-to-all-start = ((f32[16,48,128]{2,1,0:T(8,128)}), f32[16,48,128]{2,1,0:T(8,128)}, u32[]{:S(2)}, u32[]{:S(2)}) async-start(f32[16,48,128]{2,1,0:T(8,128)} %bitcast.396), calls=%async_computation | async-start | bytes 786432 | tf_op jit(solution)/shard_map/all_to_all | solution.py:105
  92.3 4.2 copy-start.3
  101.1 7.0 copy-start.4
  131.0 5.2 copy-start.79
  132.5 15.8 %all-to-all-start.1 = ((f32[48,16,128]{2,0,1:T(8,128)}), f32[48,16,128]{2,0,1:T(8,128)S(1)}, u32[]{:S(2)}, u32[]{:S(2)}) async-start(f32[48,16,128]{2,0,1:T(8,128)} %copy.75), calls=%async_computation.1 | async-start | bytes 786432 | tf_op jit(solution)/shard_map/all_to_all | solution.py:109
  150.6 58.5 %copy-start.20 = (f32[128,768]{1,0:T(8,128)}, f32[128,768]{1,0:T(8,128)S(1)}, u32[]{:S(2)}) copy-start(f32[128,768]{1,0:T(8,128)S(1)} %slice_multiply_fusion.3) | copy-start | bytes 1179652
  184.2 26.1 %copy-start.80 = (f32[768]{0:T(1024)S(1)}, f32[768]{0:T(1024)}, u32[]{:S(2)}) copy-start(f32[768]{0:T(1024)} %param.38) | copy-start | bytes 9220
  210.2 9.9 copy-start.44
  272.6 5.4 copy-start.32
  277.9 3.2 copy-start.29
  281.1 2.7 copy-start.24
  283.8 6.6 copy-start.85
  285.8 16.9 %all-to-all-start.4 = ((f32[16,48,128]{2,1,0:T(8,128)}), f32[16,48,128]{2,1,0:T(8,128)}, u32[]{:S(2)}, u32[]{:S(2)}) async-start(f32[16,48,128]{2,1,0:T(8,128)} %bitcast.398), calls=%async_computation.4 | async-start | bytes 786432 | tf_op jit(solution)/shard_map/all_to_all | solution.py:105
  319.2 16.4 %all-to-all-start.5 = ((f32[48,16,128]{2,0,1:T(8,128)}), f32[48,16,128]{2,0,1:T(8,128)}, u32[]{:S(2)}, u32[]{:S(2)}) async-start(f32[48,16,128]{2,0,1:T(8,128)} %copy.83), calls=%async_computation.5 | async-start | bytes 786432 | tf_op jit(solution)/shard_map/all_to_all | solution.py:109
  341.9 16.4 %all-to-all-start.6 = ((f32[16,48,128]{2,1,0:T(8,128)}), f32[16,48,128]{2,1,0:T(8,128)}, u32[]{:S(2)}, u32[]{:S(2)}) async-start(f32[16,48,128]{2,1,0:T(8,128)} %bitcast.395), calls=%async_computation.6 | async-start | bytes 786432 | tf_op jit(solution)/shard_map/all_to_all | solution.py:105
  346.5 2.5 copy-start.18
  373.3 5.8 copy-start.15
  373.9 6.2 copy-start.16
  374.8 21.7 %all-to-all-start.7 = ((f32[48,16,128]{2,0,1:T(8,128)}), f32[48,16,128]{2,0,1:T(8,128)}, u32[]{:S(2)}, u32[]{:S(2)}) async-start(f32[48,16,128]{2,0,1:T(8,128)} %copy.87), calls=%async_computation.7 | async-start | bytes 786432 | tf_op jit(solution)/shard_map/all_to_all | solution.py:109
  379.1 118.3 %reduce-scatter.8.cloned.1.call-start = ((), (), s32[]{:S(2)}) async-start(), calls=%async_computation.18 | async-start | bytes 811008 | tf_op jit(solution)/shard_map/reduce_scatter | solution.py:316
  386.9 3.0 copy-start.55
  389.6 4.6 copy-start.47
  389.6 4.6 copy-start.49
  389.6 4.6 copy-start.70
  389.8 5.5 copy-start.31
  389.9 4.3 copy-start.42
  394.2 3.5 copy-start.37
  395.4 2.4 copy-start.26
  397.9 3.1 collective-permute-start.1
  399.8 2.5 copy-start.12
  399.8 2.5 copy-start.57
  399.8 2.5 copy-start.59
  399.8 2.5 copy-start.61
  399.8 2.5 copy-start.68
  399.9 257.4 %all-reduce.3.cloned.1.call-start = ((), (), s32[]{:S(2)}) async-start(), calls=%async_computation.22 | async-start | bytes 415744 | tf_op jit(solution)/shard_map/psum | solution.py:335
  402.4 2.8 copy-start.10
  402.4 2.8 copy-start.52
  402.4 2.8 copy-start.76
  402.4 2.8 copy-start.77
  409.0 356.4 %reduce-scatter.10.cloned.1.call-start = ((), (), s32[]{:S(2)}) async-start(), calls=%async_computation.19 | async-start | bytes 2433024 | tf_op jit(solution)/shard_map/reduce_scatter | solution.py:313
  410.9 479.7 %reduce-scatter.6.cloned.1.call-start = ((), (), s32[]{:S(2)}) async-start(), calls=%async_computation.17 | async-start | bytes 7299072 | tf_op jit(solution)/shard_map/reduce_scatter | solution.py:312
  416.1 615.9 %reduce-scatter.12.cloned.1.call-start = ((), (), s32[]{:S(2)}) async-start(), calls=%async_computation.20 | async-start | bytes 9732096 | tf_op jit(solution)/shard_map/reduce_scatter | solution.py:314
  422.4 751.6 %reduce-scatter.14.cloned.1.call-start = ((), (), s32[]{:S(2)}) async-start(), calls=%async_computation.21 | async-start | bytes 9732096 | tf_op jit(solution)/shard_map/reduce_scatter | solution.py:315
  429.4 765.3 %copy-start.1 = (f32[12,768]{1,0:T(8,128)S(1)}, f32[12,768]{1,0:T(8,128)}, u32[]{:S(2)}) copy-start(f32[12,768]{1,0:T(8,128)} %param.24) | copy-start | bytes 110596
  (43 other events, 71.6 us)
Sparse Core Ops, SparseCore 0:
  11.5 62.9 all-gather.4
  78.0 54.3 all-gather.6
  135.9 71.8 all-gather.8
  211.2 61.3 all-gather.10
  400.0 97.2 reduce-scatter.7
  505.3 151.8 all-reduce.2
  665.2 100.0 reduce-scatter.9
  772.5 118.0 reduce-scatter.5
  897.1 134.8 reduce-scatter.11
  1039.4 134.5 reduce-scatter.13
where the time goes:
time: 1210 us; the launch traced here: 1200 us
  waiting for transfers between devices  833 us (69%)
  matrix products  162 us (13%)
  blocking collectives  87.6 us (7%)
  local copies, waits for them, and re-layouts  47.7 us (4%)
  starting transfers between devices  32 us (3%)
  other arithmetic  23.5 us (2%)
  between operations  16 us (1%)
    psum x1, waiting for transfers between devices, per_device(): lax.psum((grad_embed, grad_gain_one, grad_bias_one, grad_in_bias, grad_ta...  160 us
    reduce_scatter x1, waiting for transfers between devices, per_device(): lax.psum_scatter(grad_down, ('dp', 'seq'), scatter_dimension=0, tiled=True)  142 us
    reduce_scatter x1, waiting for transfers between devices, per_device(): lax.psum_scatter(grad_up, ('dp', 'seq'), scatter_dimension=0, tiled=True)  141 us
    reduce_scatter x1, waiting for transfers between devices, per_device(): lax.psum_scatter(grad_in, ('dp', 'seq'), scatter_dimension=0, tiled=True)  125 us
    reduce_scatter x1, waiting for transfers between devices, per_device(): lax.psum_scatter(grad_out, ('dp', 'seq'), scatter_dimension=0, tiled=True)  108 us
    dot_general x47, matrix products, exact_dot(): jnp.dot(left_side, right_side, precision=highest, preferred_element_type=...  79.5 us
    reduce_scatter x1, waiting for transfers between devices, per_device(): lax.psum_scatter(grad_filter, ('dp', 'seq'), scatter_dimension=0, tiled=T...  64 us
    all_gather x1, waiting for transfers between devices, per_device(): lax.all_gather(down_weight.astype(jnp.bfloat16), ('dp', 'seq'), axis=0, t...  52.4 us
  transfers between devices with their start and end apart: 18, of which 15 were waited for; matrix products, arithmetic and copies ran while one was open for 13% of the time, Pallas kernels for 0%

commit v1 on v0

v1 whole, which is shorter than its diff:
```python
import math
from types import SimpleNamespace

import jax
import jax.numpy as jnp
import ml_dtypes
import numpy as np
from jax import lax
from jax.experimental import pallas as pl
from jax.experimental.pallas import tpu as pltpu
from jax.sharding import PartitionSpec as P

epsilon = 1e-05
slow_rate = -math.log(0.01) / 1.5
fast_rate = -math.log(0.01) / 0.3
decay_shift = 0.05
highest = lax.Precision.HIGHEST


def exact_dot(left_side, right_side):
    return jnp.dot(left_side, right_side, precision=highest, preferred_element_type=jnp.float32)


def narrow_dot(left_side, right_side):
    return jnp.dot(left_side, right_side, preferred_element_type=jnp.float32)


def rows_inner(left_side, right_side, accuracy=None):
    return lax.dot_general(
        left_side,
        right_side,
        (((0,), (0,)), ((), ())),
        precision=accuracy,
        preferred_element_type=jnp.float32,
    )


def against_rows(left_side, right_side, accuracy=None):
    return lax.dot_general(
        left_side,
        right_side,
        (((1,), (1,)), ((), ())),
        precision=accuracy,
        preferred_element_type=jnp.float32,
    )


def normalize(values):
    center = values - jnp.mean(values, axis=-1, keepdims=True)
    inverse = lax.rsqrt(jnp.mean(center * center, axis=-1, keepdims=True) + epsilon)
    return (center * inverse, inverse)


def norm_back(upstream, unit_vals, inverse):
    return inverse * (
        upstream
        - jnp.mean(upstream, axis=-1, keepdims=True)
        - unit_vals * jnp.mean(upstream * unit_vals, axis=-1, keepdims=True)
    )


def angle_table(row_count, column_count, modulus):
    product = (
        jnp.arange(row_count, dtype=jnp.int32)[:, None]
        * jnp.arange(column_count, dtype=jnp.int32)[None, :]
        % modulus
    )
    angles = 2.0 * math.pi / modulus * product.astype(jnp.float32)
    return (jnp.cos(angles), jnp.sin(angles))


def forward_transform(signal, tables):
    cos_section, sin_section, cos_twist, sin_twist, cos_last, sin_last = tables
    real_first = jnp.einsum("kn,...nm->...km", cos_section, signal, precision=highest)
    imag_first = -jnp.einsum("kn,...nm->...km", sin_section, signal, precision=highest)
    real_turn = real_first * cos_twist + imag_first * sin_twist
    imag_turn = imag_first * cos_twist - real_first * sin_twist
    real_out = exact_dot(real_turn, cos_last) + exact_dot(imag_turn, sin_last)
    imag_out = exact_dot(imag_turn, cos_last) - exact_dot(real_turn, sin_last)
    return (real_out, imag_out)


def inverse_transform(real_spec, imag_spec, tables):
    cos_section, sin_section, cos_twist, sin_twist, cos_last, sin_last = tables
    real_turn = exact_dot(real_spec, cos_last) - exact_dot(imag_spec, sin_last)
    imag_turn = exact_dot(imag_spec, cos_last) + exact_dot(real_spec, sin_last)
    real_first = real_turn * cos_twist - imag_turn * sin_twist
    imag_first = imag_turn * cos_twist + real_turn * sin_twist
    signal = jnp.einsum("kn,...km->...nm", cos_section, real_first, precision=highest) - jnp.einsum(
        "kn,...km->...nm", sin_section, imag_first, precision=highest
    )
    return signal / (cos_twist.shape[0] * cos_twist.shape[1])


def multiply(real_one, imag_one, real_two, imag_two):
    return (real_one * real_two - imag_one * imag_two, real_one * imag_two + imag_one * real_two)


def multiply_conj(real_one, imag_one, real_two, imag_two):
    return (real_one * real_two + imag_one * imag_two, imag_one * real_two - real_one * imag_two)


def to_channels(rows_in):
    return lax.all_to_all(rows_in.T, "seq", split_axis=0, concat_axis=1, tiled=True)


def to_rows(columns):
    return lax.all_to_all(columns, "seq", split_axis=1, concat_axis=0, tiled=True).T


def gather_all(pieces):
    shapes = [piece.shape for piece in pieces]
    flat = jnp.concatenate([piece.astype(jnp.bfloat16).reshape(-1) for piece in pieces])
    whole = lax.all_gather(flat, ("dp", "seq"), axis=0, tiled=False)
    result, start = [], 0
    for shape in shapes:
        size = math.prod(shape)
        result.append(whole[:, start : start + size].reshape((-1,) + shape[1:]))
        start += size
    return result


def per_device(
    token_ids,
    embed_table,
    gain_one,
    bias_one,
    in_weight,
    in_bias,
    short_taps,
    short_bias,
    freq_weight,
    freq_bias,
    inner_weight,
    inner_bias,
    filter_weight,
    skip_scale,
    out_weight,
    out_bias,
    gain_two,
    bias_two,
    up_weight,
    up_bias,
    down_weight,
    down_bias,
    cotangent,
):
    tokens = token_ids[0]
    row_count = tokens.shape[0]
    vocab, model_width = embed_table.shape
    seq_parts = lax.axis_size("seq")
    seq_index = lax.axis_index("seq")
    dp_index = lax.axis_index("dp")
    local_width = model_width // seq_parts
    length = row_count * seq_parts
    freq_rows = 2 * seq_parts
    low_rows = seq_index * local_width

    def own_channels(table):
        parts = table.reshape(table.shape[0], -1, model_width)
        return lax.dynamic_slice_in_dim(parts, low_rows, local_width, 2)

    in_full, out_full, up_full, down_full, filter_full, tokens_full = gather_all(
        (in_weight, out_weight, up_weight, down_weight, filter_weight, token_ids)
    )
    sequence = lax.dynamic_slice_in_dim(
        tokens_full.reshape(-1, length), dp_index, 1, 0
    )[0].astype(jnp.int32)
    cos_section, sin_section = angle_table(freq_rows, seq_parts, freq_rows)
    cos_twist, sin_twist = angle_table(freq_rows, row_count, freq_rows * row_count)
    cos_last, sin_last = angle_table(row_count, row_count, row_count)
    tables = (cos_section, sin_section, cos_twist, sin_twist, cos_last, sin_last)

    unit_one, inverse_one = normalize(embed_table)
    normed = (unit_one * gain_one + bias_one).astype(jnp.bfloat16)
    table = narrow_dot(normed, in_full) + in_bias
    local_table = own_channels(table)
    local_taps = own_channels(short_taps)
    local_bias = own_channels(short_bias[None])[0]
    local_skip = own_channels(skip_scale)[:, 0, :, None]
    ids = jnp.arange(vocab, dtype=jnp.int32)[:, None]
    padded = jnp.concatenate([jnp.full((2,), -1, jnp.int32), sequence])
    shifted = jnp.concatenate(
        [(padded[None, j : j + length] == ids).astype(jnp.float32) for j in range(3)], axis=0
    )
    weights = (local_taps[:, None] * local_table[None]).reshape(3 * vocab, 3 * local_width)
    mixed = rows_inner(weights, shifted, highest) + local_bias.reshape(-1, 1)
    gate_outer = mixed[:local_width]
    gate_inner = mixed[local_width : 2 * local_width]
    value_part = mixed[2 * local_width :]

    count = (freq_weight.shape[0] - 1) // 2
    position_phase = jnp.arange(length, dtype=jnp.float32) / length
    levels = 0.0001 + jnp.arange(count, dtype=jnp.float32) * ((count - 1 - 0.0001) / (count - 1))
    angles = 2.0 * math.pi * position_phase[None, :] * levels[:, None]
    features = jnp.concatenate([position_phase[None, :], jnp.cos(angles), -jnp.sin(angles)], axis=0)
    first_pre = rows_inner(freq_weight, features, highest) + freq_bias[:, None]
    first_act = jnp.sin(first_pre)
    second_pre = rows_inner(inner_weight, first_act, highest) + inner_bias[:, None]
    second_act = jnp.sin(second_pre)
    channel = (low_rows + jnp.arange(local_width, dtype=jnp.int32)).astype(jnp.float32) / (
        model_width - 1
    )
    decay_rate = slow_rate + (fast_rate - slow_rate) * channel
    decay = jnp.exp(-position_phase[None, :] * decay_rate[:, None]) + decay_shift
    local_filter = lax.dynamic_slice_in_dim(
        filter_full.reshape(2, model_width, -1), low_rows, local_width, 1
    ).astype(jnp.float32).reshape(2 * local_width, -1)
    kernels = exact_dot(local_filter, second_act).reshape(2, local_width, length) * decay

    def forth(signal):
        shape = signal.shape[:-1] + (seq_parts, row_count)
        return forward_transform(signal.reshape(shape), tables)

    def back(real_spec, imag_spec):
        result = inverse_transform(real_spec, imag_spec, tables)
        return result.reshape(result.shape[:-2] + (length,))

    kernel_real, kernel_imag = forth(kernels)
    value_real, value_imag = forth(value_part)
    first_conv = (
        back(*multiply(value_real, value_imag, kernel_real[0], kernel_imag[0]))
        + local_skip[0] * value_part
    )
    gated = gate_inner * first_conv
    gated_real, gated_imag = forth(gated)
    second_conv = (
        back(*multiply(gated_real, gated_imag, kernel_real[1], kernel_imag[1]))
        + local_skip[1] * gated
    )
    mixer = to_rows((gate_outer * second_conv).astype(jnp.bfloat16))

    onehot = (tokens[:, None] == ids[:, 0][None, :]).astype(jnp.float32)
    hidden = exact_dot(onehot, embed_table)
    residual = hidden + narrow_dot(mixer, out_full) + out_bias
    unit_two, inverse_two = normalize(residual)
    normed_two = (unit_two * gain_two + bias_two).astype(jnp.bfloat16)
    lifted = narrow_dot(normed_two, up_full) + up_bias
    normal_cdf = 0.5 * (1.0 + lax.erf(lifted * (1.0 / math.sqrt(2.0))))
    activated = (lifted * normal_cdf).astype(jnp.bfloat16)
    block_out = residual + narrow_dot(activated, down_full) + down_bias
    seed_low = cotangent[0]
    seed = seed_low.astype(jnp.float32)
    grad_down_bias = jnp.sum(seed, axis=0)
    grad_down = rows_inner(activated, seed_low)
    grad_activated = against_rows(seed_low, down_full)
    normal_pdf = jnp.exp(-0.5 * lifted * lifted) * (1.0 / math.sqrt(2.0 * math.pi))
    grad_lifted = grad_activated * (normal_cdf + lifted * normal_pdf)
    grad_up_bias = jnp.sum(grad_lifted, axis=0)
    lifted_low = grad_lifted.astype(jnp.bfloat16)
    grad_up = rows_inner(normed_two, lifted_low)
    grad_normed_two = against_rows(lifted_low, up_full)
    grad_gain_two = jnp.sum(grad_normed_two * unit_two, axis=0)
    grad_bias_two = jnp.sum(grad_normed_two, axis=0)
    grad_residual = seed + norm_back(grad_normed_two * gain_two, unit_two, inverse_two)
    grad_out_bias = jnp.sum(grad_residual, axis=0)
    residual_low = grad_residual.astype(jnp.bfloat16)
    grad_out = rows_inner(mixer, residual_low)
    grad_mixer = to_channels(against_rows(residual_low, out_full).astype(jnp.bfloat16)).astype(
        jnp.float32
    )
    embed_sum = rows_inner(onehot, grad_residual, highest)

    grad_outer = grad_mixer * second_conv
    grad_second = grad_mixer * gate_outer
    skip_second = jnp.sum(grad_second * gated, axis=1)
    back_real, back_imag = forth(grad_second)
    grad_gated = grad_second * local_skip[1] + back(
        *multiply_conj(back_real, back_imag, kernel_real[1], kernel_imag[1])
    )
    kernel_grad_two = back(*multiply_conj(back_real, back_imag, gated_real, gated_imag))
    grad_inner_gate = grad_gated * first_conv
    grad_first = grad_gated * gate_inner
    skip_first = jnp.sum(grad_first * value_part, axis=1)
    early_real, early_imag = forth(grad_first)
    grad_value = grad_first * local_skip[0] + back(
        *multiply_conj(early_real, early_imag, kernel_real[0], kernel_imag[0])
    )
    kernel_grad_one = back(*multiply_conj(early_real, early_imag, value_real, value_imag))
    grad_mixed = jnp.concatenate([grad_outer, grad_inner_gate, grad_value], axis=0)
    id_sums = against_rows(shifted, grad_mixed, highest).reshape(3, vocab, 3, local_width)
    local_sums = jnp.sum(id_sums * local_taps[:, None], axis=0)
    local_taps_grad = jnp.sum(id_sums * local_table[None], axis=1)
    local_short_bias = jnp.sum(id_sums[2], axis=0, keepdims=True)
    local_small = jnp.concatenate(
        [
            local_sums,
            local_taps_grad,
            local_short_bias,
            jnp.pad(jnp.stack([skip_first, skip_second])[:, None], ((0, 0), (0, 2), (0, 0))),
        ],
        axis=0,
    )
    wide_small = lax.dynamic_update_slice_in_dim(
        jnp.zeros((local_small.shape[0], 3, model_width), jnp.float32), local_small, low_rows, 2
    )

    raw_grads = (jnp.stack([kernel_grad_one, kernel_grad_two]) * decay).reshape(
        2 * local_width, length
    )
    grad_local_filter = against_rows(raw_grads, second_act, highest).reshape(2, local_width, -1)
    grad_second_act = rows_inner(local_filter, raw_grads, highest)
    grad_second_pre = grad_second_act * jnp.cos(second_pre)
    grad_inner_weight = against_rows(first_act, grad_second_pre, highest)
    grad_inner_bias = jnp.sum(grad_second_pre, axis=1)
    grad_first_pre = exact_dot(inner_weight, grad_second_pre) * jnp.cos(first_pre)
    grad_freq_weight = against_rows(features, grad_first_pre, highest)
    grad_freq_bias = jnp.sum(grad_first_pre, axis=1)
    sum_filter = lax.psum_scatter(grad_local_filter, "dp", scatter_dimension=0, tiled=False)

    devices = lax.axis_size("dp") * seq_parts
    up_rows = model_width // devices
    pieces = jnp.concatenate(
        [
            grad_up.reshape(devices, -1, model_width),
            grad_down.reshape(devices, -1, model_width),
            grad_out.reshape(devices, -1, model_width),
        ],
        axis=1,
    )
    summed = lax.psum_scatter(pieces, ("dp", "seq"), scatter_dimension=0, tiled=False)
    up_size = up_rows * up_weight.shape[1] // model_width
    sum_up = summed[:up_size].reshape(up_weight.shape)
    sum_down = summed[up_size : up_size + down_weight.shape[0]]
    sum_out = summed[up_size + down_weight.shape[0] :]

    (
        wide_small,
        embed_sum,
        sum_freq_weight,
        sum_freq_bias,
        sum_inner_weight,
        sum_inner_bias,
        sum_out_bias,
        sum_gain_two,
        sum_bias_two,
        sum_up_bias,
        sum_down_bias,
    ) = lax.psum(
        (
            wide_small,
            embed_sum,
            grad_freq_weight,
            grad_freq_bias,
            grad_inner_weight,
            grad_inner_bias,
            grad_out_bias,
            grad_gain_two,
            grad_bias_two,
            grad_up_bias,
            grad_down_bias,
        ),
        ("dp", "seq"),
    )
    total_ids = wide_small[:vocab].reshape(vocab, 3 * model_width)
    sum_taps = wide_small[vocab : vocab + 3].reshape(3, 3 * model_width)
    sum_short_bias = wide_small[vocab + 3].reshape(3 * model_width)
    sum_skip = wide_small[vocab + 4 :, 0]
    sum_in_bias = jnp.sum(total_ids, axis=0)
    own_row = (dp_index * seq_parts + seq_index) * up_rows
    own_normed = lax.dynamic_slice_in_dim(normed, own_row, up_rows, 1).astype(jnp.float32)
    sum_in = rows_inner(own_normed, total_ids, highest)
    grad_normed = against_rows(total_ids, in_full.astype(jnp.float32), highest)
    sum_gain_one = jnp.sum(grad_normed * unit_one, axis=0)
    sum_bias_one = jnp.sum(grad_normed, axis=0)
    sum_embed = embed_sum + norm_back(grad_normed * gain_one, unit_one, inverse_one)
    return (
        block_out[None],
        sum_embed,
        sum_gain_one,
        sum_bias_one,
        sum_in,
        sum_in_bias,
        sum_taps,
        sum_short_bias,
        sum_freq_weight,
        sum_freq_bias,
        sum_inner_weight,
        sum_inner_bias,
        sum_filter,
        sum_skip,
        sum_out,
        sum_out_bias,
        sum_gain_two,
        sum_bias_two,
        sum_up,
        sum_up_bias,
        sum_down,
        sum_down_bias,
    )


F32, BF16 = jnp.float32, jnp.bfloat16
ROWS, PARTS, LOCAL, WIDTH, HIDDEN, SPLIT, IDS = 128, 16, 48, 768, 3072, 768, 16
GROUPS, LANE_CH = 3, 16
BINS = PARTS + 1
SPEC = BINS * LANE_CH
LENGTH = ROWS * PARTS


def tables_of(feature_count):
    b = np.arange(ROWS)
    grid = 2 * np.pi * ((b[:, None] * b[None, :]) % ROWS) / ROWS
    cos, sin = np.cos(grid), np.sin(grid)
    forth = np.block([[cos, -sin], [sin, cos]])
    high = forth.astype(ml_dtypes.bfloat16)
    low = (forth - high.astype(np.float64)).astype(ml_dtypes.bfloat16)
    mats = np.stack([high, low, high.T, low.T])
    k = np.arange(BINS)
    turn = 2 * np.pi * k[:, None] * b[None, :] / (2 * LENGTH)
    scale = np.where((k == 0) | (k == PARTS), 1.0, 2.0)[:, None] / (2 * LENGTH)
    twist = np.zeros((72, ROWS))
    twist[0:17], twist[17:34] = np.cos(turn), np.sin(turn)
    twist[34:51], twist[51:68] = np.cos(turn) * scale, np.sin(turn) * scale
    count = (feature_count - 1) // 2
    phase = np.arange(LENGTH, dtype=np.float32) / np.float32(LENGTH)
    levels = np.float32(0.0001) + np.arange(count, dtype=np.float32) * np.float32(
        (count - 1 - 0.0001) / (count - 1)
    )
    angle = np.float32(2.0 * math.pi) * phase[None, :] * levels[:, None]
    feats = np.zeros((40, LENGTH), np.float32)
    feats[0] = phase
    feats[1 : 1 + count] = np.cos(angle.astype(np.float64))
    feats[1 + count : 1 + 2 * count] = -np.sin(angle.astype(np.float64))
    feats[1 + 2 * count] = 1.0
    return mats, twist.astype(np.float32), feats


def times_turn(value, quarter_count, k, m):
    re, im = value
    c, s = math.cos(math.pi * k / m), math.sin(math.pi * k / m)
    if im is None:
        return (re * c, re * (-s))
    return (re * c + im * s, im * c - re * s)


def real_spectrum(xs):
    m = len(xs)
    if m == 1:
        return [(xs[0], None), (xs[0], None)]
    even, odd = real_spectrum(xs[0::2]), real_spectrum(xs[1::2])
    bins = [None] * (m + 1)
    bins[0] = (even[0][0] + odd[0][0], None)
    bins[m] = (even[0][0] - odd[0][0], None)
    half = m // 2
    bins[half] = (even[half][0], -odd[half][0])
    for k in range(1, half):
        er, ei = even[k]
        tr, ti = times_turn(odd[k], None, k, m)
        bins[k] = (er + tr, ei + ti)
        bins[m - k] = (er - tr, ti - ei)
    return bins


def real_signal(bins):
    m = len(bins) - 1
    if m == 1:
        return [bins[0][0] + bins[1][0]]
    half = m // 2
    even, odd = [None] * (half + 1), [None] * (half + 1)
    even[0] = (bins[0][0] + bins[m][0], None)
    odd[0] = (bins[0][0] - bins[m][0], None)
    even[half] = (bins[half][0], None)
    odd[half] = (-bins[half][1], None)
    for k in range(1, half):
        (ar, ai), (br, bi) = bins[k], bins[m - k]
        even[k] = (ar + br, ai - bi)
        dr, di = ar - br, ai + bi
        c, s = math.cos(math.pi * k / m), math.sin(math.pi * k / m)
        odd[k] = (dr * c - di * s, di * c + dr * s)
    first, second = real_signal(even), real_signal(odd)
    out = [None] * m
    out[0::2], out[1::2] = first, second
    return out


def sin_cos(x):
    n = jnp.floor(x * (1.0 / math.pi) + 0.5)
    r = x - n * 3.140625
    r = r - n * 9.67025756835937500000e-4
    r = r - n * 6.2771141529083251953e-7
    r = r - n * 1.2154201256553420762e-10
    flip = 1.0 - 2.0 * (n - 2.0 * jnp.floor(n * 0.5))
    q = r * r
    s = -2.50507477628578072866e-8
    s = s * q + 2.75573136213857245213e-6
    s = s * q - 1.98412698295895385996e-4
    s = s * q + 8.33333333332211858878e-3
    s = s * q - 1.66666666666666307295e-1
    s = (s * q) * r + r
    c = 2.08757008419747316778e-9
    c = c * q - 2.75573141792967388112e-7
    c = c * q + 2.48015872888517045348e-5
    c = c * q - 1.38888888888730564116e-3
    c = c * q + 4.16666666666665929218e-2
    c = c * q - 0.5
    c = c * q + 1.0
    return s * flip, c * flip


def dot32(a, b, ca, cb, precision=lax.Precision.HIGH):
    return lax.dot_general(
        a, b, (((ca,), (cb,)), ((), ())), precision=precision, preferred_element_type=F32
    )


def dot16(a, b, ca, cb):
    return lax.dot_general(a, b, (((ca,), (cb,)), ((), ())), preferred_element_type=F32)


def start_push(src, dst, send, recv, dp, seq):
    pltpu.make_async_remote_copy(
        src_ref=src,
        dst_ref=dst,
        send_sem=send,
        recv_sem=recv,
        device_id=(dp, seq),
        device_id_type=pl.DeviceIdType.MESH,
    ).start()


def wait_for(ref, sem):
    pltpu.make_async_copy(ref, ref, sem).wait()


def step_kernel(*refs):
    it = iter(refs)

    def take(count):
        return [next(it) for _ in range(count)]

    sources = take(len(INPUTS))
    sinks = take(len(OUTPUTS))
    v = SimpleNamespace(**dict(zip(SCRATCH, take(len(SCRATCH)))))
    sem_s, sem_r, sem_l, sem_o = take(4)
    src = SimpleNamespace(**dict(zip(INPUTS, sources)))
    out = SimpleNamespace(**dict(zip(OUTPUTS, sinks)))
    tok_v, emb_v, par_v, inw_v, mlp_v, filt_v = v.tok, v.emb, v.par, v.inw, v.mlp, v.filt
    outw_v, upw_v, downw_v, mats_v, twist_v, feats_v = v.outw, v.upw, v.downw, v.mats, v.twist, v.feats
    dp, seq = lax.axis_index("dp"), lax.axis_index("seq")
    me = dp * PARTS + seq
    z, yc = lax.div(seq, 4), lax.rem(seq, 4)
    y, core = lax.div(yc, 2), lax.rem(yc, 2)
    chip = dp * 2 + y
    twin = seq + 1 - 2 * core
    other_core = 1 - core
    other_dp = 1 - dp

    def tile(index, size):
        return pl.ds(pl.multiple_of(index * size, size), size)

    def everyone(k):
        d = lax.rem(me + k, 2 * PARTS)
        return d, lax.div(d, PARTS), lax.rem(d, PARTS)

    def of_seq(k):
        return lax.rem(seq + k, PARTS)

    def of_plane(k):
        xx, yy = lax.rem(dp + lax.div(k, 2), 2), lax.rem(y + lax.rem(k, 2), 2)
        return xx * 2 + yy, xx, z * 4 + yy * 2 + core

    def of_line(k):
        zz = lax.rem(z + k, 4)
        return zz, zz * 4 + yc

    def of_eight(k):
        j = lax.rem(dp * 4 + yc + k, 8)
        return j, lax.div(j, 4), z * 4 + lax.rem(j, 4)

    def loop(low, high, body):
        def step(k, carry):
            body(k)
            return carry

        lax.fori_loop(low, high, step, 0)

    firsts = np.cumsum([0] + list(FAMILIES.values())).tolist()
    fam = SimpleNamespace(**dict(zip(FAMILIES, firsts)))

    def s_of(first, index):
        return sem_s.at[first + index]

    def r_of(first, index):
        return sem_r.at[first + index]

    barrier = pltpu.get_barrier_semaphore()

    def greet(k):
        _, d, s = everyone(k)
        pl.semaphore_signal(barrier, inc=1, device_id=(d, s), device_id_type=pl.DeviceIdType.MESH)

    loop(1, 2 * PARTS, greet)
    loads = []

    def load(source, target):
        copy = pltpu.make_async_copy(source, target, sem_l.at[len(loads)])
        copy.start()
        loads.append(copy)

    def wait_load(*which):
        for i in which:
            loads[i].wait()

    load(src.embed_table, emb_v)
    load(src.gain_one, par_v.at[0])
    load(src.bias_one, par_v.at[1])
    load(src.in_weight, inw_v)
    load(src.token_ids, tok_v)
    load(src.filter_weight, filt_v)
    LOAD_WEIGHTS = len(loads)
    load(src.up_weight, upw_v)
    load(src.out_weight, outw_v)
    load(src.cotangent, v.seed_all.at[chip])
    LOAD_NET = len(loads)
    load(src.freq_weight, mlp_v.at[0:33, :])
    load(src.freq_bias, mlp_v.at[33])
    load(src.inner_weight, mlp_v.at[40:104, :])
    load(src.inner_bias, mlp_v.at[104])
    load(src.feats, feats_v)
    LOAD_TAIL = len(loads)
    load(src.mats, mats_v)
    load(src.twist, twist_v)
    for p in range(3):
        at = pl.ds(p * WIDTH, WIDTH)
        load(src.in_bias.at[at], par_v.at[2 + p])
        load(src.short_bias.at[at], par_v.at[14 + p])
        for t in range(3):
            load(src.short_taps.at[t : t + 1, at], par_v.at[5 + 3 * t + p : 6 + 3 * t + p, :])
    load(src.skip_scale, par_v.at[17:19, :])
    load(src.out_bias, par_v.at[19])
    load(src.gain_two, par_v.at[20])
    load(src.bias_two, par_v.at[21])
    load(src.down_bias, par_v.at[22])
    for r in range(4):
        load(src.up_bias.at[pl.ds(r * WIDTH, WIDTH)], par_v.at[23 + r])
    load(src.down_weight, downw_v)
    LOAD_END = len(loads)

    wait_load(*range(LOAD_WEIGHTS))
    lanes16 = lax.broadcasted_iota(jnp.int32, (IDS, WIDTH), 0)
    embed = jnp.concatenate([emb_v[...], jnp.zeros((4, WIDTH), F32)], axis=0)
    center = embed - jnp.mean(embed, axis=-1, keepdims=True)
    inverse_one = lax.rsqrt(jnp.mean(center * center, axis=-1, keepdims=True) + epsilon)
    unit_one = center * inverse_one
    normed = (unit_one * par_v[0:1, :] + par_v[1:2, :]).astype(BF16).astype(F32)
    normed = jnp.where(lanes16 < 12, normed, 0.0)
    normed_t = v.normed_t
    normed_t[...] = normed.T
    in_low = inw_v[...].astype(BF16).astype(F32)
    partial = dot32(normed_t[tile(me, 24), :], in_low, 0, 0, None)
    p_send, p_recv = v.p_send, v.p_recv
    for i in range(PARTS):
        block = [partial[:, p * WIDTH + i * LOCAL : p * WIDTH + (i + 1) * LOCAL] for p in range(3)]
        p_send[i] = jnp.concatenate(block, axis=1).astype(BF16)
    filt_all, tok_all = v.filt_all, v.tok_all
    filt_all[dp] = filt_v[...].astype(BF16)
    tok_all[seq] = tok_v[...]
    p_recv[seq] = p_send[seq]
    mlp_v[34:40, :] = jnp.zeros((6, 64), F32)
    mlp_v[105:112, :] = jnp.zeros((7, 64), F32)

    pl.semaphore_wait(barrier, 2 * PARTS - 1)

    def push_p(k):
        s = of_seq(k)
        start_push(p_send.at[s], p_recv.at[seq], s_of(fam.p, k), r_of(fam.p, seq), dp, s)
        start_push(tok_v, tok_all.at[seq], s_of(fam.tok, k), r_of(fam.tok, seq), dp, s)

    loop(1, PARTS, push_p)
    start_push(filt_all.at[dp], filt_all.at[dp], s_of(fam.filt, 0), r_of(fam.filt, 0), other_dp, seq)

    wait_load(*range(LOAD_WEIGHTS, LOAD_NET))
    up_send, up_all, out_all, seed_all = v.up_send, v.up_all, v.out_all, v.seed_all
    out_all[core, chip, z] = outw_v[...].astype(BF16)

    def push_out(k):
        zz, s = of_line(k)
        mine = out_all.at[core, chip, z]
        start_push(mine, mine, s_of(fam.outz, k), r_of(fam.outz, z), dp, s)

    loop(1, 4, push_out)

    def shard_of(q, c, zz):
        return (q // 2) * PARTS + zz * 4 + (q % 2) * 2 + c

    for q in range(4):
        cut = [
            upw_v[:, 96 * shard_of(q, c, zz) : 96 * (shard_of(q, c, zz) + 1)]
            for c in range(2)
            for zz in range(4)
        ]
        up_send[q] = jnp.concatenate(cut, axis=1).astype(BF16)
    up_all[core, z, chip] = up_send[chip]

    def push_up(k):
        q, d, s = of_plane(k)
        start_push(
            up_send.at[q], up_all.at[core, z, chip], s_of(fam.up, k), r_of(fam.up, chip), d, s
        )

    loop(1, 4, push_up)

    def push_seed(k):
        q, d, s = of_plane(k)
        mine = seed_all.at[chip]
        start_push(mine, mine, s_of(fam.seed, k), r_of(fam.seed, chip), d, s)

    loop(1, 4, push_seed)

    act1, cos1, act2, cos2 = v.act1, v.cos1, v.act2, v.cos2
    wait_load(*range(LOAD_NET, LOAD_TAIL))
    mlp = mlp_v[...]
    freq_t = mlp[0:40].T
    inner_bias = mlp[104:112].T[:, 0:1]
    inner = mlp[40:104]

    def network(i):
        at = tile(i, 256)
        s1, c1 = sin_cos(dot32(freq_t, feats_v[:, at], 1, 0, lax.Precision.HIGHEST))
        act1[0:64, at] = s1
        cos1[:, at] = c1
        act1[64:72, at] = jnp.where(
            lax.broadcasted_iota(jnp.int32, (8, 256), 0) == 0, 1.0, 0.0
        ).astype(F32)
        s2, c2 = sin_cos(dot32(inner, s1, 0, 0, lax.Precision.HIGHEST) + inner_bias)
        act2[:, at] = s2
        cos2[:, at] = c2

    loop(0, LENGTH // 256, network)
    def wait_up(k):
        q, _, _ = of_plane(k)
        wait_for(up_all.at[0, 0, 0], r_of(fam.up, q))

    loop(1, 4, wait_up)

    def push_up_line(k):
        zz, s = of_line(k)
        mine = up_all.at[core, z]
        start_push(mine, mine, s_of(fam.upz, k), r_of(fam.upz, z), dp, s)

    loop(1, 4, push_up_line)

    def twin_push(name, index, ref, target=None):
        start_push(ref, ref if target is None else target, s_of(name, index), r_of(name, index), dp, twin)

    twin_push(fam.upt, z, up_all.at[core, z])

    def wait_line(k):
        zz, _ = of_line(k)
        wait_for(out_all.at[0, 0, 0], r_of(fam.outz, zz))

    loop(1, 4, wait_line)

    def push_out_plane(k):
        q, d, s = of_plane(k)
        mine = out_all.at[core, chip]
        start_push(mine, mine, s_of(fam.outp, k), r_of(fam.outp, chip), d, s)

    loop(1, 4, push_out_plane)
    twin_push(fam.outt, chip, out_all.at[core, chip])

    wait_load(*range(LOAD_TAIL, LOAD_END))
    par_t = v.par_t
    for i in range(WIDTH // 128):
        par_t[128 * i : 128 * (i + 1), :] = par_v[:, 128 * i : 128 * (i + 1)].T
    own_par = par_t[tile(seq, LOCAL), :]

    def wait_p(k):
        s = of_seq(k)
        wait_for(p_recv.at[s], r_of(fam.p, s))

    loop(1, PARTS, wait_p)
    table = p_recv[0].astype(F32)
    for s in range(1, PARTS):
        table = table + p_recv[s].astype(F32)
    px_send, px_recv = v.px_send, v.px_recv
    px_send[...] = jnp.concatenate([table, jnp.zeros((IDS, 256 - 3 * LOCAL), F32)], axis=1)
    start_push(px_send, px_recv, s_of(fam.px, 0), r_of(fam.px, 0), other_dp, seq)

    kern, hi_ref, lo_ref = v.kern, v.hi, v.lo
    spec_k1, spec_k2, spec_v, spec_g = v.spec_k1, v.spec_k2, v.spec_v, v.spec_g
    wait_for(filt_all.at[0], r_of(fam.filt, 0))
    filt = jnp.concatenate([filt_all[0], filt_all[1]], axis=0).astype(F32)
    for i in range(LENGTH // 256):
        both = dot32(filt, act2[:, 256 * i : 256 * (i + 1)], 1, 0)
        for h in range(2):
            for f in range(2):
                kern[f, 2 * i + h] = both[f * LOCAL : (f + 1) * LOCAL, 128 * h : 128 * (h + 1)]
    lane = lax.broadcasted_iota(jnp.int32, (LANE_CH, ROWS), 1).astype(F32)

    def decay_of(g):
        row = lax.broadcasted_iota(jnp.int32, (LANE_CH, ROWS), 0) + (seq * LOCAL + g * LANE_CH)
        rate = slow_rate + (fast_rate - slow_rate) * (row.astype(F32) * (1.0 / (WIDTH - 1)))
        return lambda a: jnp.exp((lane + float(a * ROWS)) * (rate * (-1.0 / LENGTH))) + decay_shift

    def put(row0, k, re, im):
        rows = pl.ds(row0 + k * LANE_CH, LANE_CH)
        for part, value in ((0, re), (1, im)):
            at = pl.ds(part * ROWS, ROWS)
            high = value.astype(BF16)
            hi_ref[rows, at] = high
            lo_ref[rows, at] = (value - high.astype(F32)).astype(BF16)

    def forth(row0, values):
        for k, (re, im) in enumerate(real_spectrum(values)):
            c, s = twist_v[k : k + 1, :], twist_v[17 + k : 18 + k, :]
            if im is None:
                put(row0, k, re * c, re * (-s))
            else:
                put(row0, k, re * c + im * s, im * c - re * s)

    def dft(rows, which):
        high, low = hi_ref[0:rows, :], lo_ref[0:rows, :]
        m_high, m_low = mats_v[which], mats_v[which + 1]
        return dot16(high, m_high, 1, 0) + dot16(low, m_high, 1, 0) + dot16(high, m_low, 1, 0)

    def put_product(row0, spec, other, conj):
        a_re, a_im = spec[:, 0:ROWS], spec[:, ROWS:]
        b_re, b_im = other[:, 0:ROWS], other[:, ROWS:]
        if conj:
            re, im = a_re * b_re + a_im * b_im, a_im * b_re - a_re * b_im
        else:
            re, im = a_re * b_re - a_im * b_im, a_re * b_im + a_im * b_re
        rows = pl.ds(row0, SPEC)
        for part, value in ((0, re), (1, im)):
            at = pl.ds(part * ROWS, ROWS)
            high = value.astype(BF16)
            hi_ref[rows, at] = high
            lo_ref[rows, at] = (value - high.astype(F32)).astype(BF16)

    def back(turned, row0):
        bins = []
        for k in range(BINS):
            part = turned[row0 + k * LANE_CH : row0 + (k + 1) * LANE_CH]
            re, im = part[:, 0:ROWS], part[:, ROWS:]
            c, s = twist_v[34 + k : 35 + k, :], twist_v[51 + k : 52 + k, :]
            if k in (0, PARTS):
                bins.append((re * c - im * s, None))
            else:
                bins.append((re * c - im * s, im * c + re * s))
        return real_signal(bins)

    def kernel_spectra(g):
        at = tile(g, LANE_CH)
        decay = decay_of(g)
        damp = [decay(a) for a in range(PARTS)]
        forth(0, [kern[0, a, at, :] * damp[a] for a in range(PARTS)])
        forth(SPEC, [kern[1, a, at, :] * damp[a] for a in range(PARTS)])
        spec = dft(2 * SPEC, 0)
        spec_k1[g] = spec[0:SPEC]
        spec_k2[g] = spec[SPEC:]

    loop(0, GROUPS, kernel_spectra)

    table_t, onehot, mix = v.table_t, v.onehot, v.mix
    wait_for(px_recv, r_of(fam.px, 0))
    wide_t = (px_send[...] + px_recv[...]).T
    table_t[...] = jnp.concatenate(
        [wide_t[p * LOCAL : (p + 1) * LOCAL] + own_par[:, 2 + p : 3 + p] for p in range(3)], axis=0
    )

    def wait_tok(k):
        s = of_seq(k)
        wait_for(tok_v, r_of(fam.tok, s))

    loop(1, PARTS, wait_tok)
    id_rows = lax.broadcasted_iota(jnp.int32, (IDS, ROWS), 0)
    for a in range(PARTS):
        now = tok_all[a]
        if a == 0:
            long = jnp.concatenate([jnp.full((1, ROWS), -1, jnp.int32), now], axis=1)
        else:
            long = jnp.concatenate([tok_all[a - 1], now], axis=1)
        for t in range(3):
            moved = long[:, ROWS - 2 + t : 2 * ROWS - 2 + t]
            onehot[t * IDS : (t + 1) * IDS, a * ROWS : (a + 1) * ROWS] = (
                id_rows == moved
            ).astype(F32)

    def taps_of(t):
        return jnp.concatenate(
            [own_par[:, 5 + 3 * t + p : 6 + 3 * t + p] for p in range(3)], axis=0
        )

    short = jnp.concatenate([taps_of(t) * table_t[...] for t in range(3)], axis=1)
    short_bias = jnp.concatenate([own_par[:, 14 + p : 15 + p] for p in range(3)], axis=0)
    for i in range(LENGTH // 256):
        both = dot32(short, onehot[:, 256 * i : 256 * (i + 1)], 1, 0) + short_bias
        for h in range(2):
            for p in range(3):
                mix[p, 2 * i + h] = both[p * LOCAL : (p + 1) * LOCAL, 128 * h : 128 * (h + 1)]

    first_s, gated_s, second_s = v.first, v.gated, v.second
    mix_send, mix_recv = v.mix_send, v.mix_recv
    gm_send, gm_recv = v.gm_send, v.gm_recv

    def exchange(name, send, recv, g):
        at = tile(g, LANE_CH)

        def push(k):
            s = of_seq(k)
            start_push(
                send.at[s, at, :],
                recv.at[seq, at, :],
                s_of(name, g * PARTS + k),
                r_of(name, g * PARTS + seq),
                dp,
                s,
            )

        loop(1, PARTS, push)

    def exchanged(name, recv, g):
        def wait(k):
            s = of_seq(k)
            wait_for(recv.at[0, 0:LANE_CH, :], r_of(name, g * PARTS + s))

        loop(1, PARTS, wait)

    def operator(g):
        at = tile(g, LANE_CH)
        skips = par_t[pl.ds(pl.multiple_of(seq * LOCAL + g * LANE_CH, LANE_CH), LANE_CH), :]
        skip0, skip1 = skips[:, 17:18], skips[:, 18:19]
        forth(0, [mix[2, a, at, :] for a in range(PARTS)])
        spec = dft(SPEC, 0)
        spec_v[g] = spec
        put_product(0, spec, spec_k1[g], False)
        signal = back(dft(SPEC, 2), 0)
        gated = []
        for a in range(PARTS):
            conv = signal[a] + skip0 * mix[2, a, at, :]
            first_s[a, at, :] = conv
            gate = mix[1, a, at, :] * conv
            gated_s[a, at, :] = gate
            gated.append(gate)
        forth(0, gated)
        spec = dft(SPEC, 0)
        spec_g[g] = spec
        put_product(0, spec, spec_k2[g], False)
        signal = back(dft(SPEC, 2), 0)
        for a in range(PARTS):
            conv = signal[a] + skip1 * gated_s[a, at, :]
            second_s[a, at, :] = conv
            mix_send[a, at, :] = (mix[0, a, at, :] * conv).astype(BF16)

        exchange(fam.mix, mix_send, mix_recv, g)

    loop(0, GROUPS, operator)
    mix_recv[seq] = mix_send[seq]

    down_all = v.down_all
    down_all[core, z] = downw_v[...].astype(BF16)

    def forward_up(k):
        zz, _ = of_line(k)
        wait_for(up_all.at[0, 0], r_of(fam.upz, zz))
        twin_push(fam.upt, zz, up_all.at[core, zz])

    loop(1, 4, forward_up)

    def forward_out(k):
        q, _, _ = of_plane(k)
        wait_for(out_all.at[0, 0], r_of(fam.outp, q))
        twin_push(fam.outt, q, out_all.at[core, q])

    loop(1, 4, forward_out)
    w_up, w_out = v.w_up, v.w_out
    loop(0, 4, lambda k: wait_for(out_all.at[0, 0], r_of(fam.outt, k)))

    def place_out(i):
        q, zz = lax.div(i, 8) * 2 + lax.rem(i, 2), lax.rem(lax.div(i, 2), 4)
        both = jnp.concatenate(
            [out_all[0, q, zz].astype(F32), out_all[1, q, zz].astype(F32)], axis=0
        )
        w_out[tile(i, 48), :] = both.astype(BF16)

    loop(0, 16, place_out)
    for g in range(GROUPS):
        exchanged(fam.mix, mix_recv, g)

    def push_down(k):
        zz, s = of_line(k)
        mine = down_all.at[core, z]
        start_push(mine, mine, s_of(fam.down, k), r_of(fam.down, z), dp, s)

    loop(1, 4, push_down)
    twin_push(fam.downt, z, down_all.at[core, z])

    own_onehot = (id_rows == tok_v[...]).astype(F32)
    resid, unit2, inv2, n2_all = v.resid, v.unit2, v.inv2, v.n2_all
    mixer_t = mix_recv[...].reshape(WIDTH, ROWS)
    residual = dot32(own_onehot, embed, 0, 0) + dot16(mixer_t, w_out[...], 0, 0) + par_v[19:20, :]
    resid[...] = residual
    center = residual - jnp.mean(residual, axis=-1, keepdims=True)
    inv = lax.rsqrt(jnp.mean(center * center, axis=-1, keepdims=True) + epsilon)
    inv2[...] = inv
    unit = center * inv
    unit2[...] = unit
    n2_all[chip] = (unit * par_v[20:21, :] + par_v[21:22, :]).astype(BF16)

    def push_n2(k):
        q, d, s = of_plane(k)
        mine = n2_all.at[chip]
        start_push(mine, mine, s_of(fam.n2, k), r_of(fam.n2, chip), d, s)

    loop(1, 4, push_n2)

    loop(0, 4, lambda k: wait_for(up_all.at[0, 0], r_of(fam.upt, k)))

    def place_up(i):
        q, zz = lax.div(i, 8) * 2 + lax.rem(i, 2), lax.rem(lax.div(i, 2), 4)
        both = jnp.concatenate(
            [up_all[0, zz, q].astype(F32), up_all[1, zz, q].astype(F32)], axis=0
        )
        w_up[tile(i, 48), :] = both.astype(BF16)

    loop(0, 16, place_up)

    def wait_seed(k):
        q, _, _ = of_plane(k)
        wait_for(seed_all.at[0], r_of(fam.seed, q))

    loop(1, 4, wait_seed)

    def forward_down(k):
        zz, _ = of_line(k)
        wait_for(down_all.at[0, 0], r_of(fam.down, zz))
        twin_push(fam.downt, zz, down_all.at[core, zz])

    loop(1, 4, forward_down)
    loop(0, 4, lambda k: wait_for(down_all.at[0, 0], r_of(fam.downt, k)))

    up_bias = jnp.zeros((1, SPLIT), F32)
    for q in range(4):
        cut = []
        for c in range(2):
            for zz in range(4):
                first = 96 * shard_of(q, c, zz)
                row, lane0 = first // WIDTH, first % WIDTH
                cut.append(par_v[23 + row : 24 + row, lane0 : lane0 + 96])
        up_bias = jnp.where(chip == q, jnp.concatenate(cut, axis=1), up_bias)
    act_all, gl_all, po_all, gn_all = v.act_all, v.gl_all, v.po_all, v.gn_all
    gn_recv, po_recv = v.gn_recv, v.po_recv

    def feed(k, bias_sum):
        q, d, s = of_plane(k)

        @pl.when(k != 0)
        def _():
            wait_for(n2_all.at[0], r_of(fam.n2, q))

        down_w = down_all[...].reshape(SPLIT, WIDTH)
        lifted = dot16(n2_all[q], w_up[...], 1, 0) + up_bias
        cdf = 0.5 * (1.0 + lax.erf(lifted * (1.0 / math.sqrt(2.0))))
        pdf = jnp.exp(-0.5 * lifted * lifted) * (1.0 / math.sqrt(2.0 * math.pi))
        grad_act = dot16(seed_all[q], down_w, 1, 1)
        grad_lifted = grad_act * (cdf + lifted * pdf)
        act_all[q] = (lifted * cdf).astype(BF16)
        gl_all[q] = grad_lifted.astype(BF16)
        gn_all[q] = dot16(gl_all[q], w_up[...], 1, 1).astype(BF16)

        @pl.when(k != 0)
        def _():
            start_push(gn_all.at[q], gn_recv.at[chip], s_of(fam.gn, k), r_of(fam.gn, chip), d, s)

        po_all[q] = dot16(act_all[q], down_w, 1, 0).astype(BF16)
        return bias_sum + jnp.sum(grad_lifted, axis=0, keepdims=True)

    grad_up_bias = lax.fori_loop(0, 4, feed, jnp.zeros((1, SPLIT), F32))
    gn_recv[chip] = gn_all[chip]
    po_recv[chip] = po_all[chip]

    sd_x, sd_y, sd_t, sd_z = v.sd_x, v.sd_y, v.sd_t, v.sd_z
    su_x, su_y, su_t, su_z, su_p, su_r = (v.su_x, v.su_y, v.su_t, v.su_z, v.su_p, v.su_r)
    so_x, so_y, so_t, so_p, so_u, so_z = (v.so_x, v.so_y, v.so_t, v.so_p, v.so_u, v.so_z)
    acts = act_all[...].reshape(4 * ROWS, SPLIT)
    seeds = seed_all[...].reshape(4 * ROWS, WIDTH)
    for c in range(2):
        half = acts[:, c * 384 : (c + 1) * 384]
        sd_x[c] = dot16(half, seeds, 0, 0).astype(BF16).reshape(4, 96, WIDTH)
    twin_push(fam.sdt, 0, sd_x.at[other_core], sd_y)
    units = n2_all[...].reshape(4 * ROWS, WIDTH)
    lows = gl_all[...].reshape(4 * ROWS, SPLIT)
    for x in range(2):
        part = dot16(units[:, x * 384 : (x + 1) * 384], lows, 0, 0)
        for i in range(16):
            su_x[i % 2, i // 4, x * 2 + (i // 2) % 2] = part[24 * i : 24 * (i + 1)].astype(BF16)
    twin_push(fam.sut, 0, su_x.at[other_core], su_y)
    wait_for(sd_y, r_of(fam.sdt, 0))

    def add_sd(i):
        sd_t[i] = (sd_x[core, i].astype(F32) + sd_y[i].astype(F32)).astype(BF16)

    loop(0, 4, add_sd)
    sd_z[z] = sd_t[z]

    def push_sd(k):
        zz, s = of_line(k)
        start_push(sd_t.at[zz], sd_z.at[z], s_of(fam.sd, k), r_of(fam.sd, z), dp, s)

    loop(1, 4, push_sd)
    wait_for(su_y, r_of(fam.sut, 0))

    def add_su(i):
        for q in range(4):
            su_t[i, q] = (su_x[core, i, q].astype(F32) + su_y[i, q].astype(F32)).astype(BF16)

    loop(0, 4, add_su)
    su_z[z] = su_t[z]

    def wait_gn(k):
        q, _, _ = of_plane(k)
        wait_for(gn_recv.at[0], r_of(fam.gn, q))

    loop(1, 4, wait_gn)
    grad_n2 = gn_recv[0].astype(F32)
    for q in range(1, 4):
        grad_n2 = grad_n2 + gn_recv[q].astype(F32)
    unit, inv = unit2[...], inv2[...]
    seed = seed_all[chip].astype(F32)
    scaled = grad_n2 * par_v[20:21, :]
    grad_res = seed + inv * (
        scaled
        - jnp.mean(scaled, axis=-1, keepdims=True)
        - unit * jnp.mean(scaled * unit, axis=-1, keepdims=True)
    )
    gres = v.gres
    gres[...] = grad_res.astype(BF16)
    gm_send[...] = dot16(w_out[...], gres[...], 1, 1).astype(BF16).reshape(PARTS, LOCAL, ROWS)
    loop(0, GROUPS, lambda g: exchange(fam.gm, gm_send, gm_recv, g))
    gm_recv[seq] = gm_send[seq]

    b_x, b_y, b_p, b_t, b_z, b_f = (v.b_x, v.b_y, v.b_p, v.b_t, v.b_z, v.b_f)
    b_x[0:12, :] = dot32(own_onehot, grad_res, 1, 0)[0:12]
    b_x[12:13, :] = jnp.sum(grad_res, axis=0, keepdims=True)
    b_x[13:14, :] = jnp.sum(grad_n2 * unit, axis=0, keepdims=True)
    b_x[14:15, :] = jnp.sum(grad_n2, axis=0, keepdims=True)
    b_x[15:16, :] = jnp.sum(seed, axis=0, keepdims=True)
    for q in range(4):
        b_x[16 + q : 17 + q, :] = jnp.where(chip == q, grad_up_bias, 0.0)
    b_x[20:24, :] = jnp.zeros((4, WIDTH), F32)
    twin_push(fam.bt, 0, b_x, b_y)

    def push_po(k):
        q, d, s = of_plane(k)
        start_push(po_all.at[q], po_recv.at[chip], s_of(fam.po, k), r_of(fam.po, chip), d, s)

    loop(1, 4, push_po)
    for x in range(2):
        part = dot16(mixer_t[x * 384 : (x + 1) * 384], gres[...], 1, 0)
        for i in range(16):
            so_x[i % 2, x * 2 + (i // 2) % 2, i // 4] = part[24 * i : 24 * (i + 1)].astype(BF16)
    twin_push(fam.sot, 0, so_x.at[other_core], so_y)

    wait_for(b_y, r_of(fam.bt, 0))
    for c in range(2):

        @pl.when(core == c)
        def _():
            at = slice(c * 384, (c + 1) * 384)
            b_p[chip] = b_x[:, at] + b_y[:, at]

    def push_b(k):
        q, d, s = of_plane(k)
        mine = b_p.at[chip]
        start_push(mine, mine, s_of(fam.b, k), r_of(fam.b, chip), d, s)

    loop(1, 4, push_b)

    wait_for(so_y, r_of(fam.sot, 0))

    def add_so(i):
        for q in range(4):
            so_t[q, i] = (so_x[core, q, i].astype(F32) + so_y[q, i].astype(F32)).astype(BF16)

    loop(0, 4, add_so)
    so_p[chip] = so_t[chip]

    def push_so(k):
        q, d, s = of_plane(k)
        start_push(so_t.at[q], so_p.at[chip], s_of(fam.so, k), r_of(fam.so, chip), d, s)

    loop(1, 4, push_so)

    grad_mix, raw, q_s = v.grad_mix, v.raw, v.q_s

    def operator_back(g):
        at = tile(g, LANE_CH)
        skips = par_t[pl.ds(pl.multiple_of(seq * LOCAL + g * LANE_CH, LANE_CH), LANE_CH), :]
        skip0, skip1 = skips[:, 17:18], skips[:, 18:19]
        decay = decay_of(g)

        def rows_at(first, count=LANE_CH):
            return pl.ds(pl.multiple_of(first + g * LANE_CH, LANE_CH), count)

        seconds, total = [], jnp.zeros((LANE_CH, ROWS), F32)
        for a in range(PARTS):
            upstream = gm_recv[a, at, :].astype(F32)
            lanes = slice(a * ROWS, (a + 1) * ROWS)
            grad_mix[rows_at(0), lanes] = upstream * second_s[a, at, :]
            grad_second = upstream * mix[0, a, at, :]
            total = total + grad_second * gated_s[a, at, :]
            seconds.append(grad_second)
        q_s[rows_at(0), 49:50] = jnp.sum(total, axis=1, keepdims=True)
        forth(0, seconds)
        spec = dft(SPEC, 0)
        put_product(0, spec, spec_k2[g], True)
        put_product(SPEC, spec, spec_g[g], True)
        turned = dft(2 * SPEC, 2)
        signal = back(turned, 0)
        cross = back(turned, SPEC)
        firsts, total = [], jnp.zeros((LANE_CH, ROWS), F32)
        for a in range(PARTS):
            lanes = slice(a * ROWS, (a + 1) * ROWS)
            raw[rows_at(LOCAL), lanes] = cross[a] * decay(a)
            grad_second = gm_recv[a, at, :].astype(F32) * mix[0, a, at, :]
            grad_gated = skip1 * grad_second + signal[a]
            grad_mix[rows_at(LOCAL), lanes] = grad_gated * first_s[a, at, :]
            grad_first = grad_gated * mix[1, a, at, :]
            total = total + grad_first * mix[2, a, at, :]
            grad_mix[rows_at(2 * LOCAL), lanes] = skip0 * grad_first
            firsts.append(grad_first)
        q_s[rows_at(0), 48:49] = jnp.sum(total, axis=1, keepdims=True)
        forth(0, firsts)
        spec = dft(SPEC, 0)
        put_product(0, spec, spec_k1[g], True)
        put_product(SPEC, spec, spec_v[g], True)
        turned = dft(2 * SPEC, 2)
        signal = back(turned, 0)
        cross = back(turned, SPEC)
        for a in range(PARTS):
            lanes = slice(a * ROWS, (a + 1) * ROWS)
            raw[rows_at(0), lanes] = cross[a] * decay(a)
            grad_mix[rows_at(2 * LOCAL), lanes] = grad_mix[rows_at(2 * LOCAL), lanes] + signal[a]

    def push_su(k):
        zz, s = of_line(k)
        start_push(su_t.at[zz], su_z.at[z], s_of(fam.su, k), r_of(fam.su, z), dp, s)

    def group_back(g):
        exchanged(fam.gm, gm_recv, g)

        @pl.when(g == GROUPS - 1)
        def _():
            loop(1, 4, push_su)

        operator_back(g)

    loop(0, GROUPS, group_back)

    zx_send, zx_recv, z_send, z_recv = v.zx_send, v.zx_recv, v.z_send, v.z_recv
    by_id = dot32(grad_mix[...], onehot[...], 1, 1)
    sums = sum(taps_of(t) * by_id[:, t * IDS : (t + 1) * IDS] for t in range(3))
    taps_grad = [
        jnp.sum(table_t[...] * by_id[:, t * IDS : (t + 1) * IDS], axis=1, keepdims=True)
        for t in range(3)
    ]
    bias_grad = jnp.sum(by_id[:, 2 * IDS : 3 * IDS], axis=1, keepdims=True)
    columns = jnp.concatenate([sums[:, 0:12]] + taps_grad + [bias_grad], axis=1)
    skip_cols = jnp.concatenate(
        [q_s[:, 48:50], jnp.zeros((LOCAL, 14), F32)], axis=1
    )
    zx_send[...] = jnp.concatenate(
        [columns, skip_cols, jnp.zeros((64, IDS), F32)], axis=0
    ).T
    start_push(zx_send, zx_recv, s_of(fam.zx, 0), r_of(fam.zx, 0), other_dp, seq)

    f_send, f_recv, m_send, m_recv, m2_send, m2_recv = (v.f_send, v.f_recv, v.m_send, v.m_recv, v.m2_send, v.m2_recv)
    grad_filter = dot32(raw[...], act2[...], 1, 1)
    f_send[...] = grad_filter
    there = f_send.at[tile(other_dp, LOCAL), :]
    start_push(there, f_recv, s_of(fam.f, 0), r_of(fam.f, 0), other_dp, seq)
    grad_second_pre = dot32(filt, raw[...], 0, 0) * cos2[...]
    grad_inner = dot32(act1[...], grad_second_pre, 1, 1)
    grad_first_pre = dot32(inner, grad_second_pre, 1, 0) * cos1[...]
    grad_freq = dot32(feats_v[...], grad_first_pre, 1, 1)
    m_send[...] = jnp.concatenate(
        [
            jnp.concatenate([grad_freq, jnp.zeros((40, 64), F32)], axis=0),
            jnp.concatenate([grad_inner, jnp.zeros((8, 64), F32)], axis=0),
        ],
        axis=1,
    ).astype(BF16)
    j_me = dp * 4 + yc
    m_recv[j_me] = m_send[...]

    def push_m(k):
        j, d, s = of_eight(k)
        start_push(m_send, m_recv.at[j_me], s_of(fam.m, k), r_of(fam.m, j_me), d, s)

    loop(1, 8, push_m)

    wait_for(zx_recv, r_of(fam.zx, 0))
    z_send[...] = (zx_send[...] + zx_recv[...]).astype(BF16)
    z_recv[seq] = z_send[...]

    def push_z(k):
        s = of_seq(k)
        start_push(z_send, z_recv.at[seq], s_of(fam.z, k), r_of(fam.z, seq), dp, s)

    loop(1, PARTS, push_z)

    def wait_b(k):
        q, _, _ = of_plane(k)
        wait_for(b_p.at[0], r_of(fam.b, q))

    loop(1, 4, wait_b)
    b_t[...] = (b_p[0] + b_p[1]) + (b_p[2] + b_p[3])
    b_z[z] = b_t[...]

    def push_b2(k):
        zz, s = of_line(k)
        start_push(b_t, b_z.at[z], s_of(fam.b2, k), r_of(fam.b2, z), dp, s)

    loop(1, 4, push_b2)

    def wait_so(k):
        q, _, _ = of_plane(k)
        wait_for(so_p.at[0], r_of(fam.so, q))

    loop(1, 4, wait_so)
    for zz in range(4):
        part = so_p[0, zz].astype(F32)
        for q in range(1, 4):
            part = part + so_p[q, zz].astype(F32)
        so_u[zz] = part.astype(BF16)
    so_z[z] = so_u[z]

    def push_so2(k):
        zz, s = of_line(k)
        start_push(so_u.at[zz], so_z.at[z], s_of(fam.so2, k), r_of(fam.so2, z), dp, s)

    loop(1, 4, push_so2)

    def wait_m(k):
        j, _, _ = of_eight(k)
        wait_for(m_send, r_of(fam.m, j))

    loop(1, 8, wait_m)
    totals = m_recv[0].astype(F32)
    for j in range(1, 8):
        totals = totals + m_recv[j].astype(F32)
    m2_send[...] = totals.astype(BF16)
    m2_recv[z] = m2_send[...]

    def push_m2(k):
        zz, s = of_line(k)
        start_push(m2_send, m2_recv.at[z], s_of(fam.m2, k), r_of(fam.m2, z), dp, s)

    loop(1, 4, push_m2)

    def wait_su(k):
        zz, _ = of_line(k)
        wait_for(su_z.at[0], r_of(fam.su, zz))

    loop(1, 4, wait_su)
    for q in range(4):
        part = su_z[0, q].astype(F32)
        for zz in range(1, 4):
            part = part + su_z[zz, q].astype(F32)
        su_p[q] = part.astype(BF16)
    su_r[chip] = su_p[chip]

    def push_su2(k):
        q, d, s = of_plane(k)
        start_push(su_p.at[q], su_r.at[chip], s_of(fam.su2, k), r_of(fam.su2, chip), d, s)

    loop(1, 4, push_su2)

    wide, gt_all = v.wide, v.gt_all

    def wait_z(k):
        s = of_seq(k)
        wait_for(z_send, r_of(fam.z, s))

    loop(1, PARTS, wait_z)
    for p in range(4):
        for i in range(PARTS):
            wide[:, p * WIDTH + i * LOCAL : p * WIDTH + (i + 1) * LOCAL] = z_recv[i][
                :, p * LOCAL : (p + 1) * LOCAL
            ].astype(F32)
    by_ids = jnp.where(
        lax.broadcasted_iota(jnp.int32, (IDS, 3 * WIDTH), 0) < 12, wide[:, 0 : 3 * WIDTH], 0.0
    )
    gt_all[me] = dot32(in_low, by_ids, 1, 1)

    def push_gt(k):
        _, d, s = everyone(k)
        mine = gt_all.at[me]
        start_push(mine, mine, s_of(fam.gt, k), r_of(fam.gt, me), d, s)

    loop(1, 2 * PARTS, push_gt)

    stores = []

    def store(source, target):
        copy = pltpu.make_async_copy(source, target, sem_o.at[len(stores)])
        copy.start()
        stores.append(copy)

    o_in, o_wide, o_rows = v.o_in, v.o_wide, v.o_rows
    o_in[...] = dot32(normed_t[tile(me, 24), :], by_ids, 1, 0)
    o_wide[...] = jnp.sum(by_ids, axis=0, keepdims=True)
    o_rows[2:4, :] = wide[0:2, 3 * WIDTH :]
    store(o_in, out.in_weight)
    store(o_wide.at[0], out.in_bias)
    store(wide.at[12:15, 0 : 3 * WIDTH], out.short_taps)
    store(wide.at[15, pl.ds(0, 3 * WIDTH)], out.short_bias)
    store(o_rows.at[2:4, :], out.skip_scale)

    def wait_po(k):
        q, _, _ = of_plane(k)
        wait_for(po_recv.at[0], r_of(fam.po, q))

    loop(1, 4, wait_po)
    block = resid[...] + par_v[22:23, :]
    for q in range(4):
        block = block + po_recv[q].astype(F32)
    resid[...] = block
    store(resid, out.block)

    def wait_sd(k):
        zz, _ = of_line(k)
        wait_for(sd_z.at[0], r_of(fam.sd, zz))

    loop(1, 4, wait_sd)
    part = sd_z[0].astype(F32)
    for zz in range(1, 4):
        part = part + sd_z[zz].astype(F32)
    downw_v[...] = part
    store(downw_v, out.down_weight)
    wait_for(f_recv, r_of(fam.f, 0))
    f_recv[...] = f_send[tile(dp, LOCAL), :] + f_recv[...]
    store(f_recv, out.filter_weight)

    def wait_su2(k):
        q, _, _ = of_plane(k)
        wait_for(su_r.at[0], r_of(fam.su2, q))

    loop(1, 4, wait_su2)
    for q in range(4):
        part = su_r[q].astype(F32)
        for c in range(2):
            for zz in range(4):
                first, place = 96 * shard_of(q, c, zz), 384 * c + 96 * zz
                upw_v[:, first : first + 96] = part[:, place : place + 96]
    store(upw_v, out.up_weight)

    def wait_so2(k):
        zz, _ = of_line(k)
        wait_for(so_z.at[0], r_of(fam.so2, zz))
        wait_for(b_t, r_of(fam.b2, zz))
        wait_for(m2_send, r_of(fam.m2, zz))

    loop(1, 4, wait_so2)
    b_f[core] = (b_z[0] + b_z[1]) + (b_z[2] + b_z[3])
    mine = b_f.at[core]
    start_push(mine, mine, s_of(fam.bf, 0), r_of(fam.bf, 0), dp, twin)
    part = so_z[0].astype(F32)
    for zz in range(1, 4):
        part = part + so_z[zz].astype(F32)
    outw_v[...] = part
    store(outw_v, out.out_weight)
    totals = m2_recv[0].astype(F32)
    for zz in range(1, 4):
        totals = totals + m2_recv[zz].astype(F32)
    mlp_v[0:40, :] = totals[0:40, 0:64]
    mlp_v[40:112, :] = totals[0:72, 64:128]
    store(mlp_v.at[0:33, :], out.freq_weight)
    store(mlp_v.at[33], out.freq_bias)
    store(mlp_v.at[40:104, :], out.inner_weight)
    store(mlp_v.at[104], out.inner_bias)
    wait_for(b_f.at[0], r_of(fam.bf, 0))
    totals = jnp.concatenate([b_f[0], b_f[1]], axis=1)
    o_rows[4:8, :] = totals[12:16]
    o_up = v.o_up
    for q in range(4):
        for c in range(2):
            for zz in range(4):
                first, place = 96 * shard_of(q, c, zz), 384 * c + 96 * zz
                o_up[:, first : first + 96] = totals[16 + q : 17 + q, place : place + 96]
    store(o_rows.at[4], out.out_bias)
    store(o_rows.at[5], out.gain_two)
    store(o_rows.at[6], out.bias_two)
    store(o_rows.at[7], out.down_bias)
    store(o_up.at[0], out.up_bias)

    def wait_gt(k):
        d, _, _ = everyone(k)
        wait_for(gt_all.at[0], r_of(fam.gt, d))

    loop(1, 2 * PARTS, wait_gt)
    grad_normed = gt_all[...].reshape(WIDTH, IDS).T
    o_rows[0:1, :] = jnp.sum(grad_normed * unit_one, axis=0, keepdims=True)
    o_rows[1:2, :] = jnp.sum(grad_normed, axis=0, keepdims=True)
    scaled = grad_normed * par_v[0:1, :]
    grad_embed = inverse_one * (
        scaled
        - jnp.mean(scaled, axis=-1, keepdims=True)
        - unit_one * jnp.mean(scaled * unit_one, axis=-1, keepdims=True)
    )
    emb_v[...] = totals[0:12] + grad_embed[0:12]
    store(o_rows.at[0], out.gain_one)
    store(o_rows.at[1], out.bias_one)
    store(emb_v, out.embed_table)

    def sent(name, ref, low, high):
        loop(low, high, lambda k: wait_for(ref, s_of(name, k)))

    sent(fam.p, p_send.at[0], 1, PARTS)
    sent(fam.tok, tok_v, 1, PARTS)
    sent(fam.filt, filt_all.at[0], 0, 1)
    sent(fam.px, px_send, 0, 1)
    sent(fam.outz, out_all.at[0, 0, 0], 1, 4)
    sent(fam.outp, out_all.at[0, 0], 1, 4)
    sent(fam.outt, out_all.at[0, 0], 0, 4)
    sent(fam.up, up_send.at[0], 1, 4)
    sent(fam.upz, up_all.at[0, 0], 1, 4)
    sent(fam.upt, up_all.at[0, 0], 0, 4)
    sent(fam.seed, seed_all.at[0], 1, 4)
    sent(fam.down, down_all.at[0, 0], 1, 4)
    sent(fam.downt, down_all.at[0, 0], 0, 4)
    for g in range(GROUPS):
        sent(fam.mix, mix_send.at[0, 0:LANE_CH, :], g * PARTS + 1, (g + 1) * PARTS)
        sent(fam.gm, gm_send.at[0, 0:LANE_CH, :], g * PARTS + 1, (g + 1) * PARTS)
    sent(fam.n2, n2_all.at[0], 1, 4)
    sent(fam.gn, gn_all.at[0], 1, 4)
    sent(fam.po, po_all.at[0], 1, 4)
    sent(fam.sdt, sd_y, 0, 1)
    sent(fam.sut, su_y, 0, 1)
    sent(fam.sot, so_y, 0, 1)
    sent(fam.sd, sd_t.at[0], 1, 4)
    sent(fam.su, su_t.at[0], 1, 4)
    sent(fam.su2, su_p.at[0], 1, 4)
    sent(fam.so, so_t.at[0], 1, 4)
    sent(fam.so2, so_u.at[0], 1, 4)
    sent(fam.bt, b_x, 0, 1)
    sent(fam.b, b_p.at[0], 1, 4)
    sent(fam.b2, b_t, 1, 4)
    sent(fam.bf, b_f.at[0], 0, 1)
    sent(fam.m, m_send, 1, 8)
    sent(fam.m2, m2_send, 1, 4)
    sent(fam.z, z_send, 1, PARTS)
    sent(fam.zx, zx_send, 0, 1)
    sent(fam.f, f_recv, 0, 1)
    sent(fam.gt, gt_all.at[0], 1, 2 * PARTS)
    for copy in stores:
        copy.wait()


def copy_kernel(*refs):
    count = len(OUTPUTS)
    for source, target in zip(refs[:count], refs[count:]):
        target[...] = source[...]


FAMILIES = dict(
    p=16, tok=16, filt=1, px=1, outz=4, outp=4, outt=4, up=4,
    upz=4, upt=4, down=4, downt=4, seed=4, mix=48, gm=48, n2=4,
    gn=4, po=4, sdt=1, sd=4, sut=1, su=4, su2=4, sot=1, so=4,
    so2=4, bt=1, b=4, b2=4, bf=1, m=8, m2=4, z=16, zx=1,
    f=1, gt=32,
)
INPUTS = dict(
    token_ids=0, embed_table=0, gain_one=0, bias_one=0, in_weight=0, in_bias=0, short_taps=0, short_bias=0,
    freq_weight=0, freq_bias=0, inner_weight=0, inner_bias=0, filter_weight=0, skip_scale=0, out_weight=0,
    out_bias=0, gain_two=0, bias_two=0, up_weight=0, up_bias=0, down_weight=0, down_bias=0, cotangent=0,
    mats=0, twist=0, feats=0,
)
OUTPUTS = dict(
    block=(ROWS, WIDTH), embed_table=(12, WIDTH), gain_one=(WIDTH,),
    bias_one=(WIDTH,), in_weight=(24, 3 * WIDTH), in_bias=(3 * WIDTH,),
    short_taps=(3, 3 * WIDTH), short_bias=(3 * WIDTH,), freq_weight=(33, 64),
    freq_bias=(64,), inner_weight=(64, 64), inner_bias=(64,),
    filter_weight=(LOCAL, 64), skip_scale=(2, WIDTH), out_weight=(24, WIDTH),
    out_bias=(WIDTH,), gain_two=(WIDTH,), bias_two=(WIDTH,),
    up_weight=(24, HIDDEN), up_bias=(HIDDEN,), down_weight=(96, WIDTH),
    down_bias=(WIDTH,),
)
SPECTRUM = (GROUPS, SPEC, 2 * ROWS)
SCRATCH = dict(
    tok=((1, ROWS), jnp.int32), emb=((12, WIDTH), F32), par=((32, WIDTH), F32),
    inw=((24, 3 * WIDTH), F32), mlp=((112, 64), F32), filt=((LOCAL, 64), F32),
    outw=((24, WIDTH), F32), upw=((24, HIDDEN), F32), downw=((96, WIDTH), F32),
    mats=((4, 256, 256), BF16), twist=((72, ROWS), F32), feats=((40, LENGTH), F32),
    normed_t=((WIDTH, IDS), F32), p_send=((PARTS, IDS, 3 * LOCAL), BF16),
    p_recv=((PARTS, IDS, 3 * LOCAL), BF16), px_send=((IDS, 256), F32), px_recv=((IDS, 256), F32),
    filt_all=((2, LOCAL, 64), BF16), tok_all=((PARTS, 1, ROWS), jnp.int32),
    up_send=((4, 24, SPLIT), BF16), up_all=((2, 4, 4, 24, SPLIT), BF16),
    out_all=((2, 4, 4, 24, WIDTH), BF16), seed_all=((4, ROWS, WIDTH), BF16),
    down_all=((2, 4, 96, WIDTH), BF16), w_up=((WIDTH, SPLIT), BF16), w_out=((WIDTH, WIDTH), BF16),
    act1=((72, LENGTH), F32), cos1=((64, LENGTH), F32), act2=((64, LENGTH), F32),
    cos2=((64, LENGTH), F32), kern=((2, PARTS, LOCAL, ROWS), F32), par_t=((WIDTH, 32), F32),
    table_t=((3 * LOCAL, IDS), F32), onehot=((3 * IDS, LENGTH), F32),
    mix=((3, PARTS, LOCAL, ROWS), F32),
    hi=((2 * SPEC, 2 * ROWS), BF16), lo=((2 * SPEC, 2 * ROWS), BF16),
    spec_k1=(SPECTRUM, F32), spec_k2=(SPECTRUM, F32), spec_v=(SPECTRUM, F32),
    spec_g=(SPECTRUM, F32),
    first=((PARTS, LOCAL, ROWS), F32), gated=((PARTS, LOCAL, ROWS), F32),
    second=((PARTS, LOCAL, ROWS), F32),
    mix_send=((PARTS, LOCAL, ROWS), BF16), mix_recv=((PARTS, LOCAL, ROWS), BF16),
    gm_send=((PARTS, LOCAL, ROWS), BF16), gm_recv=((PARTS, LOCAL, ROWS), BF16),
    resid=((ROWS, WIDTH), F32), unit2=((ROWS, WIDTH), F32), inv2=((ROWS, 1), F32),
    n2_all=((4, ROWS, WIDTH), BF16), act_all=((4, ROWS, SPLIT), BF16),
    gl_all=((4, ROWS, SPLIT), BF16), po_all=((4, ROWS, WIDTH), BF16),
    po_recv=((4, ROWS, WIDTH), BF16), gn_all=((4, ROWS, WIDTH), BF16),
    gn_recv=((4, ROWS, WIDTH), BF16), gres=((ROWS, WIDTH), BF16),
    sd_x=((2, 4, 96, WIDTH), BF16), sd_y=((4, 96, WIDTH), BF16), sd_t=((4, 96, WIDTH), BF16),
    sd_z=((4, 96, WIDTH), BF16),
    su_x=((2, 4, 4, 24, SPLIT), BF16), su_y=((4, 4, 24, SPLIT), BF16),
    su_t=((4, 4, 24, SPLIT), BF16), su_z=((4, 4, 24, SPLIT), BF16), su_p=((4, 24, SPLIT), BF16),
    su_r=((4, 24, SPLIT), BF16),
    so_x=((2, 4, 4, 24, WIDTH), BF16), so_y=((4, 4, 24, WIDTH), BF16),
    so_t=((4, 4, 24, WIDTH), BF16), so_p=((4, 4, 24, WIDTH), BF16), so_u=((4, 24, WIDTH), BF16),
    so_z=((4, 24, WIDTH), BF16),
    b_x=((24, WIDTH), F32), b_y=((24, WIDTH), F32), b_p=((4, 24, 384), F32),
    b_t=((24, 384), F32), b_z=((4, 24, 384), F32), b_f=((2, 24, 384), F32),
    grad_mix=((3 * LOCAL, LENGTH), F32), raw=((2 * LOCAL, LENGTH), F32), q_s=((LOCAL, 128), F32),
    z_send=((IDS, 256), BF16), z_recv=((PARTS, IDS, 256), BF16), zx_send=((IDS, 256), F32),
    zx_recv=((IDS, 256), F32), wide=((IDS, 4 * WIDTH), F32), gt_all=((32, 24, IDS), F32),
    m_send=((80, 128), BF16), m_recv=((8, 80, 128), BF16), m2_send=((80, 128), BF16),
    m2_recv=((4, 80, 128), BF16), f_send=((2 * LOCAL, 64), F32), f_recv=((LOCAL, 64), F32),
    o_in=((24, 3 * WIDTH), F32), o_wide=((1, 3 * WIDTH), F32), o_rows=((8, WIDTH), F32),
    o_up=((1, HIDDEN), F32),
)


def fits(mesh_shape, args):
    return (
        mesh_shape["dp"] == 2
        and mesh_shape["seq"] == PARTS
        and args[0].shape == (1, ROWS)
        and args[1].shape == (12, WIDTH)
        and args[4].shape == (24, 3 * WIDTH)
        and args[8].shape == (33, 64)
        and args[18].shape == (24, HIDDEN)
    )


def fast_device(*args):
    given = SimpleNamespace(**dict(zip(INPUTS, args)))
    tables = tables_of(given.freq_weight.shape[0])
    given.mats, given.twist, given.feats = (jnp.asarray(table) for table in tables)
    given.cotangent = given.cotangent[0]
    anywhere, near = (pl.BlockSpec(memory_space=space) for space in (pl.ANY, pltpu.VMEM))
    shapes = [jax.ShapeDtypeStruct(shape, F32) for shape in OUTPUTS.values()]
    sem_count = sum(FAMILIES.values())
    made = pl.pallas_call(
        step_kernel,
        out_shape=shapes,
        in_specs=[anywhere] * len(INPUTS),
        out_specs=[anywhere] * len(shapes),
        scratch_shapes=[pltpu.VMEM(shape, kind) for shape, kind in SCRATCH.values()]
        + [pltpu.SemaphoreType.DMA((count,)) for count in (sem_count, sem_count, 48, len(shapes))],
        compiler_params=pltpu.CompilerParams(
            collective_id=0, has_side_effects=True, vmem_limit_bytes=60 * 1024 * 1024
        ),
    )(*(getattr(given, name) for name in INPUTS))
    made = pl.pallas_call(
        copy_kernel,
        out_shape=shapes,
        in_specs=[near] * len(shapes),
        out_specs=[near] * len(shapes),
    )(*made)
    return (made[0][None], *made[1:])


def solution(mesh):
    in_specs = (
        P("dp", "seq"),
        P(),
        P(),
        P(),
        P(("dp", "seq"), None),
        P(),
        P(),
        P(),
        P(),
        P(),
        P(),
        P(),
        P(("dp", "seq"), None),
        P(),
        P(("dp", "seq"), None),
        P(),
        P(),
        P(),
        P(("dp", "seq"), None),
        P(),
        P(("dp", "seq"), None),
        P(),
        P("dp", "seq", None),
    )
    out_specs = (
        P("dp", "seq", None),
        P(),
        P(),
        P(),
        P(("dp", "seq"), None),
        P(),
        P(),
        P(),
        P(),
        P(),
        P(),
        P(),
        P(("dp", "seq"), None),
        P(),
        P(("dp", "seq"), None),
        P(),
        P(),
        P(),
        P(("dp", "seq"), None),
        P(),
        P(("dp", "seq"), None),
        P(),
    )

    def either(*args):
        return (fast_device if fits(mesh.shape, args) else per_device)(*args)

    return jax.shard_map(
        either, mesh=mesh, in_specs=in_specs, out_specs=out_specs, check_vma=False
    )
```

time: 1210 us -> 129 us (0.11)
  waiting for transfers between devices: 833 us -> 0 us
  matrix products: 162 us -> 0 us
  Pallas kernels: 0 us -> 128 us
  blocking collectives: 87.6 us -> 0 us
  local copies, waits for them, and re-layouts: 47.7 us -> 0 us
  starting transfers between devices: 32 us -> 0 us
  other arithmetic: 23.5 us -> 0 us
  between operations: 16 us -> 0.83 us
    reduce_scatter x5 -> x0, waiting for transfers between devices: 581 us -> none  [the longest x1 142 us: per_device(): lax.psum_scatter(grad_down, ('dp', 'seq'), scatter_dimension=0, tiled=True)]
    dot_general x88 -> x0, matrix products: 162 us -> none  [the longest x47 79.5 us: exact_dot(): jnp.dot(left_side, right_side, precision=highest, preferred_element_type=...]
    psum x1 -> x0, waiting for transfers between devices: 160 us -> none  [per_device(): lax.psum((grad_embed, grad_gain_one, grad_bias_one, grad_in_bias, grad_ta...]
    pallas_call x0 -> x2, Pallas kernels: none -> 128 us  [the longest x1 125 us: fast_device(): pl.pallas_call(step_kernel, out_shape=shapes, in_specs=[anywhere] * len(I...]
    all_gather x4 -> x0, waiting for transfers between devices: 52.5 us -> none  [the longest x1 52.4 us: per_device(): lax.all_gather(down_weight.astype(jnp.bfloat16), ('dp', 'seq'), axis=0, t...]
    all_gather x1 -> x0, blocking collectives: 44.8 us -> none  [per_device(): lax.all_gather(filter_weight.astype(jnp.bfloat16), ('dp', 'seq'), axis=0,...]
    all_to_all x2 -> x0, blocking collectives: 42.7 us -> none  [the longest x1 22.9 us: to_rows(): lax.all_to_all(columns, 'seq', split_axis=1, concat_axis=0, tiled=True)]
    all_to_all x6 -> x0, waiting for transfers between devices: 37.7 us -> none  [the longest x3 19.3 us: to_channels(): lax.all_to_all(rows_in.T, 'seq', split_axis=0, concat_axis=1, tiled=True)]
  transfers between devices with their start and end apart: 18 -> 0, of which waited for: 15 -> 0; matrix products, arithmetic and copies ran while one was open for 13% -> 0% of each run, Pallas kernels for 0% -> 0%
where the time goes in v1:
time: 129 us
  Pallas kernels  128 us (99%)
    pallas_call x1, Pallas kernels, fast_device(): pl.pallas_call(step_kernel, out_shape=shapes, in_specs=[anywhere] * len(I...  125 us
    pallas_call x1, Pallas kernels, fast_device(): pl.pallas_call(copy_kernel, out_shape=shapes, in_specs=[near] * len(shape...  2.67 us

profile of v1, /device:TPU:0, one launch (start us, length us, event | category | flops | bytes accessed | tf_op | source)
XLA Modules:
  0.0 128.6 jit_solution(5255636448695848775)
XLA Ops:
  0.7 125.1 %shard_map.417 = (f32[128,768]{1,0:T(8,128)}, f32[12,768]{1,0:T(8,128)}, f32[768]{0:T(1024)}, f32[768]{0:T(1024)}, f32[24,2304]{1,0:T(8,128)}, /*index=5*/f32[23...) custom-call(s32[1,128]{1,0:T(1,128)} %refs_0_.1, ...), custom_call_target="tpu_custom_call" | custom-call | tf_op jit(solution)/shard_map/pallas_call | solution.py:1649
  125.8 2.7 %shard_map.418 = (f32[128,768]{1,0:T(8,128)}, f32[12,768]{1,0:T(8,128)}, f32[768]{0:T(1024)}, f32[768]{0:T(1024)}, f32[24,2304]{1,0:T(8,128)}, /*index=5*/f32[23...) custom-call(f32[128,768]{1,0:T(8,128)} %get-tuple-element.66.refs_0_, ...), custom_call_target="tpu_custom_call" | custom-call | tf_op jit(solution)/shard_map/pallas_call | solution.py:1660

commit v2 on v1

--- a/solution.py
+++ b/solution.py
@@ -576,13 +576,19 @@
         lax.fori_loop(low, high, step, 0)
 
     firsts = np.cumsum([0] + list(FAMILIES.values())).tolist()
-    fam = SimpleNamespace(**dict(zip(FAMILIES, firsts)))
-
-    def s_of(first, index):
-        return sem_s.at[first + index]
-
-    def r_of(first, index):
-        return sem_r.at[first + index]
+    fam = SimpleNamespace(**dict(zip(FAMILIES, zip(range(len(FAMILIES)), firsts))))
+
+    def s_of(family):
+        return sem_s.at[family[0]]
+
+    def r_of(family, index=0):
+        return sem_r.at[family[1] + index]
+
+    def push(family, source, target, dp_to, seq_to, index=0):
+        start_push(source, target, s_of(family), r_of(family, index), dp_to, seq_to)
+
+    def arrived(family, ref, index=0):
+        wait_for(ref, r_of(family, index))
 
     barrier = pltpu.get_barrier_semaphore()
 
@@ -597,6 +603,10 @@
         copy = pltpu.make_async_copy(source, target, sem_l.at[len(loads)])
         copy.start()
         loads.append(copy)
+
+    def load_row(source, row):
+        target = par_v.at[row] if len(source.shape) == 1 else par_v.at[row : row + 1, :]
+        pltpu.make_async_copy(source, target, sem_l.at[LOADS]).start()
 
     def wait_load(*which):
         for i in which:
@@ -612,6 +622,7 @@
     load(src.up_weight, upw_v)
     load(src.out_weight, outw_v)
     load(src.cotangent, v.seed_all.at[chip])
+    load(src.down_weight, downw_v)
     LOAD_NET = len(loads)
     load(src.freq_weight, mlp_v.at[0:33, :])
     load(src.freq_bias, mlp_v.at[33])
@@ -623,18 +634,18 @@
     load(src.twist, twist_v)
     for p in range(3):
         at = pl.ds(p * WIDTH, WIDTH)
-        load(src.in_bias.at[at], par_v.at[2 + p])
-        load(src.short_bias.at[at], par_v.at[14 + p])
+        load_row(src.in_bias.at[at], 2 + p)
+        load_row(src.short_bias.at[at], 14 + p)
         for t in range(3):
-            load(src.short_taps.at[t : t + 1, at], par_v.at[5 + 3 * t + p : 6 + 3 * t + p, :])
-    load(src.skip_scale, par_v.at[17:19, :])
+            load_row(src.short_taps.at[t : t + 1, at], 5 + 3 * t + p)
+    for t in range(2):
+        load_row(src.skip_scale.at[t : t + 1, :], 17 + t)
     load(src.out_bias, par_v.at[19])
-    load(src.gain_two, par_v.at[20])
-    load(src.bias_two, par_v.at[21])
-    load(src.down_bias, par_v.at[22])
+    load_row(src.gain_two, 20)
+    load_row(src.bias_two, 21)
+    load_row(src.down_bias, 22)
     for r in range(4):
-        load(src.up_bias.at[pl.ds(r * WIDTH, WIDTH)], par_v.at[23 + r])
-    load(src.down_weight, downw_v)
+        load_row(src.up_bias.at[pl.ds(r * WIDTH, WIDTH)], 23 + r)
     LOAD_END = len(loads)
 
     wait_load(*range(LOAD_WEIGHTS))
@@ -652,7 +663,7 @@
     p_send, p_recv = v.p_send, v.p_recv
     for i in range(PARTS):
         block = [partial[:, p * WIDTH + i * LOCAL : p * WIDTH + (i + 1) * LOCAL] for p in range(3)]
-        p_send[i] = jnp.concatenate(block, axis=1).astype(BF16)
+        p_send[i] = jnp.concatenate(block + [jnp.zeros((IDS, 256 - 3 * LOCAL), F32)], axis=1).astype(BF16)
     filt_all, tok_all = v.filt_all, v.tok_all
     filt_all[dp] = filt_v[...].astype(BF16)
     tok_all[seq] = tok_v[...]
@@ -664,12 +675,9 @@
 
     def push_p(k):
         s = of_seq(k)
-        start_push(p_send.at[s], p_recv.at[seq], s_of(fam.p, k), r_of(fam.p, seq), dp, s)
-        start_push(tok_v, tok_all.at[seq], s_of(fam.tok, k), r_of(fam.tok, seq), dp, s)
+        push(fam.p, p_send.at[s], p_recv.at[seq], dp, s)
 
     loop(1, PARTS, push_p)
-    start_push(filt_all.at[dp], filt_all.at[dp], s_of(fam.filt, 0), r_of(fam.filt, 0), other_dp, seq)
-
     wait_load(*range(LOAD_WEIGHTS, LOAD_NET))
     up_send, up_all, out_all, seed_all = v.up_send, v.up_all, v.out_all, v.seed_all
     out_all[core, chip, z] = outw_v[...].astype(BF16)
@@ -677,9 +685,17 @@
     def push_out(k):
         zz, s = of_line(k)
         mine = out_all.at[core, chip, z]
-        start_push(mine, mine, s_of(fam.outz, k), r_of(fam.outz, z), dp, s)
+        push(fam.outz, mine, mine, dp, s)
 
     loop(1, 4, push_out)
+
+    def push_tok(k):
+        s = of_seq(k)
+        push(fam.tok, tok_v, tok_all.at[seq], dp, s)
+
+    loop(1, PARTS, push_tok)
+    push(fam.filt, filt_all.at[dp], filt_all.at[dp], other_dp, seq)
+
 
     def shard_of(q, c, zz):
         return (q // 2) * PARTS + zz * 4 + (q % 2) * 2 + c
@@ -691,23 +707,23 @@
             for zz in range(4)
         ]
         up_send[q] = jnp.concatenate(cut, axis=1).astype(BF16)
-    up_all[core, z, chip] = up_send[chip]
 
     def push_up(k):
         q, d, s = of_plane(k)
-        start_push(
-            up_send.at[q], up_all.at[core, z, chip], s_of(fam.up, k), r_of(fam.up, chip), d, s
-        )
+        push(fam.up, up_send.at[q], up_all.at[core, z, chip], d, s)
+
+    across = lax.rem(z + 2, 4)
+    beside = z + 1 - 2 * lax.rem(z, 2)
+    beside_across = lax.rem(beside + 2, 4)
+
+    def to_twin(family, source, target=None):
+        push(family, source, source if target is None else target, dp, twin)
+
+    def to_line(family, source, target, zz, index):
+        push(family, source, target, dp, zz * 4 + yc, index)
 
     loop(1, 4, push_up)
-
-    def push_seed(k):
-        q, d, s = of_plane(k)
-        mine = seed_all.at[chip]
-        start_push(mine, mine, s_of(fam.seed, k), r_of(fam.seed, chip), d, s)
-
-    loop(1, 4, push_seed)
-
+    up_all[core, z, chip] = up_send[chip]
     act1, cos1, act2, cos2 = v.act1, v.cos1, v.act2, v.cos2
     wait_load(*range(LOAD_NET, LOAD_TAIL))
     mlp = mlp_v[...]
@@ -716,71 +732,59 @@
     inner = mlp[40:104]
 
     def network(i):
-        at = tile(i, 256)
-        s1, c1 = sin_cos(dot32(freq_t, feats_v[:, at], 1, 0, lax.Precision.HIGHEST))
+        at = tile(i, 512)
+        s1, c1 = sin_cos(dot32(freq_t, feats_v[:, at], 1, 0))
         act1[0:64, at] = s1
         cos1[:, at] = c1
         act1[64:72, at] = jnp.where(
-            lax.broadcasted_iota(jnp.int32, (8, 256), 0) == 0, 1.0, 0.0
+            lax.broadcasted_iota(jnp.int32, (8, 512), 0) == 0, 1.0, 0.0
         ).astype(F32)
-        s2, c2 = sin_cos(dot32(inner, s1, 0, 0, lax.Precision.HIGHEST) + inner_bias)
+        s2, c2 = sin_cos(dot32(inner, s1, 0, 0) + inner_bias)
         act2[:, at] = s2
         cos2[:, at] = c2
 
-    loop(0, LENGTH // 256, network)
-    def wait_up(k):
+    loop(0, 4, network)
+    arrived(fam.p, p_recv.at[0 : PARTS - 1])
+    table = p_recv[0].astype(F32)
+    for s in range(1, PARTS):
+        table = table + p_recv[s].astype(F32)
+    px_send, px_recv = v.px_send, v.px_recv
+    px_send[...] = table
+    push(fam.px, px_send, px_recv, other_dp, seq)
+    arrived(fam.up, up_send.at[0:3])
+    to_line(fam.upz, up_all.at[core, z], up_all.at[core, z], across, 0)
+    to_twin(fam.upt, up_all.at[core, z])
+    down_all = v.down_all
+    down_all[core, z] = downw_v[...].astype(BF16)
+    own_down = down_all.at[core, z]
+    to_line(fam.down, own_down, own_down, beside, 1)
+    to_twin(fam.downt, own_down)
+    arrived(fam.outz, out_all.at[0, 0, 0:3])
+
+    def gather_first(family, ref, k):
+        _, d, s = of_plane(k)
+        push(family, ref.at[chip], ref.at[chip], d, s, 0)
+
+    def gather_second(family, ref, k):
+        arrived(family, ref.at[0], 0)
         q, _, _ = of_plane(k)
-        wait_for(up_all.at[0, 0, 0], r_of(fam.up, q))
-
-    loop(1, 4, wait_up)
-
-    def push_up_line(k):
-        zz, s = of_line(k)
-        mine = up_all.at[core, z]
-        start_push(mine, mine, s_of(fam.upz, k), r_of(fam.upz, z), dp, s)
-
-    loop(1, 4, push_up_line)
-
-    def twin_push(name, index, ref, target=None):
-        start_push(ref, ref if target is None else target, s_of(name, index), r_of(name, index), dp, twin)
-
-    twin_push(fam.upt, z, up_all.at[core, z])
-
-    def wait_line(k):
-        zz, _ = of_line(k)
-        wait_for(out_all.at[0, 0, 0], r_of(fam.outz, zz))
-
-    loop(1, 4, wait_line)
-
-    def push_out_plane(k):
-        q, d, s = of_plane(k)
-        mine = out_all.at[core, chip]
-        start_push(mine, mine, s_of(fam.outp, k), r_of(fam.outp, chip), d, s)
-
-    loop(1, 4, push_out_plane)
-    twin_push(fam.outt, chip, out_all.at[core, chip])
+        _, d, s = of_plane(3 - k)
+        push(family, ref.at[chip], ref.at[chip], d, s, 1)
+        push(family, ref.at[q], ref.at[q], d, s, 1)
+
+    gather_first(fam.outp, out_all.at[core], 1)
+    to_twin(fam.outt, out_all.at[core, chip])
 
     wait_load(*range(LOAD_TAIL, LOAD_END))
+    wait_for(par_v.at[0:24], sem_l.at[LOADS])
     par_t = v.par_t
     for i in range(WIDTH // 128):
         par_t[128 * i : 128 * (i + 1), :] = par_v[:, 128 * i : 128 * (i + 1)].T
     own_par = par_t[tile(seq, LOCAL), :]
 
-    def wait_p(k):
-        s = of_seq(k)
-        wait_for(p_recv.at[s], r_of(fam.p, s))
-
-    loop(1, PARTS, wait_p)
-    table = p_recv[0].astype(F32)
-    for s in range(1, PARTS):
-        table = table + p_recv[s].astype(F32)
-    px_send, px_recv = v.px_send, v.px_recv
-    px_send[...] = jnp.concatenate([table, jnp.zeros((IDS, 256 - 3 * LOCAL), F32)], axis=1)
-    start_push(px_send, px_recv, s_of(fam.px, 0), r_of(fam.px, 0), other_dp, seq)
-
     kern, hi_ref, lo_ref = v.kern, v.hi, v.lo
     spec_k1, spec_k2, spec_v, spec_g = v.spec_k1, v.spec_k2, v.spec_v, v.spec_g
-    wait_for(filt_all.at[0], r_of(fam.filt, 0))
+    arrived(fam.filt, filt_all.at[0])
     filt = jnp.concatenate([filt_all[0], filt_all[1]], axis=0).astype(F32)
     for i in range(LENGTH // 256):
         both = dot32(filt, act2[:, 256 * i : 256 * (i + 1)], 1, 0)
@@ -853,18 +857,15 @@
 
     loop(0, GROUPS, kernel_spectra)
 
+
     table_t, onehot, mix = v.table_t, v.onehot, v.mix
-    wait_for(px_recv, r_of(fam.px, 0))
+    arrived(fam.px, px_recv)
     wide_t = (px_send[...] + px_recv[...]).T
     table_t[...] = jnp.concatenate(
         [wide_t[p * LOCAL : (p + 1) * LOCAL] + own_par[:, 2 + p : 3 + p] for p in range(3)], axis=0
     )
 
-    def wait_tok(k):
-        s = of_seq(k)
-        wait_for(tok_v, r_of(fam.tok, s))
-
-    loop(1, PARTS, wait_tok)
+    arrived(fam.tok, tok_all.at[0 : PARTS - 1])
     id_rows = lax.broadcasted_iota(jnp.int32, (IDS, ROWS), 0)
     for a in range(PARTS):
         now = tok_all[a]
@@ -895,28 +896,17 @@
     mix_send, mix_recv = v.mix_send, v.mix_recv
     gm_send, gm_recv = v.gm_send, v.gm_recv
 
-    def exchange(name, send, recv, g):
+    def exchange(family, send, recv, g):
         at = tile(g, LANE_CH)
 
-        def push(k):
+        def one(k):
             s = of_seq(k)
-            start_push(
-                send.at[s, at, :],
-                recv.at[seq, at, :],
-                s_of(name, g * PARTS + k),
-                r_of(name, g * PARTS + seq),
-                dp,
-                s,
-            )
-
-        loop(1, PARTS, push)
-
-    def exchanged(name, recv, g):
-        def wait(k):
-            s = of_seq(k)
-            wait_for(recv.at[0, 0:LANE_CH, :], r_of(name, g * PARTS + s))
-
-        loop(1, PARTS, wait)
+            push(family, send.at[s, at, :], recv.at[seq, at, :], dp, s, g)
+
+        loop(1, PARTS, one)
+
+    def exchanged(family, recv, g):
+        arrived(family, recv.at[0 : PARTS - 1, 0:LANE_CH, :], g)
 
     def operator(g):
         at = tile(g, LANE_CH)
@@ -946,27 +936,35 @@
 
         exchange(fam.mix, mix_send, mix_recv, g)
 
+        @pl.when(g == 0)
+        def _():
+            gather_second(fam.outp, out_all.at[core], 1)
+
+        @pl.when(g == 1)
+        def _():
+            gather_second(fam.seed, seed_all, 2 - core)
+
+    gather_first(fam.seed, seed_all, 2 - core)
     loop(0, GROUPS, operator)
+    arrived(fam.upz, up_all.at[0, 0], 0)
+    to_line(fam.upz, up_all.at[core, z], up_all.at[core, z], beside, 1)
+    to_line(fam.upz, up_all.at[core, across], up_all.at[core, across], beside, 1)
+    to_twin(fam.upt, up_all.at[core, across])
+    to_line(fam.down, own_down, own_down, across, 0)
     mix_recv[seq] = mix_send[seq]
 
-    down_all = v.down_all
-    down_all[core, z] = downw_v[...].astype(BF16)
-
-    def forward_up(k):
-        zz, _ = of_line(k)
-        wait_for(up_all.at[0, 0], r_of(fam.upz, zz))
-        twin_push(fam.upt, zz, up_all.at[core, zz])
-
-    loop(1, 4, forward_up)
+    own_onehot = (id_rows == tok_v[...]).astype(F32)
+    resid, unit2, inv2, n2_all = v.resid, v.unit2, v.inv2, v.n2_all
+    resid[...] = dot32(own_onehot, embed, 0, 0) + par_v[19:20, :]
+    arrived(fam.outp, out_all.at[0, 0:2], 1)
 
     def forward_out(k):
         q, _, _ = of_plane(k)
-        wait_for(out_all.at[0, 0], r_of(fam.outp, q))
-        twin_push(fam.outt, q, out_all.at[core, q])
+        to_twin(fam.outt, out_all.at[core, q])
 
     loop(1, 4, forward_out)
     w_up, w_out = v.w_up, v.w_out
-    loop(0, 4, lambda k: wait_for(out_all.at[0, 0], r_of(fam.outt, k)))
+    arrived(fam.outt, out_all.at[0])
 
     def place_out(i):
         q, zz = lax.div(i, 8) * 2 + lax.rem(i, 2), lax.rem(lax.div(i, 2), 4)
@@ -979,18 +977,11 @@
     for g in range(GROUPS):
         exchanged(fam.mix, mix_recv, g)
 
-    def push_down(k):
-        zz, s = of_line(k)
-        mine = down_all.at[core, z]
-        start_push(mine, mine, s_of(fam.down, k), r_of(fam.down, z), dp, s)
-
-    loop(1, 4, push_down)
-    twin_push(fam.downt, z, down_all.at[core, z])
-
-    own_onehot = (id_rows == tok_v[...]).astype(F32)
-    resid, unit2, inv2, n2_all = v.resid, v.unit2, v.inv2, v.n2_all
+
+    to_line(fam.down, own_down, own_down, beside_across, 2)
+
     mixer_t = mix_recv[...].reshape(WIDTH, ROWS)
-    residual = dot32(own_onehot, embed, 0, 0) + dot16(mixer_t, w_out[...], 0, 0) + par_v[19:20, :]
+    residual = resid[...] + dot16(mixer_t, w_out[...], 0, 0)
     resid[...] = residual
     center = residual - jnp.mean(residual, axis=-1, keepdims=True)
     inv = lax.rsqrt(jnp.mean(center * center, axis=-1, keepdims=True) + epsilon)
@@ -1002,11 +993,14 @@
     def push_n2(k):
         q, d, s = of_plane(k)
         mine = n2_all.at[chip]
-        start_push(mine, mine, s_of(fam.n2, k), r_of(fam.n2, chip), d, s)
-
-    loop(1, 4, push_n2)
-
-    loop(0, 4, lambda k: wait_for(up_all.at[0, 0], r_of(fam.upt, k)))
+        push(fam.n2, mine, mine, d, s, chip)
+
+    loop(1, 3, push_n2)
+
+    arrived(fam.upz, up_all.at[0, 0:2], 1)
+    to_twin(fam.upt, up_all.at[core, beside])
+    to_twin(fam.upt, up_all.at[core, beside_across])
+    arrived(fam.upt, up_all.at[0])
 
     def place_up(i):
         q, zz = lax.div(i, 8) * 2 + lax.rem(i, 2), lax.rem(lax.div(i, 2), 4)
@@ -1016,21 +1010,10 @@
         w_up[tile(i, 48), :] = both.astype(BF16)
 
     loop(0, 16, place_up)
-
-    def wait_seed(k):
-        q, _, _ = of_plane(k)
-        wait_for(seed_all.at[0], r_of(fam.seed, q))
-
-    loop(1, 4, wait_seed)
-
-    def forward_down(k):
-        zz, _ = of_line(k)
-        wait_for(down_all.at[0, 0], r_of(fam.down, zz))
-        twin_push(fam.downt, zz, down_all.at[core, zz])
-
-    loop(1, 4, forward_down)
-    loop(0, 4, lambda k: wait_for(down_all.at[0, 0], r_of(fam.downt, k)))
-
+    push_n2(3)
+    for index, place in ((0, across), (1, beside), (2, beside_across)):
+        arrived(fam.down, down_all.at[0, 0], index)
+        to_twin(fam.downt, down_all.at[core, place])
     up_bias = jnp.zeros((1, SPLIT), F32)
     for q in range(4):
         cut = []
@@ -1040,80 +1023,94 @@
                 row, lane0 = first // WIDTH, first % WIDTH
                 cut.append(par_v[23 + row : 24 + row, lane0 : lane0 + 96])
         up_bias = jnp.where(chip == q, jnp.concatenate(cut, axis=1), up_bias)
-    act_all, gl_all, po_all, gn_all = v.act_all, v.gl_all, v.po_all, v.gn_all
+
+    act_all, gl_all, po_all, gn_all, slope = v.act_all, v.gl_all, v.po_all, v.gn_all, v.slope
     gn_recv, po_recv = v.gn_recv, v.po_recv
 
-    def feed(k, bias_sum):
-        q, d, s = of_plane(k)
+    def feed(k):
+        q, _, _ = of_plane(k)
 
         @pl.when(k != 0)
         def _():
-            wait_for(n2_all.at[0], r_of(fam.n2, q))
-
-        down_w = down_all[...].reshape(SPLIT, WIDTH)
+            arrived(fam.n2, n2_all.at[0], q)
+
         lifted = dot16(n2_all[q], w_up[...], 1, 0) + up_bias
         cdf = 0.5 * (1.0 + lax.erf(lifted * (1.0 / math.sqrt(2.0))))
         pdf = jnp.exp(-0.5 * lifted * lifted) * (1.0 / math.sqrt(2.0 * math.pi))
-        grad_act = dot16(seed_all[q], down_w, 1, 1)
-        grad_lifted = grad_act * (cdf + lifted * pdf)
         act_all[q] = (lifted * cdf).astype(BF16)
+        slope[q] = cdf + lifted * pdf
+
+    loop(0, 4, feed)
+    arrived(fam.seed, seed_all.at[0:2], 1)
+    arrived(fam.downt, down_all.at[0])
+
+    def feed_back(k, bias_sum):
+        q, d, s = of_plane(lax.rem(k, 4))
+        grad_act = dot16(seed_all[q], down_all[...].reshape(SPLIT, WIDTH), 1, 1)
+        grad_lifted = grad_act * slope[q]
         gl_all[q] = grad_lifted.astype(BF16)
         gn_all[q] = dot16(gl_all[q], w_up[...], 1, 1).astype(BF16)
 
-        @pl.when(k != 0)
+        @pl.when(k != 4)
         def _():
-            start_push(gn_all.at[q], gn_recv.at[chip], s_of(fam.gn, k), r_of(fam.gn, chip), d, s)
-
-        po_all[q] = dot16(act_all[q], down_w, 1, 0).astype(BF16)
+            push(fam.gn, gn_all.at[q], gn_recv.at[chip], d, s)
+
         return bias_sum + jnp.sum(grad_lifted, axis=0, keepdims=True)
 
-    grad_up_bias = lax.fori_loop(0, 4, feed, jnp.zeros((1, SPLIT), F32))
+    grad_up_bias = lax.fori_loop(1, 5, feed_back, jnp.zeros((1, SPLIT), F32))
     gn_recv[chip] = gn_all[chip]
-    po_recv[chip] = po_all[chip]
 
     sd_x, sd_y, sd_t, sd_z = v.sd_x, v.sd_y, v.sd_t, v.sd_z
-    su_x, su_y, su_t, su_z, su_p, su_r = (v.su_x, v.su_y, v.su_t, v.su_z, v.su_p, v.su_r)
-    so_x, so_y, so_t, so_p, so_u, so_z = (v.so_x, v.so_y, v.so_t, v.so_p, v.so_u, v.so_z)
+    su_x, su_y, su_t, su_z, su_p, su_r = v.su_x, v.su_y, v.su_t, v.su_z, v.su_p, v.su_r
+    so_x, so_y, so_t, so_p, so_u, so_z = v.so_x, v.so_y, v.so_t, v.so_p, v.so_u, v.so_z
     acts = act_all[...].reshape(4 * ROWS, SPLIT)
     seeds = seed_all[...].reshape(4 * ROWS, WIDTH)
     for c in range(2):
         half = acts[:, c * 384 : (c + 1) * 384]
         sd_x[c] = dot16(half, seeds, 0, 0).astype(BF16).reshape(4, 96, WIDTH)
-    twin_push(fam.sdt, 0, sd_x.at[other_core], sd_y)
+    to_twin(fam.sdt, sd_x.at[other_core], sd_y)
     units = n2_all[...].reshape(4 * ROWS, WIDTH)
     lows = gl_all[...].reshape(4 * ROWS, SPLIT)
     for x in range(2):
         part = dot16(units[:, x * 384 : (x + 1) * 384], lows, 0, 0)
         for i in range(16):
             su_x[i % 2, i // 4, x * 2 + (i // 2) % 2] = part[24 * i : 24 * (i + 1)].astype(BF16)
-    twin_push(fam.sut, 0, su_x.at[other_core], su_y)
-    wait_for(sd_y, r_of(fam.sdt, 0))
-
-    def add_sd(i):
-        sd_t[i] = (sd_x[core, i].astype(F32) + sd_y[i].astype(F32)).astype(BF16)
-
+    to_twin(fam.sut, su_x.at[other_core], su_y)
+
+    def add_sd(zz):
+        sd_t[zz] = (sd_x[core, zz].astype(F32) + sd_y[zz].astype(F32)).astype(BF16)
+
+    def add_su(zz):
+        for q in range(4):
+            su_t[zz, q] = (su_x[core, zz, q].astype(F32) + su_y[zz, q].astype(F32)).astype(BF16)
+
+    def pair_first(family, sums, landing):
+        to_line(family, sums.at[beside_across], landing.at[1], beside, 0)
+
+    def pair_own(family, sums, landing):
+        to_line(family, sums.at[beside], landing.at[0], beside, 2)
+
+    def pair_second(family, sums, landing):
+        arrived(family, landing.at[0], 0)
+        sums[across] = (sums[across].astype(F32) + landing[1].astype(F32)).astype(BF16)
+        to_line(family, sums.at[across], landing.at[2], across, 1)
+
+    arrived(fam.sdt, sd_y)
     loop(0, 4, add_sd)
-    sd_z[z] = sd_t[z]
-
-    def push_sd(k):
-        zz, s = of_line(k)
-        start_push(sd_t.at[zz], sd_z.at[z], s_of(fam.sd, k), r_of(fam.sd, z), dp, s)
-
-    loop(1, 4, push_sd)
-    wait_for(su_y, r_of(fam.sut, 0))
-
-    def add_su(i):
-        for q in range(4):
-            su_t[i, q] = (su_x[core, i, q].astype(F32) + su_y[i, q].astype(F32)).astype(BF16)
-
+    pair_first(fam.sd, sd_t, sd_z)
+    pair_own(fam.sd, sd_t, sd_z)
+    arrived(fam.sut, su_y)
     loop(0, 4, add_su)
-    su_z[z] = su_t[z]
-
-    def wait_gn(k):
+    pair_first(fam.su, su_t, su_z)
+
+
+    def outputs_part(k):
         q, _, _ = of_plane(k)
-        wait_for(gn_recv.at[0], r_of(fam.gn, q))
-
-    loop(1, 4, wait_gn)
+        po_all[q] = dot16(act_all[q], down_all[...].reshape(SPLIT, WIDTH), 1, 0).astype(BF16)
+
+    loop(0, 4, outputs_part)
+
+    arrived(fam.gn, gn_all.at[0:3])
     grad_n2 = gn_recv[0].astype(F32)
     for q in range(1, 4):
         grad_n2 = grad_n2 + gn_recv[q].astype(F32)
@@ -1131,7 +1128,20 @@
     loop(0, GROUPS, lambda g: exchange(fam.gm, gm_send, gm_recv, g))
     gm_recv[seq] = gm_send[seq]
 
-    b_x, b_y, b_p, b_t, b_z, b_f = (v.b_x, v.b_y, v.b_p, v.b_t, v.b_z, v.b_f)
+    def sum_first(family, sums, landing, k):
+        q, d, s = of_plane(k)
+        push(family, sums.at[q], landing.at[0], d, s, 0)
+        q, _, _ = of_plane(3)
+        push(family, sums.at[q], landing.at[1], d, s, 0)
+
+    def sum_second(family, sums, landing, k):
+        arrived(family, landing.at[0:2], 0)
+        q, d, s = of_plane(3 - k)
+        sums[q] = (sums[q].astype(F32) + landing[1].astype(F32)).astype(BF16)
+        push(family, sums.at[q], landing.at[2], d, s, 1)
+
+    sum_first(fam.po, po_all, po_recv, 2 - core)
+    b_x, b_y, b_p, b_t, b_z, b_f = v.b_x, v.b_y, v.b_p, v.b_t, v.b_z, v.b_f
     b_x[0:12, :] = dot32(own_onehot, grad_res, 1, 0)[0:12]
     b_x[12:13, :] = jnp.sum(grad_res, axis=0, keepdims=True)
     b_x[13:14, :] = jnp.sum(grad_n2 * unit, axis=0, keepdims=True)
@@ -1140,48 +1150,21 @@
     for q in range(4):
         b_x[16 + q : 17 + q, :] = jnp.where(chip == q, grad_up_bias, 0.0)
     b_x[20:24, :] = jnp.zeros((4, WIDTH), F32)
-    twin_push(fam.bt, 0, b_x, b_y)
-
-    def push_po(k):
-        q, d, s = of_plane(k)
-        start_push(po_all.at[q], po_recv.at[chip], s_of(fam.po, k), r_of(fam.po, chip), d, s)
-
-    loop(1, 4, push_po)
+    to_twin(fam.bt, b_x, b_y)
     for x in range(2):
         part = dot16(mixer_t[x * 384 : (x + 1) * 384], gres[...], 1, 0)
         for i in range(16):
             so_x[i % 2, x * 2 + (i // 2) % 2, i // 4] = part[24 * i : 24 * (i + 1)].astype(BF16)
-    twin_push(fam.sot, 0, so_x.at[other_core], so_y)
-
-    wait_for(b_y, r_of(fam.bt, 0))
-    for c in range(2):
-
-        @pl.when(core == c)
-        def _():
-            at = slice(c * 384, (c + 1) * 384)
-            b_p[chip] = b_x[:, at] + b_y[:, at]
+    to_twin(fam.sot, so_x.at[other_core], so_y)
 
     def push_b(k):
         q, d, s = of_plane(k)
         mine = b_p.at[chip]
-        start_push(mine, mine, s_of(fam.b, k), r_of(fam.b, chip), d, s)
-
-    loop(1, 4, push_b)
-
-    wait_for(so_y, r_of(fam.sot, 0))
-
-    def add_so(i):
+        push(fam.b, mine, mine, d, s)
+
+    def add_so(zz):
         for q in range(4):
-            so_t[q, i] = (so_x[core, q, i].astype(F32) + so_y[q, i].astype(F32)).astype(BF16)
-
-    loop(0, 4, add_so)
-    so_p[chip] = so_t[chip]
-
-    def push_so(k):
-        q, d, s = of_plane(k)
-        start_push(so_t.at[q], so_p.at[chip], s_of(fam.so, k), r_of(fam.so, chip), d, s)
-
-    loop(1, 4, push_so)
+            so_t[q, zz] = (so_x[core, q, zz].astype(F32) + so_y[q, zz].astype(F32)).astype(BF16)
 
     grad_mix, raw, q_s = v.grad_mix, v.raw, v.q_s
 
@@ -1234,20 +1217,37 @@
             raw[rows_at(0), lanes] = cross[a] * decay(a)
             grad_mix[rows_at(2 * LOCAL), lanes] = grad_mix[rows_at(2 * LOCAL), lanes] + signal[a]
 
-    def push_su(k):
-        zz, s = of_line(k)
-        start_push(su_t.at[zz], su_z.at[z], s_of(fam.su, k), r_of(fam.su, z), dp, s)
+    def sums_of_rows():
+        arrived(fam.bt, b_y)
+        for c in range(2):
+
+            @pl.when(core == c)
+            def _():
+                at = slice(c * 384, (c + 1) * 384)
+                b_p[chip] = b_x[:, at] + b_y[:, at]
+
+        loop(1, 4, push_b)
 
     def group_back(g):
         exchanged(fam.gm, gm_recv, g)
 
-        @pl.when(g == GROUPS - 1)
+        @pl.when(g == 0)
         def _():
-            loop(1, 4, push_su)
+            pair_second(fam.su, su_t, su_z)
+            arrived(fam.sot, so_y)
+            loop(0, 4, add_so)
+            sum_first(fam.so, so_t, so_p, 2)
 
         operator_back(g)
 
+        @pl.when(g == 0)
+        def _():
+            sums_of_rows()
+            pair_second(fam.sd, sd_t, sd_z)
+            pair_own(fam.su, su_t, su_z)
+
     loop(0, GROUPS, group_back)
+    sum_second(fam.po, po_all, po_recv, 2 - core)
 
     zx_send, zx_recv, z_send, z_recv = v.zx_send, v.zx_recv, v.z_send, v.z_recv
     by_id = dot32(grad_mix[...], onehot[...], 1, 1)
@@ -1264,13 +1264,14 @@
     zx_send[...] = jnp.concatenate(
         [columns, skip_cols, jnp.zeros((64, IDS), F32)], axis=0
     ).T
-    start_push(zx_send, zx_recv, s_of(fam.zx, 0), r_of(fam.zx, 0), other_dp, seq)
+    push(fam.zx, zx_send, zx_recv, other_dp, seq)
+    sum_second(fam.so, so_t, so_p, 2)
 
     f_send, f_recv, m_send, m_recv, m2_send, m2_recv = (v.f_send, v.f_recv, v.m_send, v.m_recv, v.m2_send, v.m2_recv)
     grad_filter = dot32(raw[...], act2[...], 1, 1)
     f_send[...] = grad_filter
     there = f_send.at[tile(other_dp, LOCAL), :]
-    start_push(there, f_recv, s_of(fam.f, 0), r_of(fam.f, 0), other_dp, seq)
+    push(fam.f, there, f_recv, other_dp, seq)
     grad_second_pre = dot32(filt, raw[...], 0, 0) * cos2[...]
     grad_inner = dot32(act1[...], grad_second_pre, 1, 1)
     grad_first_pre = dot32(inner, grad_second_pre, 1, 0) * cos1[...]
@@ -1287,57 +1288,32 @@
 
     def push_m(k):
         j, d, s = of_eight(k)
-        start_push(m_send, m_recv.at[j_me], s_of(fam.m, k), r_of(fam.m, j_me), d, s)
+        push(fam.m, m_send, m_recv.at[j_me], d, s)
 
     loop(1, 8, push_m)
 
-    wait_for(zx_recv, r_of(fam.zx, 0))
+    arrived(fam.zx, zx_recv)
     z_send[...] = (zx_send[...] + zx_recv[...]).astype(BF16)
     z_recv[seq] = z_send[...]
 
     def push_z(k):
         s = of_seq(k)
-        start_push(z_send, z_recv.at[seq], s_of(fam.z, k), r_of(fam.z, seq), dp, s)
+        push(fam.z, z_send, z_recv.at[seq], dp, s)
 
     loop(1, PARTS, push_z)
-
-    def wait_b(k):
-        q, _, _ = of_plane(k)
-        wait_for(b_p.at[0], r_of(fam.b, q))
-
-    loop(1, 4, wait_b)
-    b_t[...] = (b_p[0] + b_p[1]) + (b_p[2] + b_p[3])
-    b_z[z] = b_t[...]
-
-    def push_b2(k):
-        zz, s = of_line(k)
-        start_push(b_t, b_z.at[z], s_of(fam.b2, k), r_of(fam.b2, z), dp, s)
-
-    loop(1, 4, push_b2)
-
-    def wait_so(k):
-        q, _, _ = of_plane(k)
-        wait_for(so_p.at[0], r_of(fam.so, q))
-
-    loop(1, 4, wait_so)
-    for zz in range(4):
-        part = so_p[0, zz].astype(F32)
-        for q in range(1, 4):
-            part = part + so_p[q, zz].astype(F32)
-        so_u[zz] = part.astype(BF16)
-    so_z[z] = so_u[z]
-
-    def push_so2(k):
-        zz, s = of_line(k)
-        start_push(so_u.at[zz], so_z.at[z], s_of(fam.so2, k), r_of(fam.so2, z), dp, s)
-
-    loop(1, 4, push_so2)
-
-    def wait_m(k):
-        j, _, _ = of_eight(k)
-        wait_for(m_send, r_of(fam.m, j))
-
-    loop(1, 8, wait_m)
+    arrived(fam.su, su_z.at[2], 1)
+    arrived(fam.su, su_z.at[0], 2)
+    for q in range(4):
+        part = su_t[z, q].astype(F32) + su_z[0, q].astype(F32) + su_z[2, q].astype(F32)
+        su_p[q] = part.astype(BF16)
+    su_r[chip] = su_p[chip]
+
+    def push_su2(k):
+        q, d, s = of_plane(k)
+        push(fam.su2, su_p.at[q], su_r.at[chip], d, s)
+
+    loop(1, 4, push_su2)
+    arrived(fam.m, m_recv.at[0:7])
     totals = m_recv[0].astype(F32)
     for j in range(1, 8):
         totals = totals + m_recv[j].astype(F32)
@@ -1346,35 +1322,34 @@
 
     def push_m2(k):
         zz, s = of_line(k)
-        start_push(m2_send, m2_recv.at[z], s_of(fam.m2, k), r_of(fam.m2, z), dp, s)
+        push(fam.m2, m2_send, m2_recv.at[z], dp, s)
 
     loop(1, 4, push_m2)
 
-    def wait_su(k):
-        zz, _ = of_line(k)
-        wait_for(su_z.at[0], r_of(fam.su, zz))
-
-    loop(1, 4, wait_su)
-    for q in range(4):
-        part = su_z[0, q].astype(F32)
-        for zz in range(1, 4):
-            part = part + su_z[zz, q].astype(F32)
-        su_p[q] = part.astype(BF16)
-    su_r[chip] = su_p[chip]
-
-    def push_su2(k):
-        q, d, s = of_plane(k)
-        start_push(su_p.at[q], su_r.at[chip], s_of(fam.su2, k), r_of(fam.su2, chip), d, s)
-
-    loop(1, 4, push_su2)
+
+    arrived(fam.b, b_p.at[0:3])
+    b_t[...] = (b_p[0] + b_p[1]) + (b_p[2] + b_p[3])
+    b_z[z] = b_t[...]
+
+    def push_b2(k):
+        zz, s = of_line(k)
+        push(fam.b2, b_t, b_z.at[z], dp, s)
+
+    loop(1, 4, push_b2)
+    arrived(fam.so, so_p.at[0], 1)
+    for zz in range(4):
+        part = so_t[chip, zz].astype(F32) + so_p[0, zz].astype(F32) + so_p[2, zz].astype(F32)
+        so_u[zz] = part.astype(BF16)
+    so_z[z] = so_u[z]
+
+    def push_so2(k):
+        zz, s = of_line(k)
+        push(fam.so2, so_u.at[zz], so_z.at[z], dp, s)
+
+    loop(1, 4, push_so2)
 
     wide, gt_all = v.wide, v.gt_all
-
-    def wait_z(k):
-        s = of_seq(k)
-        wait_for(z_send, r_of(fam.z, s))
-
-    loop(1, PARTS, wait_z)
+    arrived(fam.z, z_recv.at[0 : PARTS - 1])
     for p in range(4):
         for i in range(PARTS):
             wide[:, p * WIDTH + i * LOCAL : p * WIDTH + (i + 1) * LOCAL] = z_recv[i][
@@ -1383,12 +1358,15 @@
     by_ids = jnp.where(
         lax.broadcasted_iota(jnp.int32, (IDS, 3 * WIDTH), 0) < 12, wide[:, 0 : 3 * WIDTH], 0.0
     )
-    gt_all[me] = dot32(in_low, by_ids, 1, 1)
+    own_gt = dot32(in_low, by_ids, 1, 1)
+    gt_all[me] = jnp.concatenate(
+        [own_gt[8 * t : 8 * (t + 1)] for t in range(3)] + [jnp.zeros((8, 80), F32)], axis=1
+    )
 
     def push_gt(k):
         _, d, s = everyone(k)
         mine = gt_all.at[me]
-        start_push(mine, mine, s_of(fam.gt, k), r_of(fam.gt, me), d, s)
+        push(fam.gt, mine, mine, d, s)
 
     loop(1, 2 * PARTS, push_gt)
 
@@ -1409,36 +1387,22 @@
     store(wide.at[15, pl.ds(0, 3 * WIDTH)], out.short_bias)
     store(o_rows.at[2:4, :], out.skip_scale)
 
-    def wait_po(k):
-        q, _, _ = of_plane(k)
-        wait_for(po_recv.at[0], r_of(fam.po, q))
-
-    loop(1, 4, wait_po)
-    block = resid[...] + par_v[22:23, :]
-    for q in range(4):
-        block = block + po_recv[q].astype(F32)
+    arrived(fam.po, po_recv.at[0], 1)
+    block = resid[...] + par_v[22:23, :] + po_all[chip].astype(F32)
+    block = block + po_recv[0].astype(F32) + po_recv[2].astype(F32)
     resid[...] = block
     store(resid, out.block)
 
-    def wait_sd(k):
-        zz, _ = of_line(k)
-        wait_for(sd_z.at[0], r_of(fam.sd, zz))
-
-    loop(1, 4, wait_sd)
-    part = sd_z[0].astype(F32)
-    for zz in range(1, 4):
-        part = part + sd_z[zz].astype(F32)
+    arrived(fam.sd, sd_z.at[2], 1)
+    arrived(fam.sd, sd_z.at[0], 2)
+    part = sd_t[z].astype(F32) + sd_z[0].astype(F32) + sd_z[2].astype(F32)
     downw_v[...] = part
     store(downw_v, out.down_weight)
-    wait_for(f_recv, r_of(fam.f, 0))
+    arrived(fam.f, f_recv)
     f_recv[...] = f_send[tile(dp, LOCAL), :] + f_recv[...]
     store(f_recv, out.filter_weight)
 
-    def wait_su2(k):
-        q, _, _ = of_plane(k)
-        wait_for(su_r.at[0], r_of(fam.su2, q))
-
-    loop(1, 4, wait_su2)
+    arrived(fam.su2, su_r.at[0:3])
     for q in range(4):
         part = su_r[q].astype(F32)
         for c in range(2):
@@ -1447,21 +1411,16 @@
                 upw_v[:, first : first + 96] = part[:, place : place + 96]
     store(upw_v, out.up_weight)
 
-    def wait_so2(k):
-        zz, _ = of_line(k)
-        wait_for(so_z.at[0], r_of(fam.so2, zz))
-        wait_for(b_t, r_of(fam.b2, zz))
-        wait_for(m2_send, r_of(fam.m2, zz))
-
-    loop(1, 4, wait_so2)
+    arrived(fam.b2, b_z.at[0:3])
     b_f[core] = (b_z[0] + b_z[1]) + (b_z[2] + b_z[3])
-    mine = b_f.at[core]
-    start_push(mine, mine, s_of(fam.bf, 0), r_of(fam.bf, 0), dp, twin)
+    to_twin(fam.bf, b_f.at[core])
+    arrived(fam.so2, so_z.at[0:3])
     part = so_z[0].astype(F32)
     for zz in range(1, 4):
         part = part + so_z[zz].astype(F32)
     outw_v[...] = part
     store(outw_v, out.out_weight)
+    arrived(fam.m2, m2_recv.at[0:3])
     totals = m2_recv[0].astype(F32)
     for zz in range(1, 4):
         totals = totals + m2_recv[zz].astype(F32)
@@ -1471,7 +1430,7 @@
     store(mlp_v.at[33], out.freq_bias)
     store(mlp_v.at[40:104, :], out.inner_weight)
     store(mlp_v.at[104], out.inner_bias)
-    wait_for(b_f.at[0], r_of(fam.bf, 0))
+    arrived(fam.bf, b_f.at[0])
     totals = jnp.concatenate([b_f[0], b_f[1]], axis=1)
     o_rows[4:8, :] = totals[12:16]
     o_up = v.o_up
@@ -1486,12 +1445,10 @@
     store(o_rows.at[7], out.down_bias)
     store(o_up.at[0], out.up_bias)
 
-    def wait_gt(k):
-        d, _, _ = everyone(k)
-        wait_for(gt_all.at[0], r_of(fam.gt, d))
-
-    loop(1, 2 * PARTS, wait_gt)
-    grad_normed = gt_all[...].reshape(WIDTH, IDS).T
+    arrived(fam.gt, gt_all.at[0 : 2 * PARTS - 1])
+    gts = gt_all[...]
+    grad_normed = jnp.concatenate([gts[:, :, IDS * t : IDS * (t + 1)] for t in range(3)], axis=1)
+    grad_normed = grad_normed.reshape(WIDTH, IDS).T
     o_rows[0:1, :] = jnp.sum(grad_normed * unit_one, axis=0, keepdims=True)
     o_rows[1:2, :] = jnp.sum(grad_normed, axis=0, keepdims=True)
     scaled = grad_normed * par_v[0:1, :]
@@ -1505,46 +1462,20 @@
     store(o_rows.at[1], out.bias_one)
     store(emb_v, out.embed_table)
 
-    def sent(name, ref, low, high):
-        loop(low, high, lambda k: wait_for(ref, s_of(name, k)))
-
-    sent(fam.p, p_send.at[0], 1, PARTS)
-    sent(fam.tok, tok_v, 1, PARTS)
-    sent(fam.filt, filt_all.at[0], 0, 1)
-    sent(fam.px, px_send, 0, 1)
-    sent(fam.outz, out_all.at[0, 0, 0], 1, 4)
-    sent(fam.outp, out_all.at[0, 0], 1, 4)
-    sent(fam.outt, out_all.at[0, 0], 0, 4)
-    sent(fam.up, up_send.at[0], 1, 4)
-    sent(fam.upz, up_all.at[0, 0], 1, 4)
-    sent(fam.upt, up_all.at[0, 0], 0, 4)
-    sent(fam.seed, seed_all.at[0], 1, 4)
-    sent(fam.down, down_all.at[0, 0], 1, 4)
-    sent(fam.downt, down_all.at[0, 0], 0, 4)
-    for g in range(GROUPS):
-        sent(fam.mix, mix_send.at[0, 0:LANE_CH, :], g * PARTS + 1, (g + 1) * PARTS)
-        sent(fam.gm, gm_send.at[0, 0:LANE_CH, :], g * PARTS + 1, (g + 1) * PARTS)
-    sent(fam.n2, n2_all.at[0], 1, 4)
-    sent(fam.gn, gn_all.at[0], 1, 4)
-    sent(fam.po, po_all.at[0], 1, 4)
-    sent(fam.sdt, sd_y, 0, 1)
-    sent(fam.sut, su_y, 0, 1)
-    sent(fam.sot, so_y, 0, 1)
-    sent(fam.sd, sd_t.at[0], 1, 4)
-    sent(fam.su, su_t.at[0], 1, 4)
-    sent(fam.su2, su_p.at[0], 1, 4)
-    sent(fam.so, so_t.at[0], 1, 4)
-    sent(fam.so2, so_u.at[0], 1, 4)
-    sent(fam.bt, b_x, 0, 1)
-    sent(fam.b, b_p.at[0], 1, 4)
-    sent(fam.b2, b_t, 1, 4)
-    sent(fam.bf, b_f.at[0], 0, 1)
-    sent(fam.m, m_send, 1, 8)
-    sent(fam.m2, m2_send, 1, 4)
-    sent(fam.z, z_send, 1, PARTS)
-    sent(fam.zx, zx_send, 0, 1)
-    sent(fam.f, f_recv, 0, 1)
-    sent(fam.gt, gt_all.at[0], 1, 2 * PARTS)
+    for family, ref in (
+        (fam.p, p_send.at[0 : PARTS - 1]), (fam.tok, tok_all.at[0 : PARTS - 1]), (fam.filt, filt_all.at[0]),
+        (fam.px, px_send), (fam.outz, out_all.at[0, 0, 0:3]), (fam.outp, out_all.at[0, 0:3]),
+        (fam.outt, out_all.at[0]), (fam.up, up_send.at[0:3]), (fam.upz, up_all.at[0, 0:3]),
+        (fam.upt, up_all.at[0]), (fam.seed, seed_all.at[0:3]), (fam.down, down_all.at[0, 0:3]),
+        (fam.downt, down_all.at[0]), (fam.mix, mix_send.at[0 : PARTS - 1]),
+        (fam.gm, gm_send.at[0 : PARTS - 1]), (fam.n2, n2_all.at[0:3]), (fam.gn, gn_all.at[0:3]),
+        (fam.po, po_all.at[0:3]), (fam.sdt, sd_y), (fam.sut, su_y), (fam.sot, so_y), (fam.sd, sd_t.at[0:3]),
+        (fam.su, su_t.at[0:3]), (fam.su2, su_p.at[0:3]), (fam.so, so_t.at[0:3]), (fam.so2, so_u.at[0:3]),
+        (fam.bt, b_x), (fam.b, b_p.at[0:3]), (fam.b2, b_z.at[0:3]), (fam.bf, b_f.at[0]),
+        (fam.m, m_recv.at[0:7]), (fam.m2, m2_recv.at[0:3]), (fam.z, z_recv.at[0 : PARTS - 1]),
+        (fam.zx, zx_send), (fam.f, f_recv), (fam.gt, gt_all.at[0 : 2 * PARTS - 1]),
+    ):
+        wait_for(ref, s_of(family))
     for copy in stores:
         copy.wait()
 
@@ -1556,12 +1487,11 @@
 
 
 FAMILIES = dict(
-    p=16, tok=16, filt=1, px=1, outz=4, outp=4, outt=4, up=4,
-    upz=4, upt=4, down=4, downt=4, seed=4, mix=48, gm=48, n2=4,
-    gn=4, po=4, sdt=1, sd=4, sut=1, su=4, su2=4, sot=1, so=4,
-    so2=4, bt=1, b=4, b2=4, bf=1, m=8, m2=4, z=16, zx=1,
-    f=1, gt=32,
+    p=1, tok=1, filt=1, px=1, outz=1, outp=2, outt=1, up=1, upz=2, upt=1, down=3, downt=1, seed=2, mix=3,
+    gm=3, n2=4, gn=1, po=2, sdt=1, sd=3, sut=1, su=3, su2=1, sot=1, so=2, so2=1, bt=1, b=1, b2=1, bf=1,
+    m=1, m2=1, z=1, zx=1, f=1, gt=1,
 )
+LOADS = 18
 INPUTS = dict(
     token_ids=0, embed_table=0, gain_one=0, bias_one=0, in_weight=0, in_bias=0, short_taps=0, short_bias=0,
     freq_weight=0, freq_bias=0, inner_weight=0, inner_bias=0, filter_weight=0, skip_scale=0, out_weight=0,
@@ -1584,8 +1514,8 @@
     inw=((24, 3 * WIDTH), F32), mlp=((112, 64), F32), filt=((LOCAL, 64), F32),
     outw=((24, WIDTH), F32), upw=((24, HIDDEN), F32), downw=((96, WIDTH), F32),
     mats=((4, 256, 256), BF16), twist=((72, ROWS), F32), feats=((40, LENGTH), F32),
-    normed_t=((WIDTH, IDS), F32), p_send=((PARTS, IDS, 3 * LOCAL), BF16),
-    p_recv=((PARTS, IDS, 3 * LOCAL), BF16), px_send=((IDS, 256), F32), px_recv=((IDS, 256), F32),
+    normed_t=((WIDTH, IDS), F32), p_send=((PARTS, IDS, 256), BF16),
+    p_recv=((PARTS, IDS, 256), BF16), px_send=((IDS, 256), F32), px_recv=((IDS, 256), F32),
     filt_all=((2, LOCAL, 64), BF16), tok_all=((PARTS, 1, ROWS), jnp.int32),
     up_send=((4, 24, SPLIT), BF16), up_all=((2, 4, 4, 24, SPLIT), BF16),
     out_all=((2, 4, 4, 24, WIDTH), BF16), seed_all=((4, ROWS, WIDTH), BF16),
@@ -1603,22 +1533,22 @@
     gm_send=((PARTS, LOCAL, ROWS), BF16), gm_recv=((PARTS, LOCAL, ROWS), BF16),
     resid=((ROWS, WIDTH), F32), unit2=((ROWS, WIDTH), F32), inv2=((ROWS, 1), F32),
     n2_all=((4, ROWS, WIDTH), BF16), act_all=((4, ROWS, SPLIT), BF16),
-    gl_all=((4, ROWS, SPLIT), BF16), po_all=((4, ROWS, WIDTH), BF16),
-    po_recv=((4, ROWS, WIDTH), BF16), gn_all=((4, ROWS, WIDTH), BF16),
+    gl_all=((4, ROWS, SPLIT), BF16), slope=((4, ROWS, SPLIT), F32), po_all=((4, ROWS, WIDTH), BF16),
+    po_recv=((3, ROWS, WIDTH), BF16), gn_all=((4, ROWS, WIDTH), BF16),
     gn_recv=((4, ROWS, WIDTH), BF16), gres=((ROWS, WIDTH), BF16),
     sd_x=((2, 4, 96, WIDTH), BF16), sd_y=((4, 96, WIDTH), BF16), sd_t=((4, 96, WIDTH), BF16),
-    sd_z=((4, 96, WIDTH), BF16),
+    sd_z=((3, 96, WIDTH), BF16),
     su_x=((2, 4, 4, 24, SPLIT), BF16), su_y=((4, 4, 24, SPLIT), BF16),
-    su_t=((4, 4, 24, SPLIT), BF16), su_z=((4, 4, 24, SPLIT), BF16), su_p=((4, 24, SPLIT), BF16),
+    su_t=((4, 4, 24, SPLIT), BF16), su_z=((3, 4, 24, SPLIT), BF16), su_p=((4, 24, SPLIT), BF16),
     su_r=((4, 24, SPLIT), BF16),
     so_x=((2, 4, 4, 24, WIDTH), BF16), so_y=((4, 4, 24, WIDTH), BF16),
-    so_t=((4, 4, 24, WIDTH), BF16), so_p=((4, 4, 24, WIDTH), BF16), so_u=((4, 24, WIDTH), BF16),
+    so_t=((4, 4, 24, WIDTH), BF16), so_p=((3, 4, 24, WIDTH), BF16), so_u=((4, 24, WIDTH), BF16),
     so_z=((4, 24, WIDTH), BF16),
     b_x=((24, WIDTH), F32), b_y=((24, WIDTH), F32), b_p=((4, 24, 384), F32),
     b_t=((24, 384), F32), b_z=((4, 24, 384), F32), b_f=((2, 24, 384), F32),
     grad_mix=((3 * LOCAL, LENGTH), F32), raw=((2 * LOCAL, LENGTH), F32), q_s=((LOCAL, 128), F32),
     z_send=((IDS, 256), BF16), z_recv=((PARTS, IDS, 256), BF16), zx_send=((IDS, 256), F32),
-    zx_recv=((IDS, 256), F32), wide=((IDS, 4 * WIDTH), F32), gt_all=((32, 24, IDS), F32),
+    zx_recv=((IDS, 256), F32), wide=((IDS, 4 * WIDTH), F32), gt_all=((32, 8, 128), F32),
     m_send=((80, 128), BF16), m_recv=((8, 80, 128), BF16), m2_send=((80, 128), BF16),
     m2_recv=((4, 80, 128), BF16), f_send=((2 * LOCAL, 64), F32), f_recv=((LOCAL, 64), F32),
     o_in=((24, 3 * WIDTH), F32), o_wide=((1, 3 * WIDTH), F32), o_rows=((8, WIDTH), F32),
@@ -1645,14 +1575,14 @@
     given.cotangent = given.cotangent[0]
     anywhere, near = (pl.BlockSpec(memory_space=space) for space in (pl.ANY, pltpu.VMEM))
     shapes = [jax.ShapeDtypeStruct(shape, F32) for shape in OUTPUTS.values()]
-    sem_count = sum(FAMILIES.values())
+    counts = (len(FAMILIES), sum(FAMILIES.values()), LOADS + 1, len(shapes))
     made = pl.pallas_call(
         step_kernel,
         out_shape=shapes,
         in_specs=[anywhere] * len(INPUTS),
         out_specs=[anywhere] * len(shapes),
         scratch_shapes=[pltpu.VMEM(shape, kind) for shape, kind in SCRATCH.values()]
-        + [pltpu.SemaphoreType.DMA((count,)) for count in (sem_count, sem_count, 48, len(shapes))],
+        + [pltpu.SemaphoreType.DMA((count,)) for count in counts],
         compiler_params=pltpu.CompilerParams(
             collective_id=0, has_side_effects=True, vmem_limit_bytes=60 * 1024 * 1024
         ),

time: 129 us -> 105 us (0.81)
  Pallas kernels: 128 us -> 104 us
    pallas_call x1, Pallas kernels: 125 us -> 102 us  [fast_device(): pl.pallas_call(step_kernel, out_shape=shapes, in_specs=[anywhere] * len(I...]
where the time goes in v2:
time: 105 us
  Pallas kernels  104 us (99%)
    pallas_call x1, Pallas kernels, fast_device(): pl.pallas_call(step_kernel, out_shape=shapes, in_specs=[anywhere] * len(I...  102 us
    pallas_call x1, Pallas kernels, fast_device(): pl.pallas_call(copy_kernel, out_shape=shapes, in_specs=[near] * len(shape...  2.67 us

profile of v2, /device:TPU:0, one launch (start us, length us, event | category | flops | bytes accessed | tf_op | source)
XLA Modules:
  0.0 105.0 jit_solution(17610908325072348174)
XLA Ops:
  0.7 101.5 %shard_map.417 = (f32[128,768]{1,0:T(8,128)}, f32[12,768]{1,0:T(8,128)}, f32[768]{0:T(1024)}, f32[768]{0:T(1024)}, f32[24,2304]{1,0:T(8,128)}, /*index=5*/f32[23...) custom-call(s32[1,128]{1,0:T(1,128)} %refs_0_.1, ...), custom_call_target="tpu_custom_call" | custom-call | tf_op jit(solution)/shard_map/pallas_call | solution.py:1579
  102.2 2.7 %shard_map.418 = (f32[128,768]{1,0:T(8,128)}, f32[12,768]{1,0:T(8,128)}, f32[768]{0:T(1024)}, f32[768]{0:T(1024)}, f32[24,2304]{1,0:T(8,128)}, /*index=5*/f32[23...) custom-call(f32[128,768]{1,0:T(8,128)} %get-tuple-element.66.refs_0_, ...), custom_call_target="tpu_custom_call" | custom-call | tf_op jit(solution)/shard_map/pallas_call | solution.py:1590

commit v3 on v2

--- a/solution.py
+++ b/solution.py
@@ -547,7 +547,7 @@
     other_dp = 1 - dp
 
     def tile(index, size):
-        return pl.ds(pl.multiple_of(index * size, size), size)
+        return pl.ds(index * size if isinstance(index, int) else pl.multiple_of(index * size, size), size)
 
     def everyone(k):
         d = lax.rem(me + k, 2 * PARTS)
@@ -719,10 +719,66 @@
     def to_twin(family, source, target=None):
         push(family, source, source if target is None else target, dp, twin)
 
+    def relay(family, onward, ref, block, zz):
+        start_push(ref.at[block], ref.at[block], s_of(onward), r_of(family, block), dp, zz * 4 + yc)
+
+    def spread_start(family, ref):
+        @pl.when(z > 0)
+        def _():
+            relay(family, family, ref, z, z - 1)
+
+        @pl.when(z < 3)
+        def _():
+            relay(family, family, ref, z, z + 1)
+
+    def spread_near(family, onward, twins, ref):
+        @pl.when(z > 0)
+        def _():
+            arrived(family, ref.at[0], z - 1)
+
+            @pl.when(z < 3)
+            def _():
+                relay(family, onward, ref, z - 1, z + 1)
+
+            to_twin(twins, ref.at[z - 1])
+
+        @pl.when(z < 3)
+        def _():
+            arrived(family, ref.at[0], z + 1)
+
+            @pl.when(z > 0)
+            def _():
+                relay(family, onward, ref, z + 1, z - 1)
+
+            to_twin(twins, ref.at[z + 1])
+
+    def spread_far(family, onward, twins, ref):
+        arrived(family, ref.at[0], across)
+
+        @pl.when(z == 1)
+        def _():
+            relay(family, onward, ref, across, 0)
+
+        @pl.when(z == 2)
+        def _():
+            relay(family, onward, ref, across, 3)
+
+        to_twin(twins, ref.at[across])
+
+    def spread_last(family, twins, ref):
+        @pl.when(lax.rem(z, 3) == 0)
+        def _():
+            arrived(family, ref.at[0], 3 - z)
+            to_twin(twins, ref.at[3 - z])
+
     def to_line(family, source, target, zz, index):
         push(family, source, target, dp, zz * 4 + yc, index)
 
     loop(1, 4, push_up)
+    down_all = v.down_all
+    down_all[core, z] = downw_v[...].astype(BF16)
+    spread_start(fam.down, down_all.at[core])
+    to_twin(fam.downt, down_all.at[core, z])
     up_all[core, z, chip] = up_send[chip]
     act1, cos1, act2, cos2 = v.act1, v.cos1, v.act2, v.cos2
     wait_load(*range(LOAD_NET, LOAD_TAIL))
@@ -744,23 +800,6 @@
         cos2[:, at] = c2
 
     loop(0, 4, network)
-    arrived(fam.p, p_recv.at[0 : PARTS - 1])
-    table = p_recv[0].astype(F32)
-    for s in range(1, PARTS):
-        table = table + p_recv[s].astype(F32)
-    px_send, px_recv = v.px_send, v.px_recv
-    px_send[...] = table
-    push(fam.px, px_send, px_recv, other_dp, seq)
-    arrived(fam.up, up_send.at[0:3])
-    to_line(fam.upz, up_all.at[core, z], up_all.at[core, z], across, 0)
-    to_twin(fam.upt, up_all.at[core, z])
-    down_all = v.down_all
-    down_all[core, z] = downw_v[...].astype(BF16)
-    own_down = down_all.at[core, z]
-    to_line(fam.down, own_down, own_down, beside, 1)
-    to_twin(fam.downt, own_down)
-    arrived(fam.outz, out_all.at[0, 0, 0:3])
-
     def gather_first(family, ref, k):
         _, d, s = of_plane(k)
         push(family, ref.at[chip], ref.at[chip], d, s, 0)
@@ -772,8 +811,6 @@
         push(family, ref.at[chip], ref.at[chip], d, s, 1)
         push(family, ref.at[q], ref.at[q], d, s, 1)
 
-    gather_first(fam.outp, out_all.at[core], 1)
-    to_twin(fam.outt, out_all.at[core, chip])
 
     wait_load(*range(LOAD_TAIL, LOAD_END))
     wait_for(par_v.at[0:24], sem_l.at[LOADS])
@@ -798,13 +835,15 @@
         rate = slow_rate + (fast_rate - slow_rate) * (row.astype(F32) * (1.0 / (WIDTH - 1)))
         return lambda a: jnp.exp((lane + float(a * ROWS)) * (rate * (-1.0 / LENGTH))) + decay_shift
 
+    turn = [0]
+
     def put(row0, k, re, im):
         rows = pl.ds(row0 + k * LANE_CH, LANE_CH)
         for part, value in ((0, re), (1, im)):
             at = pl.ds(part * ROWS, ROWS)
             high = value.astype(BF16)
-            hi_ref[rows, at] = high
-            lo_ref[rows, at] = (value - high.astype(F32)).astype(BF16)
+            hi_ref[turn[0], rows, at] = high
+            lo_ref[turn[0], rows, at] = (value - high.astype(F32)).astype(BF16)
 
     def forth(row0, values):
         for k, (re, im) in enumerate(real_spectrum(values)):
@@ -815,7 +854,7 @@
                 put(row0, k, re * c + im * s, im * c - re * s)
 
     def dft(rows, which):
-        high, low = hi_ref[0:rows, :], lo_ref[0:rows, :]
+        high, low = hi_ref[turn[0], 0:rows, :], lo_ref[turn[0], 0:rows, :]
         m_high, m_low = mats_v[which], mats_v[which + 1]
         return dot16(high, m_high, 1, 0) + dot16(low, m_high, 1, 0) + dot16(high, m_low, 1, 0)
 
@@ -830,8 +869,8 @@
         for part, value in ((0, re), (1, im)):
             at = pl.ds(part * ROWS, ROWS)
             high = value.astype(BF16)
-            hi_ref[rows, at] = high
-            lo_ref[rows, at] = (value - high.astype(F32)).astype(BF16)
+            hi_ref[turn[0], rows, at] = high
+            lo_ref[turn[0], rows, at] = (value - high.astype(F32)).astype(BF16)
 
     def back(turned, row0):
         bins = []
@@ -846,6 +885,7 @@
         return real_signal(bins)
 
     def kernel_spectra(g):
+        turn[0] = g
         at = tile(g, LANE_CH)
         decay = decay_of(g)
         damp = [decay(a) for a in range(PARTS)]
@@ -855,7 +895,24 @@
         spec_k1[g] = spec[0:SPEC]
         spec_k2[g] = spec[SPEC:]
 
-    loop(0, GROUPS, kernel_spectra)
+    kernel_spectra(0)
+    kernel_spectra(1)
+
+    arrived(fam.p, p_recv.at[0 : PARTS - 1])
+    table = p_recv[0].astype(F32)
+    for s in range(1, PARTS):
+        table = table + p_recv[s].astype(F32)
+    px_send, px_recv = v.px_send, v.px_recv
+    px_send[...] = table
+    push(fam.px, px_send, px_recv, other_dp, seq)
+    arrived(fam.up, up_send.at[0:3])
+    spread_start(fam.upz, up_all.at[core])
+    to_twin(fam.upt, up_all.at[core, z])
+    arrived(fam.outz, out_all.at[0, 0, 0:3])
+    gather_first(fam.outp, out_all.at[core], 2 - core)
+    to_twin(fam.outt, out_all.at[core, chip])
+    kernel_spectra(2)
+    spread_near(fam.down, fam.downf, fam.downt, down_all.at[core])
 
 
     table_t, onehot, mix = v.table_t, v.onehot, v.mix
@@ -896,19 +953,15 @@
     mix_send, mix_recv = v.mix_send, v.mix_recv
     gm_send, gm_recv = v.gm_send, v.gm_recv
 
-    def exchange(family, send, recv, g):
-        at = tile(g, LANE_CH)
-
+    def exchange(family, send, recv):
         def one(k):
             s = of_seq(k)
-            push(family, send.at[s, at, :], recv.at[seq, at, :], dp, s, g)
+            push(family, send.at[s], recv.at[seq], dp, s)
 
         loop(1, PARTS, one)
 
-    def exchanged(family, recv, g):
-        arrived(family, recv.at[0 : PARTS - 1, 0:LANE_CH, :], g)
-
     def operator(g):
+        turn[0] = g
         at = tile(g, LANE_CH)
         skips = par_t[pl.ds(pl.multiple_of(seq * LOCAL + g * LANE_CH, LANE_CH), LANE_CH), :]
         skip0, skip1 = skips[:, 17:18], skips[:, 18:19]
@@ -934,23 +987,13 @@
             second_s[a, at, :] = conv
             mix_send[a, at, :] = (mix[0, a, at, :] * conv).astype(BF16)
 
-        exchange(fam.mix, mix_send, mix_recv, g)
-
-        @pl.when(g == 0)
-        def _():
-            gather_second(fam.outp, out_all.at[core], 1)
-
-        @pl.when(g == 1)
-        def _():
-            gather_second(fam.seed, seed_all, 2 - core)
-
+
+    gather_second(fam.outp, out_all.at[core], 2 - core)
     gather_first(fam.seed, seed_all, 2 - core)
-    loop(0, GROUPS, operator)
-    arrived(fam.upz, up_all.at[0, 0], 0)
-    to_line(fam.upz, up_all.at[core, z], up_all.at[core, z], beside, 1)
-    to_line(fam.upz, up_all.at[core, across], up_all.at[core, across], beside, 1)
-    to_twin(fam.upt, up_all.at[core, across])
-    to_line(fam.down, own_down, own_down, across, 0)
+    for g in range(GROUPS):
+        operator(g)
+    exchange(fam.mix, mix_send, mix_recv)
+    spread_near(fam.upz, fam.upf, fam.upt, up_all.at[core])
     mix_recv[seq] = mix_send[seq]
 
     own_onehot = (id_rows == tok_v[...]).astype(F32)
@@ -974,11 +1017,8 @@
         w_out[tile(i, 48), :] = both.astype(BF16)
 
     loop(0, 16, place_out)
-    for g in range(GROUPS):
-        exchanged(fam.mix, mix_recv, g)
-
-
-    to_line(fam.down, own_down, own_down, beside_across, 2)
+    arrived(fam.mix, mix_recv.at[0 : PARTS - 1])
+
 
     mixer_t = mix_recv[...].reshape(WIDTH, ROWS)
     residual = resid[...] + dot16(mixer_t, w_out[...], 0, 0)
@@ -990,30 +1030,16 @@
     unit2[...] = unit
     n2_all[chip] = (unit * par_v[20:21, :] + par_v[21:22, :]).astype(BF16)
 
-    def push_n2(k):
-        q, d, s = of_plane(k)
-        mine = n2_all.at[chip]
-        push(fam.n2, mine, mine, d, s, chip)
-
-    loop(1, 3, push_n2)
-
-    arrived(fam.upz, up_all.at[0, 0:2], 1)
-    to_twin(fam.upt, up_all.at[core, beside])
-    to_twin(fam.upt, up_all.at[core, beside_across])
-    arrived(fam.upt, up_all.at[0])
-
-    def place_up(i):
-        q, zz = lax.div(i, 8) * 2 + lax.rem(i, 2), lax.rem(lax.div(i, 2), 4)
-        both = jnp.concatenate(
-            [up_all[0, zz, q].astype(F32), up_all[1, zz, q].astype(F32)], axis=0
-        )
-        w_up[tile(i, 48), :] = both.astype(BF16)
-
-    loop(0, 16, place_up)
-    push_n2(3)
-    for index, place in ((0, across), (1, beside), (2, beside_across)):
-        arrived(fam.down, down_all.at[0, 0], index)
-        to_twin(fam.downt, down_all.at[core, place])
+    def push_n2(k, q):
+        _, d, s = of_plane(k)
+        push(fam.n2, n2_all.at[q], n2_all.at[q], d, s, q)
+
+    push_n2(1, chip)
+    push_n2(2, chip)
+    gather_second(fam.seed, seed_all, 2 - core)
+    spread_far(fam.upz, fam.upf, fam.upt, up_all.at[core])
+    spread_far(fam.down, fam.downf, fam.downt, down_all.at[core])
+
     up_bias = jnp.zeros((1, SPLIT), F32)
     for q in range(4):
         cut = []
@@ -1024,41 +1050,41 @@
                 cut.append(par_v[23 + row : 24 + row, lane0 : lane0 + 96])
         up_bias = jnp.where(chip == q, jnp.concatenate(cut, axis=1), up_bias)
 
+    spread_last(fam.upz, fam.upt, up_all.at[core])
+    arrived(fam.upt, up_all.at[0])
+
+    def place_up(i):
+        q, zz = lax.div(i, 8) * 2 + lax.rem(i, 2), lax.rem(lax.div(i, 2), 4)
+        both = jnp.concatenate(
+            [up_all[0, zz, q].astype(F32), up_all[1, zz, q].astype(F32)], axis=0
+        )
+        w_up[tile(i, 48), :] = both.astype(BF16)
+
+    loop(0, 16, place_up)
     act_all, gl_all, po_all, gn_all, slope = v.act_all, v.gl_all, v.po_all, v.gn_all, v.slope
     gn_recv, po_recv = v.gn_recv, v.po_recv
 
     def feed(k):
         q, _, _ = of_plane(k)
-
-        @pl.when(k != 0)
-        def _():
-            arrived(fam.n2, n2_all.at[0], q)
-
         lifted = dot16(n2_all[q], w_up[...], 1, 0) + up_bias
         cdf = 0.5 * (1.0 + lax.erf(lifted * (1.0 / math.sqrt(2.0))))
         pdf = jnp.exp(-0.5 * lifted * lifted) * (1.0 / math.sqrt(2.0 * math.pi))
         act_all[q] = (lifted * cdf).astype(BF16)
         slope[q] = cdf + lifted * pdf
 
-    loop(0, 4, feed)
+    feed(0)
+    first_k = 2 - core
+    first_q, _, _ = of_plane(first_k)
+    arrived(fam.n2, n2_all.at[0], first_q)
+    push_n2(3 - first_k, first_q)
+    feed(first_k)
+    second_q, _, _ = of_plane(3 - first_k)
+    arrived(fam.n2, n2_all.at[0], second_q)
+    feed(3 - first_k)
+    last_q, _, _ = of_plane(3)
+    arrived(fam.n2, n2_all.at[0], last_q)
+    feed(3)
     arrived(fam.seed, seed_all.at[0:2], 1)
-    arrived(fam.downt, down_all.at[0])
-
-    def feed_back(k, bias_sum):
-        q, d, s = of_plane(lax.rem(k, 4))
-        grad_act = dot16(seed_all[q], down_all[...].reshape(SPLIT, WIDTH), 1, 1)
-        grad_lifted = grad_act * slope[q]
-        gl_all[q] = grad_lifted.astype(BF16)
-        gn_all[q] = dot16(gl_all[q], w_up[...], 1, 1).astype(BF16)
-
-        @pl.when(k != 4)
-        def _():
-            push(fam.gn, gn_all.at[q], gn_recv.at[chip], d, s)
-
-        return bias_sum + jnp.sum(grad_lifted, axis=0, keepdims=True)
-
-    grad_up_bias = lax.fori_loop(1, 5, feed_back, jnp.zeros((1, SPLIT), F32))
-    gn_recv[chip] = gn_all[chip]
 
     sd_x, sd_y, sd_t, sd_z = v.sd_x, v.sd_y, v.sd_t, v.sd_z
     su_x, su_y, su_t, su_z, su_p, su_r = v.su_x, v.su_y, v.su_t, v.su_z, v.su_p, v.su_r
@@ -1069,6 +1095,91 @@
         half = acts[:, c * 384 : (c + 1) * 384]
         sd_x[c] = dot16(half, seeds, 0, 0).astype(BF16).reshape(4, 96, WIDTH)
     to_twin(fam.sdt, sd_x.at[other_core], sd_y)
+
+    def add_sd(zz):
+        sd_t[zz] = (sd_x[core, zz].astype(F32) + sd_y[zz].astype(F32)).astype(BF16)
+
+    def add_su(zz):
+        for q in range(4):
+            su_t[zz, q] = (su_x[core, zz, q].astype(F32) + su_y[zz, q].astype(F32)).astype(BF16)
+
+    def fold_send(family, sums, landing, block, zz, side):
+        to_line(family, sums.at[block], landing.at[side, block], zz, side * 4 + block)
+
+    def fold_add(family, sums, landing, block, side):
+        arrived(family, landing.at[side, block], side * 4 + block)
+        sums[block] = (sums[block].astype(F32) + landing[side, block].astype(F32)).astype(BF16)
+
+    def fold_start(family, sums, landing, blocks):
+        @pl.when(z == 0)
+        def _():
+            for far in blocks:
+                fold_send(family, sums, landing, far, 1, 0)
+
+        @pl.when(z == 3)
+        def _():
+            for far in blocks:
+                fold_send(family, sums, landing, 3 - far, 2, 1)
+
+    def fold_middle(family, sums, landing):
+        @pl.when(z == 1)
+        def _():
+            for block in (3, 2):
+                fold_add(family, sums, landing, block, 0)
+                fold_send(family, sums, landing, block, 2, 0)
+
+        @pl.when(z == 2)
+        def _():
+            for block in (0, 1):
+                fold_add(family, sums, landing, block, 1)
+                fold_send(family, sums, landing, block, 1, 1)
+
+    def fold_end(family, sums, landing):
+        @pl.when(z == 2)
+        def _():
+            fold_add(family, sums, landing, 3, 0)
+            fold_send(family, sums, landing, 3, 3, 0)
+
+        @pl.when(z == 1)
+        def _():
+            fold_add(family, sums, landing, 0, 1)
+            fold_send(family, sums, landing, 0, 0, 1)
+
+    def fold_total(family, sums, landing, total):
+        total[...] = sums[z].astype(F32)
+
+        @pl.when(z > 0)
+        def _():
+            arrived(family, landing.at[0, z], z)
+            total[...] = total[...] + landing[0, z].astype(F32)
+
+        @pl.when(z < 3)
+        def _():
+            arrived(family, landing.at[1, z], 4 + z)
+            total[...] = total[...] + landing[1, z].astype(F32)
+
+    spread_last(fam.down, fam.downt, down_all.at[core])
+    arrived(fam.downt, down_all.at[0])
+
+    def feed_back(k, bias_sum):
+        q, d, s = of_plane(lax.rem(k, 4))
+        grad_act = dot16(seed_all[q], down_all[...].reshape(SPLIT, WIDTH), 1, 1)
+        grad_lifted = grad_act * slope[q]
+        gl_all[q] = grad_lifted.astype(BF16)
+        gn_all[q] = dot16(gl_all[q], w_up[...], 1, 1).astype(BF16)
+
+        @pl.when(k != 4)
+        def _():
+            push(fam.gn, gn_all.at[q], gn_recv.at[chip], d, s)
+
+        return bias_sum + jnp.sum(grad_lifted, axis=0, keepdims=True)
+
+    grad_up_bias = lax.fori_loop(1, 3, feed_back, jnp.zeros((1, SPLIT), F32))
+    arrived(fam.sdt, sd_y)
+    loop(0, 4, add_sd)
+    fold_start(fam.sd, sd_t, sd_z, (3, 2))
+    grad_up_bias = lax.fori_loop(3, 5, feed_back, grad_up_bias)
+    gn_recv[chip] = gn_all[chip]
     units = n2_all[...].reshape(4 * ROWS, WIDTH)
     lows = gl_all[...].reshape(4 * ROWS, SPLIT)
     for x in range(2):
@@ -1076,32 +1187,9 @@
         for i in range(16):
             su_x[i % 2, i // 4, x * 2 + (i // 2) % 2] = part[24 * i : 24 * (i + 1)].astype(BF16)
     to_twin(fam.sut, su_x.at[other_core], su_y)
-
-    def add_sd(zz):
-        sd_t[zz] = (sd_x[core, zz].astype(F32) + sd_y[zz].astype(F32)).astype(BF16)
-
-    def add_su(zz):
-        for q in range(4):
-            su_t[zz, q] = (su_x[core, zz, q].astype(F32) + su_y[zz, q].astype(F32)).astype(BF16)
-
-    def pair_first(family, sums, landing):
-        to_line(family, sums.at[beside_across], landing.at[1], beside, 0)
-
-    def pair_own(family, sums, landing):
-        to_line(family, sums.at[beside], landing.at[0], beside, 2)
-
-    def pair_second(family, sums, landing):
-        arrived(family, landing.at[0], 0)
-        sums[across] = (sums[across].astype(F32) + landing[1].astype(F32)).astype(BF16)
-        to_line(family, sums.at[across], landing.at[2], across, 1)
-
-    arrived(fam.sdt, sd_y)
-    loop(0, 4, add_sd)
-    pair_first(fam.sd, sd_t, sd_z)
-    pair_own(fam.sd, sd_t, sd_z)
     arrived(fam.sut, su_y)
     loop(0, 4, add_su)
-    pair_first(fam.su, su_t, su_z)
+    fold_start(fam.su, su_t, su_z, (3, 2))
 
 
     def outputs_part(k):
@@ -1109,6 +1197,8 @@
         po_all[q] = dot16(act_all[q], down_all[...].reshape(SPLIT, WIDTH), 1, 0).astype(BF16)
 
     loop(0, 4, outputs_part)
+
+    fold_middle(fam.sd, sd_t, sd_z)
 
     arrived(fam.gn, gn_all.at[0:3])
     grad_n2 = gn_recv[0].astype(F32)
@@ -1125,7 +1215,7 @@
     gres = v.gres
     gres[...] = grad_res.astype(BF16)
     gm_send[...] = dot16(w_out[...], gres[...], 1, 1).astype(BF16).reshape(PARTS, LOCAL, ROWS)
-    loop(0, GROUPS, lambda g: exchange(fam.gm, gm_send, gm_recv, g))
+    exchange(fam.gm, gm_send, gm_recv)
     gm_recv[seq] = gm_send[seq]
 
     def sum_first(family, sums, landing, k):
@@ -1169,13 +1259,14 @@
     grad_mix, raw, q_s = v.grad_mix, v.raw, v.q_s
 
     def operator_back(g):
+        turn[0] = g
         at = tile(g, LANE_CH)
         skips = par_t[pl.ds(pl.multiple_of(seq * LOCAL + g * LANE_CH, LANE_CH), LANE_CH), :]
         skip0, skip1 = skips[:, 17:18], skips[:, 18:19]
         decay = decay_of(g)
 
         def rows_at(first, count=LANE_CH):
-            return pl.ds(pl.multiple_of(first + g * LANE_CH, LANE_CH), count)
+            return pl.ds(first + g * LANE_CH, count)
 
         seconds, total = [], jnp.zeros((LANE_CH, ROWS), F32)
         for a in range(PARTS):
@@ -1224,30 +1315,35 @@
             @pl.when(core == c)
             def _():
                 at = slice(c * 384, (c + 1) * 384)
-                b_p[chip] = b_x[:, at] + b_y[:, at]
+                b_p[chip] = (b_x[:, at] + b_y[:, at]).astype(BF16)
 
         loop(1, 4, push_b)
 
-    def group_back(g):
-        exchanged(fam.gm, gm_recv, g)
-
-        @pl.when(g == 0)
-        def _():
-            pair_second(fam.su, su_t, su_z)
-            arrived(fam.sot, so_y)
-            loop(0, 4, add_so)
-            sum_first(fam.so, so_t, so_p, 2)
-
+    arrived(fam.gm, gm_recv.at[0 : PARTS - 1])
+    fold_end(fam.sd, sd_t, sd_z)
+    fold_middle(fam.su, su_t, su_z)
+    arrived(fam.sot, so_y)
+    loop(0, 4, add_so)
+    sum_first(fam.so, so_t, so_p, 2 - core)
+    sums_of_rows()
+    fold_start(fam.su, su_t, su_z, (1,))
+    fold_start(fam.sd, sd_t, sd_z, (1,))
+    for g in range(GROUPS):
         operator_back(g)
-
-        @pl.when(g == 0)
-        def _():
-            sums_of_rows()
-            pair_second(fam.sd, sd_t, sd_z)
-            pair_own(fam.su, su_t, su_z)
-
-    loop(0, GROUPS, group_back)
+    fold_end(fam.su, su_t, su_z)
+    sum_second(fam.so, so_t, so_p, 2 - core)
     sum_second(fam.po, po_all, po_recv, 2 - core)
+    arrived(fam.b, b_p.at[0:3])
+    b_t[...] = (
+        (b_p[0].astype(F32) + b_p[1].astype(F32)) + (b_p[2].astype(F32) + b_p[3].astype(F32))
+    ).astype(BF16)
+    b_z[z] = b_t[...]
+
+    def push_b2(k):
+        zz, s = of_line(k)
+        push(fam.b2, b_t, b_z.at[z], dp, s)
+
+    loop(1, 4, push_b2)
 
     zx_send, zx_recv, z_send, z_recv = v.zx_send, v.zx_recv, v.z_send, v.z_recv
     by_id = dot32(grad_mix[...], onehot[...], 1, 1)
@@ -1265,7 +1361,6 @@
         [columns, skip_cols, jnp.zeros((64, IDS), F32)], axis=0
     ).T
     push(fam.zx, zx_send, zx_recv, other_dp, seq)
-    sum_second(fam.so, so_t, so_p, 2)
 
     f_send, f_recv, m_send, m_recv, m2_send, m2_recv = (v.f_send, v.f_recv, v.m_send, v.m_recv, v.m2_send, v.m2_recv)
     grad_filter = dot32(raw[...], act2[...], 1, 1)
@@ -1301,11 +1396,19 @@
         push(fam.z, z_send, z_recv.at[seq], dp, s)
 
     loop(1, PARTS, push_z)
-    arrived(fam.su, su_z.at[2], 1)
-    arrived(fam.su, su_z.at[0], 2)
-    for q in range(4):
-        part = su_t[z, q].astype(F32) + su_z[0, q].astype(F32) + su_z[2, q].astype(F32)
-        su_p[q] = part.astype(BF16)
+    arrived(fam.so, so_p.at[0], 1)
+    for zz in range(4):
+        part = so_t[chip, zz].astype(F32) + so_p[0, zz].astype(F32) + so_p[2, zz].astype(F32)
+        so_u[zz] = part.astype(BF16)
+    so_z[z] = so_u[z]
+
+    def push_so2(k):
+        zz, s = of_line(k)
+        push(fam.so2, so_u.at[zz], so_z.at[z], dp, s)
+
+    loop(1, 4, push_so2)
+    fold_total(fam.su, su_t, su_z, v.su_f)
+    su_p[...] = v.su_f[...].astype(BF16)
     su_r[chip] = su_p[chip]
 
     def push_su2(k):
@@ -1313,6 +1416,8 @@
         push(fam.su2, su_p.at[q], su_r.at[chip], d, s)
 
     loop(1, 4, push_su2)
+
+
     arrived(fam.m, m_recv.at[0:7])
     totals = m_recv[0].astype(F32)
     for j in range(1, 8):
@@ -1325,28 +1430,6 @@
         push(fam.m2, m2_send, m2_recv.at[z], dp, s)
 
     loop(1, 4, push_m2)
-
-
-    arrived(fam.b, b_p.at[0:3])
-    b_t[...] = (b_p[0] + b_p[1]) + (b_p[2] + b_p[3])
-    b_z[z] = b_t[...]
-
-    def push_b2(k):
-        zz, s = of_line(k)
-        push(fam.b2, b_t, b_z.at[z], dp, s)
-
-    loop(1, 4, push_b2)
-    arrived(fam.so, so_p.at[0], 1)
-    for zz in range(4):
-        part = so_t[chip, zz].astype(F32) + so_p[0, zz].astype(F32) + so_p[2, zz].astype(F32)
-        so_u[zz] = part.astype(BF16)
-    so_z[z] = so_u[z]
-
-    def push_so2(k):
-        zz, s = of_line(k)
-        push(fam.so2, so_u.at[zz], so_z.at[z], dp, s)
-
-    loop(1, 4, push_so2)
 
     wide, gt_all = v.wide, v.gt_all
     arrived(fam.z, z_recv.at[0 : PARTS - 1])
@@ -1393,10 +1476,7 @@
     resid[...] = block
     store(resid, out.block)
 
-    arrived(fam.sd, sd_z.at[2], 1)
-    arrived(fam.sd, sd_z.at[0], 2)
-    part = sd_t[z].astype(F32) + sd_z[0].astype(F32) + sd_z[2].astype(F32)
-    downw_v[...] = part
+    fold_total(fam.sd, sd_t, sd_z, downw_v)
     store(downw_v, out.down_weight)
     arrived(fam.f, f_recv)
     f_recv[...] = f_send[tile(dp, LOCAL), :] + f_recv[...]
@@ -1412,7 +1492,7 @@
     store(upw_v, out.up_weight)
 
     arrived(fam.b2, b_z.at[0:3])
-    b_f[core] = (b_z[0] + b_z[1]) + (b_z[2] + b_z[3])
+    b_f[core] = (b_z[0].astype(F32) + b_z[1].astype(F32)) + (b_z[2].astype(F32) + b_z[3].astype(F32))
     to_twin(fam.bf, b_f.at[core])
     arrived(fam.so2, so_z.at[0:3])
     part = so_z[0].astype(F32)
@@ -1465,8 +1545,8 @@
     for family, ref in (
         (fam.p, p_send.at[0 : PARTS - 1]), (fam.tok, tok_all.at[0 : PARTS - 1]), (fam.filt, filt_all.at[0]),
         (fam.px, px_send), (fam.outz, out_all.at[0, 0, 0:3]), (fam.outp, out_all.at[0, 0:3]),
-        (fam.outt, out_all.at[0]), (fam.up, up_send.at[0:3]), (fam.upz, up_all.at[0, 0:3]),
-        (fam.upt, up_all.at[0]), (fam.seed, seed_all.at[0:3]), (fam.down, down_all.at[0, 0:3]),
+        (fam.outt, out_all.at[0]), (fam.up, up_send.at[0:3]),
+        (fam.upt, up_all.at[0]), (fam.seed, seed_all.at[0:3]),
         (fam.downt, down_all.at[0]), (fam.mix, mix_send.at[0 : PARTS - 1]),
         (fam.gm, gm_send.at[0 : PARTS - 1]), (fam.n2, n2_all.at[0:3]), (fam.gn, gn_all.at[0:3]),
         (fam.po, po_all.at[0:3]), (fam.sdt, sd_y), (fam.sut, su_y), (fam.sot, so_y), (fam.sd, sd_t.at[0:3]),
@@ -1476,6 +1556,20 @@
         (fam.zx, zx_send), (fam.f, f_recv), (fam.gt, gt_all.at[0 : 2 * PARTS - 1]),
     ):
         wait_for(ref, s_of(family))
+    for family, onward, ref in (
+        (fam.upz, fam.upf, up_all.at[0]),
+        (fam.down, fam.downf, down_all.at[0]),
+    ):
+
+        @pl.when(lax.rem(z, 3) == 0)
+        def _():
+            wait_for(ref.at[0], s_of(family))
+
+        @pl.when(lax.rem(z, 3) != 0)
+        def _():
+            wait_for(ref.at[0:2], s_of(family))
+            wait_for(ref.at[0:3], s_of(onward))
+
     for copy in stores:
         copy.wait()
 
@@ -1487,8 +1581,8 @@
 
 
 FAMILIES = dict(
-    p=1, tok=1, filt=1, px=1, outz=1, outp=2, outt=1, up=1, upz=2, upt=1, down=3, downt=1, seed=2, mix=3,
-    gm=3, n2=4, gn=1, po=2, sdt=1, sd=3, sut=1, su=3, su2=1, sot=1, so=2, so2=1, bt=1, b=1, b2=1, bf=1,
+    p=1, tok=1, filt=1, px=1, outz=1, outp=2, outt=1, up=1, upz=4, upf=0, upt=1, down=4, downf=0, downt=1, seed=2, mix=1,
+    gm=1, n2=4, gn=1, po=2, sdt=1, sd=8, sut=1, su=8, su2=1, sot=1, so=2, so2=1, bt=1, b=1, b2=1, bf=1,
     m=1, m2=1, z=1, zx=1, f=1, gt=1,
 )
 LOADS = 18
@@ -1524,7 +1618,7 @@
     cos2=((64, LENGTH), F32), kern=((2, PARTS, LOCAL, ROWS), F32), par_t=((WIDTH, 32), F32),
     table_t=((3 * LOCAL, IDS), F32), onehot=((3 * IDS, LENGTH), F32),
     mix=((3, PARTS, LOCAL, ROWS), F32),
-    hi=((2 * SPEC, 2 * ROWS), BF16), lo=((2 * SPEC, 2 * ROWS), BF16),
+    hi=((GROUPS, 2 * SPEC, 2 * ROWS), BF16), lo=((GROUPS, 2 * SPEC, 2 * ROWS), BF16),
     spec_k1=(SPECTRUM, F32), spec_k2=(SPECTRUM, F32), spec_v=(SPECTRUM, F32),
     spec_g=(SPECTRUM, F32),
     first=((PARTS, LOCAL, ROWS), F32), gated=((PARTS, LOCAL, ROWS), F32),
@@ -1537,15 +1631,15 @@
     po_recv=((3, ROWS, WIDTH), BF16), gn_all=((4, ROWS, WIDTH), BF16),
     gn_recv=((4, ROWS, WIDTH), BF16), gres=((ROWS, WIDTH), BF16),
     sd_x=((2, 4, 96, WIDTH), BF16), sd_y=((4, 96, WIDTH), BF16), sd_t=((4, 96, WIDTH), BF16),
-    sd_z=((3, 96, WIDTH), BF16),
+    sd_z=((2, 4, 96, WIDTH), BF16),
     su_x=((2, 4, 4, 24, SPLIT), BF16), su_y=((4, 4, 24, SPLIT), BF16),
-    su_t=((4, 4, 24, SPLIT), BF16), su_z=((3, 4, 24, SPLIT), BF16), su_p=((4, 24, SPLIT), BF16),
+    su_t=((4, 4, 24, SPLIT), BF16), su_z=((2, 4, 4, 24, SPLIT), BF16), su_f=((4, 24, SPLIT), F32), su_p=((4, 24, SPLIT), BF16),
     su_r=((4, 24, SPLIT), BF16),
     so_x=((2, 4, 4, 24, WIDTH), BF16), so_y=((4, 4, 24, WIDTH), BF16),
     so_t=((4, 4, 24, WIDTH), BF16), so_p=((3, 4, 24, WIDTH), BF16), so_u=((4, 24, WIDTH), BF16),
     so_z=((4, 24, WIDTH), BF16),
-    b_x=((24, WIDTH), F32), b_y=((24, WIDTH), F32), b_p=((4, 24, 384), F32),
-    b_t=((24, 384), F32), b_z=((4, 24, 384), F32), b_f=((2, 24, 384), F32),
+    b_x=((24, WIDTH), F32), b_y=((24, WIDTH), F32), b_p=((4, 24, 384), BF16),
+    b_t=((24, 384), BF16), b_z=((4, 24, 384), BF16), b_f=((2, 24, 384), F32),
     grad_mix=((3 * LOCAL, LENGTH), F32), raw=((2 * LOCAL, LENGTH), F32), q_s=((LOCAL, 128), F32),
     z_send=((IDS, 256), BF16), z_recv=((PARTS, IDS, 256), BF16), zx_send=((IDS, 256), F32),
     zx_recv=((IDS, 256), F32), wide=((IDS, 4 * WIDTH), F32), gt_all=((32, 8, 128), F32),

time: 105 us -> 96 us (0.914)
  Pallas kernels: 104 us -> 95 us
    pallas_call x1, Pallas kernels: 102 us -> 92.4 us  [fast_device(): pl.pallas_call(step_kernel, out_shape=shapes, in_specs=[anywhere] * len(I...]
where the time goes in v3:
time: 96 us; the launch traced here: 95.9 us
  Pallas kernels  95 us (99%)
    pallas_call x1, Pallas kernels, fast_device(): pl.pallas_call(step_kernel, out_shape=shapes, in_specs=[anywhere] * len(I...  92.4 us
    pallas_call x1, Pallas kernels, fast_device(): pl.pallas_call(copy_kernel, out_shape=shapes, in_specs=[near] * len(shape...  2.67 us

profile of v3, /device:TPU:0, one launch (start us, length us, event | category | flops | bytes accessed | tf_op | source)
XLA Modules:
  0.0 95.9 jit_solution(15272575310683350075)
XLA Ops:
  0.7 92.4 %shard_map.417 = (f32[128,768]{1,0:T(8,128)}, f32[12,768]{1,0:T(8,128)}, f32[768]{0:T(1024)}, f32[768]{0:T(1024)}, f32[24,2304]{1,0:T(8,128)}, /*index=5*/f32[23...) custom-call(s32[1,128]{1,0:T(1,128)} %refs_0_.1, ...), custom_call_target="tpu_custom_call" | custom-call | tf_op jit(solution)/shard_map/pallas_call | solution.py:1673
  93.0 2.7 %shard_map.418 = (f32[128,768]{1,0:T(8,128)}, f32[12,768]{1,0:T(8,128)}, f32[768]{0:T(1024)}, f32[768]{0:T(1024)}, f32[24,2304]{1,0:T(8,128)}, /*index=5*/f32[23...) custom-call(f32[128,768]{1,0:T(8,128)} %get-tuple-element.66.refs_0_, ...), custom_call_target="tpu_custom_call" | custom-call | tf_op jit(solution)/shard_map/pallas_call | solution.py:1684

commit v4 on v3

--- a/solution.py
+++ b/solution.py
@@ -1319,13 +1319,13 @@
 
         loop(1, 4, push_b)
 
-    arrived(fam.gm, gm_recv.at[0 : PARTS - 1])
-    fold_end(fam.sd, sd_t, sd_z)
-    fold_middle(fam.su, su_t, su_z)
     arrived(fam.sot, so_y)
     loop(0, 4, add_so)
     sum_first(fam.so, so_t, so_p, 2 - core)
     sums_of_rows()
+    arrived(fam.gm, gm_recv.at[0 : PARTS - 1])
+    fold_end(fam.sd, sd_t, sd_z)
+    fold_middle(fam.su, su_t, su_z)
     fold_start(fam.su, su_t, su_z, (1,))
     fold_start(fam.sd, sd_t, sd_z, (1,))
     for g in range(GROUPS):

time: 96 us -> 95.5 us (level)
  no operation moved by 1% of the time
where the time goes in v4:
time: 95.5 us; the launch traced here: 95.4 us
  Pallas kernels  94.5 us (99%)
    pallas_call x1, Pallas kernels, fast_device(): pl.pallas_call(step_kernel, out_shape=shapes, in_specs=[anywhere] * len(I...  91.9 us
    pallas_call x1, Pallas kernels, fast_device(): pl.pallas_call(copy_kernel, out_shape=shapes, in_specs=[near] * len(shape...  2.67 us

profile of v4, /device:TPU:0, one launch (start us, length us, event | category | flops | bytes accessed | tf_op | source)
XLA Modules:
  0.0 95.4 jit_solution(13504367506769030439)
XLA Ops:
  0.7 91.9 %shard_map.417 = (f32[128,768]{1,0:T(8,128)}, f32[12,768]{1,0:T(8,128)}, f32[768]{0:T(1024)}, f32[768]{0:T(1024)}, f32[24,2304]{1,0:T(8,128)}, /*index=5*/f32[23...) custom-call(s32[1,128]{1,0:T(1,128)} %refs_0_.1, ...), custom_call_target="tpu_custom_call" | custom-call | tf_op jit(solution)/shard_map/pallas_call | solution.py:1673
  92.5 2.7 %shard_map.418 = (f32[128,768]{1,0:T(8,128)}, f32[12,768]{1,0:T(8,128)}, f32[768]{0:T(1024)}, f32[768]{0:T(1024)}, f32[24,2304]{1,0:T(8,128)}, /*index=5*/f32[23...) custom-call(f32[128,768]{1,0:T(8,128)} %get-tuple-element.66.refs_0_, ...), custom_call_target="tpu_custom_call" | custom-call | tf_op jit(solution)/shard_map/pallas_call | solution.py:1684
